TPU v7x, 32 devices: a whole 2x2x4 slice. The times are simulated.
32 devices in a mesh: outer: 8 (over y, x, core), inner: 4 (over z).
Axes of the slice: x: 2, y: 2, z: 4, core: 2. Of those that a mesh axis runs over, the one named last changes fastest.
Arguments:
- queries: bfloat16 [4096, 5120], P(('outer', 'inner')), may hold values from -100 to 100
- key_values: bfloat16 [4096, 2048], P(('outer', 'inner')), may hold values from -64 to 64
- doc_lengths: int32 [8, 8], P('outer'), may hold values from 1 to 256, 512 in all within a row
- pairing: int32 [8], replicated, may hold values from 0 to 7, as said below
- swap_ids: int32 [8, 4, 2], P('outer', 'inner'), may hold values from 0 to 3, as said below
- dest: int32 [4096, 1], P(('outer', 'inner')), may hold values from 0 to 3; in each aligned block of 128 rows (0 to 127, 128 to 255, ...) at most 64 rows name the same one
- gain: float32 [5120], replicated, may hold values from 0.1 to 1.9
Outputs:
- normed: bfloat16 [8192, 5120], P(('outer', 'inner'))
Inputs may be any that keep to these rules, and one draw needn't show every extreme that they name: pairing[g] = g XOR m for one m of 1 to 7 in each draw, so pairing[pairing[g]] = g. Each device's listed numbers are distinct and increasing, and swap_ids[pairing[g]] = swap_ids[g]. `dest`: the rows of one device name each destination at most 64 times.
All inputs are finite; a program needn't handle non-finite values.
Results may differ from a plain program's by a relative error of at most 0.0059.
Values may be sent and summed in bfloat16 or wider, within the bound.
No kernel may reach another device: no remote copies, remote signals or barrier semaphores. Data moves between devices by JAX's collectives and lax.ppermute only.
A program may use at most 128 MiB of HBM per device.

v0:
```python
import math

import jax
import jax.numpy as jnp
from jax import lax
from jax.sharding import PartitionSpec as P

QUERY_HEADS = 40
KEY_VALUE_HEADS = 8
HEAD_SIZE = 128
BLK = 32


NEGATIVE_LARGE = -1e30


def from_partner(value, axis, bit):
    mask = 2**bit
    pairs = [(source, source ^ mask) for source in range(lax.axis_size(axis))]
    return lax.ppermute(value, axis, pairs)


def doc_index(positions, lengths):
    ends = jnp.cumsum(lengths)
    return jnp.sum((positions[:, None] >= ends[None, :]).astype(jnp.int32), axis=1)


def normalize(row_list, gain):
    value_matrix = row_list.astype(jnp.float32)
    factor = lax.rsqrt(jnp.mean(value_matrix * value_matrix, axis=-1, keepdims=True) + 1e-06)
    return (value_matrix * factor * gain).astype(jnp.bfloat16)


def slot_rank(dest_rows, n_inner):
    onehot = (dest_rows[:, :, None] == jnp.arange(n_inner, dtype=jnp.int32)[None, None, :]).astype(
        jnp.int32
    )
    return jnp.sum(jnp.cumsum(onehot, axis=1) * onehot, axis=2) - 1


def swap_blocks(queries, key_values, pairing, swap_ids):
    row_list, width_q = queries.shape
    width_kv = key_values.shape[1]
    n_blocks = row_list // BLK
    listed = swap_ids[0, 0]
    q_blocks = queries.reshape(n_blocks, BLK, width_q)
    kv_blocks = key_values.reshape(n_blocks, BLK, width_kv)
    outgoing = jnp.concatenate([q_blocks[listed], kv_blocks[listed]], axis=2)
    pair_bits = pairing[0]
    levels = lax.axis_size("outer").bit_length() - 1
    for level in range(levels):
        arrived = from_partner(outgoing, "outer", level)
        outgoing = jnp.where(pair_bits >> level & 1 == 1, arrived, outgoing)
    query_sequence = q_blocks.at[listed].set(outgoing[:, :, :width_q]).reshape(row_list, width_q)
    key_value_sequence = (
        kv_blocks.at[listed].set(outgoing[:, :, width_q:]).reshape(row_list, width_kv)
    )
    return (query_sequence, key_value_sequence)


def attend_sequence(query_sequence, key_value_sequence, lengths):
    row_list = query_sequence.shape[0]
    portion_each = QUERY_HEADS // KEY_VALUE_HEADS
    scale = 1.0 / math.sqrt(HEAD_SIZE)
    first = lax.axis_index("inner") * row_list
    q_pos = first + jnp.arange(row_list, dtype=jnp.int32)
    q_doc = doc_index(q_pos, lengths)
    query_rank4 = query_sequence.reshape(row_list, KEY_VALUE_HEADS, portion_each, HEAD_SIZE)
    slice_part = lax.all_gather(key_value_sequence, "inner", axis=0, tiled=True)
    block_count = slice_part.shape[0]
    k_pos = jnp.arange(block_count, dtype=jnp.int32)
    k_doc = doc_index(k_pos, lengths)
    key_value_rank4 = slice_part.reshape(block_count, KEY_VALUE_HEADS, 2, HEAD_SIZE)
    scores = (
        jnp.einsum(
            "tkgd,rkd->kgtr",
            query_rank4,
            key_value_rank4[:, :, 0],
            preferred_element_type=jnp.float32,
        )
        * scale
    )
    allowed = (k_pos[None, :] <= q_pos[:, None]) & (k_doc[None, :] == q_doc[:, None])
    scores = jnp.where(allowed, scores, NEGATIVE_LARGE)
    previous_max = jnp.full((KEY_VALUE_HEADS, portion_each, row_list), NEGATIVE_LARGE, jnp.float32)
    new_max = jnp.maximum(previous_max, jnp.max(scores, axis=-1))
    expo = jnp.where(allowed, jnp.exp(scores - new_max[..., None]), 0.0)
    total = jnp.sum(expo, axis=-1)
    weights = expo.astype(jnp.bfloat16)
    update = jnp.einsum(
        "kgtr,rkd->tkgd", weights, key_value_rank4[:, :, 1], preferred_element_type=jnp.float32
    )
    accum = update
    final_max, total, accum = (new_max, total, accum)
    result = accum / jnp.transpose(total, (2, 0, 1))[..., None]
    return result.astype(jnp.bfloat16).reshape(row_list, QUERY_HEADS * HEAD_SIZE)


def shards(queries, key_values, doc_lengths, pairing, swap_ids, dest, gain):
    query_sequence, key_value_sequence = swap_blocks(queries, key_values, pairing, swap_ids)
    row_list, width = queries.shape
    n_inner = lax.axis_size("inner")
    capacity = 2 * row_list // n_inner
    lengths = doc_lengths[0]
    attn = attend_sequence(query_sequence, key_value_sequence, lengths)
    my_dest = dest[:, 0]
    rank = slot_rank(my_dest[None, :], n_inner)[0]
    place = my_dest * capacity + rank
    buffer = jnp.zeros((n_inner * capacity, width), jnp.bfloat16).at[place].set(attn)
    arrived = (lambda part: normalize(part, gain))(
        lax.all_to_all(
            buffer.reshape(n_inner, capacity, width),
            "inner",
            split_axis=0,
            concat_axis=0,
            tiled=True,
        )
    )
    return arrived.reshape(n_inner * capacity, width)


def solution(mesh):
    return jax.shard_map(
        shards,
        mesh=mesh,
        in_specs=(
            P(("outer", "inner"), None),
            P(("outer", "inner"), None),
            P("outer", None),
            P(),
            P("outer", "inner", None),
            P(("outer", "inner"), None),
            P(),
        ),
        out_specs=P(("outer", "inner"), None),
        check_vma=False,
    )
```

profile of v0, /device:TPU:8, one launch (start us, length us, event | category | flops | bytes accessed | tf_op | source)
XLA Modules:
  0.0 195.4 jit_solution(1540050683725108730)
XLA Ops:
  6.5 1.4 copy.42
  8.1 0.6 gather_fusion
  8.7 0.6 gather_fusion.1
  9.4 2.4 %collective-permute-done = bf16[2,32,7168]{2,1,0:T(8,128)(2,1)S(1)} collective-permute-done((bf16[2,32,7168]{2,1,0:T(8,128)(2,1)S(1)}, bf16[2,32,7168]{2,1,0:T(8,128)(2,1)S(1)}, u32[]{:S(2)}, u32[]{:S(2)}) %collective-permute-start) | collective-permute-done | bytes 917536 | tf_op jit(solution)/shard_map/ppermute | solution.py:20
  11.8 0.1 broadcast_select_fusion
  12.0 1.6 collective-permute-start.1
  13.6 20.9 %collective-permute-done.1 = bf16[2,32,7168]{2,1,0:T(8,128)(2,1)S(1)} collective-permute-done((bf16[2,32,7168]{2,1,0:T(8,128)(2,1)S(1)}, bf16[2,32,7168]{2,1,0:T(8,128)(2,1)S(1)}, u32[]{:S(2)}, u32[]{:S(2)}) %collective-permute-start.1) | collective-permute-done | bytes 917536 | tf_op jit(solution)/shard_map/ppermute | solution.py:20
  34.4 0.1 broadcast_select_fusion.1
  34.5 1.6 collective-permute-start.2
  36.2 20.0 %collective-permute-done.2 = bf16[2,32,7168]{2,1,0:T(8,128)(2,1)S(1)} collective-permute-done((bf16[2,32,7168]{2,1,0:T(8,128)(2,1)S(1)}, bf16[2,32,7168]{2,1,0:T(8,128)(2,1)S(1)}, u32[]{:S(2)}, u32[]{:S(2)}) %collective-permute-start.2) | collective-permute-done | bytes 917536 | tf_op jit(solution)/shard_map/ppermute | solution.py:20
  56.2 0.1 broadcast_select_fusion.2
  56.3 0.6 scatter_fusion
  57.0 0.8 copy-done.1
  57.8 0.2 reduce-window.8
  58.1 0.2 reduce_window_sum.19
  58.2 0.1 convert_reduce_fusion
  58.3 0.1 convert_reduce_fusion.1
  58.4 0.2 select_reduce_fusion
  58.6 0.1 fusion.16
  58.8 0.7 scatter_fusion.1
  59.5 1.6 reshape_reshape.3
  61.1 42.3 %all-gather.2.cloned.1.call-done = bf16[512,2048]{1,0:T(8,128)(2,1)} async-done(((bf16[128,2048]{1,0:T(8,128)(2,1)}), bf16[512,2048]{1,0:T(8,128)(2,1)}) %all-gather.2.cloned.1.call-update) | async-done | bytes 2097168 | tf_op jit(solution)/shard_map/all_gather | solution.py:69
  103.4 3.9 %copy.22 = bf16[512,2048]{0,1:T(8,128)(2,1)} copy(bf16[512,2048]{1,0:T(8,128)(2,1)} %all-gather.2.cloned.1.call-done) | data formatting | bytes 4194304 | tf_op jit(solution)/shard_map/all_gather | solution.py:69
  107.3 4.3 %fusion = (f32[8,5,128]{2,1,0:T(8,128)S(1)}, f32[8,512,128,5]{2,1,3,0:T(8,128)S(1)}) fusion(pred[128,512]{0,1:T(8,128)(4,1)S(1)} %fusion.16, bf16[128,8,5,128]{3,2,1,0:T(8,128)(2,1)S(1)} %reshape_reshape.3, bf16[512,8,2,128]{0,3,2,1:T(8,128)(2,1)} %bitcast.62), kind=kOutput, calls=%fused_computation.7 | convolution fusion | flops 678947840 | bytes 12931072 | tf_op jit(solution)/shard_map/tkgd,rkd->kgtr/dot_general | solution.py:75
  111.6 2.7 %fusion.1 = f32[8,5,128]{2,1,0:T(8,128)S(1)} fusion(f32[8,512,128,5]{2,1,3,0:T(8,128)S(1)} %get-tuple-element.6, f32[8,5,128]{2,1,0:T(8,128)S(1)} %broadcast_maximum_fusion, pred[128,512]{0,1:T(8,128)(4,1)S(1)} %fusion.16), kind=kLoop, calls=%fused_computation.8 | loop fusion | flops 13102080 | bytes 10592256 | tf_op jit(solution)/shard_map/reduce_sum | solution.py:88
  114.3 3.2 %fusion.9 = bf16[128,8,5,128]{0,3,2,1:T(8,128)(2,1)S(1)} fusion(f32[8,512,128,5]{2,1,3,0:T(8,128)S(1)} %get-tuple-element.6, f32[8,5,128]{2,1,0:T(8,128)S(1)} %broadcast_maximum_fusion, pred[128,512]{0,1:T(8,128)(4,1)S(1)} %fusion.16, f32[128,8,5]{0,2,1:T(8,128)S(1)} %bitcast.68, bf16[512,8,2,128]{0,3,2,1:T(8,128)(2,1)S(1)} %bitcast.63), kind=kOutput, calls=%fused_computation.18 | convolution fusion | flops 685506560 | bytes 12976128 | tf_op jit(solution)/shard_map/kgtr,rkd->tkgd/dot_general | solution.py:90
  117.5 1.4 copy.27
  119.0 4.0 %scatter_custom_fusion.2 = bf16[256,5120]{1,0:T(8,128)(2,1)S(1)} fusion(s32[128]{0:T(128)S(1)} %fusion.18, bf16[128,5120]{1,0:T(8,128)(2,1)} %copy.27, bf16[]{:T(256)} %constant.18.clone.1), kind=kCustom, calls=%fused_computation.21 | custom fusion | bytes 2621952 | tf_op jit(solution)/shard_map/scatter | solution.py:109
  123.0 62.5 %all_to_all.5 = bf16[4,64,5120]{2,1,0:T(8,128)(2,1)S(1)} all-to-all(bf16[4,64,5120]{2,1,0:T(8,128)(2,1)S(1)} %bitcast.61), channel_id=1, replica_groups=mesh['outer'=8,'inner'=4] {'inner'}, dimensions={0} | all-to-all | bytes 5242880 | tf_op jit(solution)/shard_map/all_to_all | solution.py:111
  185.5 0.6 fusion.3
  186.1 0.1 copy-done.3
  186.3 2.3 %fusion.5 = bf16[4,64,5120]{2,1,0:T(8,128)(2,1)} fusion(bf16[4,64,5120]{2,1,0:T(8,128)(2,1)S(1)} %all_to_all.5, f32[5120]{0:T(1024)S(1)} %copy-done.3, f32[4,64]{1,0:T(4,128)S(1)} %add_rsqrt_fusion), kind=kLoop, calls=%fused_computation.14 | loop fusion | flops 5242880 | bytes 5264384 | tf_op jit(solution)/shard_map/convert_element_type | solution.py:31
  (29 shorter events, 0.5 us)
Async XLA Ops:
  6.5 1.4 copy-start.2
  6.5 1.5 copy-start.5
  6.5 96.9 %all-gather.2.cloned.1.call-start = ((), (), s32[]{:S(2)}) async-start(), calls=%async_computation.1 | async-start | bytes 2621440 | tf_op jit(solution)/shard_map/all_gather | solution.py:69
  8.0 1.4 copy-start.6
  9.3 2.5 %collective-permute-start = (bf16[2,32,7168]{2,1,0:T(8,128)(2,1)S(1)}, bf16[2,32,7168]{2,1,0:T(8,128)(2,1)S(1)}, u32[]{:S(2)}, u32[]{:S(2)}) collective-permute-start(bf16[2,32,7168]{2,1,0:T(8,128)(2,1)S(1)} %constant_dynamic-update-slice_fusion), channel_id=1, source_target_pairs={{0,4},{4,0},{8,12},{12,8},{16,20},{20,16},{24,28},{28,24},{1,5},{5... | collective-permute-start | bytes 2752520 | tf_op jit(solution)/shard_map/ppermute | solution.py:20
  12.0 22.5 %collective-permute-start.1 = (bf16[2,32,7168]{2,1,0:T(8,128)(2,1)S(1)}, bf16[2,32,7168]{2,1,0:T(8,128)(2,1)S(1)}, u32[]{:S(2)}, u32[]{:S(2)}) collective-permute-start(bf16[2,32,7168]{2,1,0:T(8,128)(2,1)S(1)} %broadcast_select_fusion), channel_id=1, source_target_pairs={{0,8},{4,12},{8,0},{12,4},{16,24},{20,28},{24,16},{28,20},{1,9},{5... | collective-permute-start | bytes 2752520 | tf_op jit(solution)/shard_map/ppermute | solution.py:20
  34.5 23.2 %copy-start.7 = (s32[1,8]{1,0:T(1,128)S(1)}, s32[1,8]{1,0:T(1,128)}, u32[]{:S(2)}) copy-start(s32[1,8]{1,0:T(1,128)} %param.9) | copy-start | bytes 100
  34.5 23.4 %copy-start.4 = (s32[128,1]{0,1:T(1,128)S(1)}, s32[128,1]{0,1:T(1,128)}, u32[]{:S(2)}) copy-start(s32[128,1]{0,1:T(1,128)} %param.12) | copy-start | bytes 1540
  34.5 21.6 %collective-permute-start.2 = (bf16[2,32,7168]{2,1,0:T(8,128)(2,1)S(1)}, bf16[2,32,7168]{2,1,0:T(8,128)(2,1)S(1)}, u32[]{:S(2)}, u32[]{:S(2)}) collective-permute-start(bf16[2,32,7168]{2,1,0:T(8,128)(2,1)S(1)} %broadcast_select_fusion.1), channel_id=1, source_target_pairs={{0,16},{4,20},{8,24},{12,28},{16,0},{20,4},{24,8},{28,12},{1,17},{... | collective-permute-start | bytes 2752520 | tf_op jit(solution)/shard_map/ppermute | solution.py:20
  56.9 0.8 copy-start.1
  111.6 2.7 %copy-start = (bf16[512,2048]{0,1:T(8,128)(2,1)S(1)}, bf16[512,2048]{0,1:T(8,128)(2,1)}, u32[]{:S(2)}) copy-start(bf16[512,2048]{0,1:T(8,128)(2,1)} %copy.22) | copy-start | bytes 6291460
  185.5 0.7 copy-start.3
Sparse Core Ops, SparseCore 0:
  57.9 45.4 all-gather.1
where the time goes:
time: 199 us; the launch traced here: 195 us
  waiting for transfers between devices  85.6 us (43%)
  blocking collectives  62.5 us (31%)
  local copies, waits for them, and re-layouts  16 us (8%)
  between operations  13.8 us (7%)
  matrix products  7.46 us (4%)
  other arithmetic  6.8 us (3%)
  starting transfers between devices  3.21 us (2%)
    all_to_all x1, blocking collectives, shards(): lax.all_to_all(buffer.reshape(n_inner, capacity, width), 'inner', split_a...  62.5 us
    ppermute x3, waiting for transfers between devices, from_partner(): return lax.ppermute(value, axis, pairs)  43.3 us
    all_gather x1, waiting for transfers between devices, attend_sequence(): slice_part = lax.all_gather(key_value_sequence, 'inner', axis=0, tiled=True)  42.3 us
    dot_general x1, matrix products, attend_sequence(): jnp.einsum('tkgd,rkd->kgtr', query_rank4, key_value_rank4[:, :, 0], prefe...  4.26 us
    scatter x1, local copies, waits for them, and re-layouts, shards(): jnp.zeros((n_inner * capacity, width), jnp.bfloat16).at[place].set(attn)  4.02 us
  transfers between devices with their start and end apart: 4, of which 4 were waited for; matrix products, arithmetic and copies ran while one was open for 2% of the time, Pallas kernels for 0%

commit v1 on v0

v1 whole, which is shorter than its diff:
```python
import functools
import math

import jax
import jax.numpy as jnp
from jax import lax
from jax.experimental import pallas as pl
from jax.experimental.pallas import tpu as pltpu
from jax.sharding import PartitionSpec as P

QUERY_HEADS = 40
KEY_VALUE_HEADS = 8
PORTION = QUERY_HEADS // KEY_VALUE_HEADS
HEAD_SIZE = 128
BLK = 32
NSWAP = 2

NEGATIVE_LARGE = -1e30
HEAD_GROUPS = (4, 4)
VMEM_LIMIT = 48 * 1024 * 1024


def params():
    return pltpu.CompilerParams(vmem_limit_bytes=VMEM_LIMIT)


def ring(step, size):
    return [(i, (i + step) % size) for i in range(size)]


def from_partner(value, level, size):
    return lax.ppermute(value, "outer", [(i, i ^ (1 << level)) for i in range(size)])


def block_order(listed, n_blocks):
    ids = jnp.arange(n_blocks, dtype=jnp.int32)
    is_listed = jnp.any(ids[:, None] == listed[None, :], axis=1).astype(jnp.int32)
    place = jnp.where(
        is_listed == 1,
        n_blocks - listed.shape[0] + jnp.cumsum(is_listed) - 1,
        jnp.cumsum(1 - is_listed) - 1,
    )
    return jnp.sum(jnp.where(place[None, :] == ids[:, None], ids[None, :], 0), axis=1)


def split_kernel(order, q_ref, kv_ref, kv_rest, kv_listed, q_listed, sems):
    n_rest = kv_rest.shape[0] // BLK
    copies = []
    for b in range(kv_ref.shape[0] // BLK):
        here = pl.ds(pl.multiple_of(order[b] * BLK, BLK), BLK)
        if b < n_rest:
            pairs = [(kv_ref, kv_rest, b)]
        else:
            pairs = [(kv_ref, kv_listed, b - n_rest), (q_ref, q_listed, b - n_rest)]
        for source, target, at in pairs:
            copies.append((source.at[here], target.at[pl.ds(at * BLK, BLK)]))
    copies = [pltpu.make_async_copy(s, t, sems.at[i]) for i, (s, t) in enumerate(copies)]
    for copy in copies:
        copy.start()
    for copy in copies:
        copy.wait()


def split_blocks(order, queries, key_values):
    row_list, width = queries.shape
    kv_width = key_values.shape[1]
    some = NSWAP * BLK
    anywhere = pl.BlockSpec(memory_space=pl.ANY)
    return pl.pallas_call(
        split_kernel,
        out_shape=(
            jax.ShapeDtypeStruct((row_list - some, kv_width), jnp.bfloat16),
            jax.ShapeDtypeStruct((some, kv_width), jnp.bfloat16),
            jax.ShapeDtypeStruct((some, width), jnp.bfloat16),
        ),
        in_specs=[pl.BlockSpec(memory_space=pltpu.SMEM), anywhere, anywhere],
        out_specs=(anywhere,) * 3,
        scratch_shapes=[pltpu.SemaphoreType.DMA((row_list // BLK + NSWAP,))],
        compiler_params=params(),
        name="split_blocks",
    )(order, queries, key_values)


def exchange(listed_rows, pair_bits, n_outer):
    levels = n_outer.bit_length() - 1

    def hop(value, level):
        arrived = from_partner(value, level, n_outer)
        return jnp.where((pair_bits >> level) & 1 == 1, arrived, value)

    value = hop(listed_rows, 0)
    rest = list(range(1, levels))
    turn = (len(rest) + 1) // 2
    halves = []
    for part, order in enumerate((rest, rest[turn:] + rest[:turn])):
        half = value[part * BLK : (part + 1) * BLK]
        for level in order:
            half = hop(half, level)
        halves.append(half)
    return halves


def attend_kernel(n_keys, n_out, order, key_pos, q_pos, q_start, place, q_ref, *refs):
    q_new = refs[:NSWAP]
    kv_refs = refs[NSWAP : NSWAP + n_keys]
    outs = refs[NSWAP + n_keys : NSWAP + n_keys + n_out]
    q_all = refs[-1]
    row_list = q_ref.shape[0]
    capacity = outs[0].shape[0]
    n_rest = row_list // BLK - NSWAP

    q_all[...] = q_ref[...]
    for part in range(NSWAP):
        at = pl.multiple_of(order[n_rest + part] * BLK, BLK)
        q_all[pl.ds(at, BLK), :] = q_new[part][...]

    key = jnp.concatenate([ref[:, :HEAD_SIZE] for ref in kv_refs], axis=0)
    value = jnp.concatenate([ref[:, HEAD_SIZE:] for ref in kv_refs], axis=0)
    query = jnp.concatenate(
        [q_all[:, h * HEAD_SIZE : (h + 1) * HEAD_SIZE] for h in range(PORTION)], axis=0
    )
    scores = lax.dot_general(
        query, key, (((1,), (1,)), ((), ())), preferred_element_type=jnp.float32
    ) * (1.0 / math.sqrt(HEAD_SIZE))
    allowed = (key_pos[...] <= q_pos[...]) & (key_pos[...] >= q_start[...])
    allowed = jnp.concatenate([allowed] * PORTION, axis=0)
    scores = jnp.where(allowed, scores, NEGATIVE_LARGE)
    expo = jnp.exp(scores - jnp.max(scores, axis=1, keepdims=True))
    expo = jnp.where(allowed, expo, 0.0)
    total = jnp.sum(expo, axis=1, keepdims=True)
    attn = jnp.dot(expo.astype(jnp.bfloat16), value, preferred_element_type=jnp.float32)
    attn = (attn / total).astype(jnp.bfloat16)
    attn = jnp.concatenate(
        [attn[h * row_list : (h + 1) * row_list] for h in range(PORTION)], axis=1
    )
    slots = lax.broadcasted_iota(jnp.int32, (n_out * capacity, row_list), 0)
    chosen = (slots == place[...]).astype(jnp.bfloat16)
    routed = jnp.dot(chosen, attn, preferred_element_type=jnp.float32).astype(jnp.bfloat16)
    for k in range(n_out):
        outs[k][...] = routed[k * capacity : (k + 1) * capacity]


def attend(first, heads, order, key_pos, q_pos, q_start, place, queries, q_new, kv_parts, n_out):
    row_list = queries.shape[0]
    capacity = NSWAP * row_list // n_out
    wide = PORTION * HEAD_SIZE
    n_all = sum(part.shape[0] for part in kv_parts)

    def whole(shape):
        return pl.BlockSpec(shape, lambda s: (0, 0))

    def columns(rows, width):
        return pl.BlockSpec((rows, width), lambda s: (0, first + s))

    return pl.pallas_call(
        functools.partial(attend_kernel, len(kv_parts), n_out),
        grid=(heads,),
        out_shape=[jax.ShapeDtypeStruct((capacity, heads * wide), jnp.bfloat16)] * n_out,
        in_specs=[
            pl.BlockSpec(memory_space=pltpu.SMEM),
            whole((1, n_all)),
            whole((row_list, 1)),
            whole((row_list, 1)),
            whole((1, row_list)),
            columns(row_list, wide),
        ]
        + [columns(BLK, wide)] * NSWAP
        + [columns(part.shape[0], 2 * HEAD_SIZE) for part in kv_parts],
        out_specs=[pl.BlockSpec((capacity, wide), lambda s: (0, s))] * n_out,
        scratch_shapes=[pltpu.VMEM((row_list, wide), jnp.bfloat16)],
        compiler_params=params(),
        cost_estimate=pl.CostEstimate(
            flops=heads * PORTION * row_list * n_all * HEAD_SIZE * 4,
            bytes_accessed=heads * (4 * wide * row_list * 2 + n_all * 512),
            transcendentals=heads * PORTION * row_list * n_all,
        ),
        name="attend",
    )(order, key_pos, q_pos, q_start, place, queries, *q_new, *kv_parts)


def norm_kernel(n_inner, n_groups, me, gain, *refs):
    parts = refs[: n_inner * n_groups]
    out = refs[n_inner * n_groups]
    held, ready, in_sems, out_sems = refs[n_inner * n_groups + 1 :]
    capacity, width = parts[0].shape[0], held.shape[2]
    loads = []
    for k in range(n_inner):
        column = 0
        for g in range(n_groups):
            ref = parts[g * n_inner + k]
            wide = ref.shape[1]
            loads.append(
                pltpu.make_async_copy(
                    ref, held.at[k, :, pl.ds(column, wide)], in_sems.at[k, g]
                )
            )
            loads[-1].start()
            column += wide
    stores = []
    for k in range(n_inner):
        for g in range(n_groups):
            loads[k * n_groups + g].wait()
        value = held[k].astype(jnp.float32)
        factor = lax.rsqrt(jnp.sum(value * value, axis=1, keepdims=True) / width + 1e-06)
        ready[k] = (value * factor * gain[...]).astype(jnp.bfloat16)
        source = lax.rem(me[0] - k + n_inner, n_inner)
        there = pl.ds(pl.multiple_of(source * capacity, capacity), capacity)
        stores.append(pltpu.make_async_copy(ready.at[k], out.at[there], out_sems.at[k]))
        stores[-1].start()
    for store in stores:
        store.wait()


def normalize(me, gain, parts, n_inner):
    n_groups = len(parts) // n_inner
    capacity = parts[0].shape[0]
    width = gain.shape[0]
    return pl.pallas_call(
        functools.partial(norm_kernel, n_inner, n_groups),
        out_shape=jax.ShapeDtypeStruct((n_inner * capacity, width), jnp.bfloat16),
        in_specs=[
            pl.BlockSpec(memory_space=pltpu.SMEM),
            pl.BlockSpec((1, width), lambda: (0, 0)),
        ]
        + [pl.BlockSpec(memory_space=pl.ANY)] * len(parts),
        out_specs=pl.BlockSpec(memory_space=pl.ANY),
        scratch_shapes=[
            pltpu.VMEM((n_inner, capacity, width), jnp.bfloat16),
            pltpu.VMEM((n_inner, capacity, width), jnp.bfloat16),
            pltpu.SemaphoreType.DMA((n_inner, n_groups)),
            pltpu.SemaphoreType.DMA((n_inner,)),
        ],
        compiler_params=params(),
        name="normalize",
    )(me.reshape(1), gain.reshape(1, width), *parts)


def shards(queries, key_values, doc_lengths, pairing, swap_ids, dest, gain):
    row_list = queries.shape[0]
    n_inner = lax.axis_size("inner")
    n_outer = lax.axis_size("outer")
    me = lax.axis_index("inner")
    n_blocks = row_list // BLK
    n_back = n_inner // 2
    pair_bits = pairing[0]
    order = block_order(swap_ids[0, 0], n_blocks)

    kv_rest, kv_listed, q_listed = split_blocks(order, queries, key_values)

    rest_parts, orders = [kv_rest], [order]
    for _ in range(n_back):
        rest_parts.append(lax.ppermute(rest_parts[-1], "inner", ring(1, n_inner)))
        orders.append(lax.ppermute(orders[-1], "inner", ring(1, n_inner)))
    kv_new = jnp.concatenate(exchange(kv_listed, pair_bits, n_outer), axis=0)
    listed_parts = [kv_new]
    for _ in range(n_back):
        listed_parts.append(lax.ppermute(listed_parts[-1], "inner", ring(1, n_inner)))
    q_new = exchange(q_listed, pair_bits, n_outer)

    inside = jnp.arange(BLK, dtype=jnp.int32)
    key_pos = []
    for back in range(n_back + 1):
        pos = (orders[back][:, None] * BLK + inside[None, :]).reshape(-1)
        key_pos.append(jnp.where(me >= back, pos + (me - back) * row_list, -1))
    key_pos = jnp.concatenate(key_pos)[None, :]
    q_pos = me * row_list + jnp.arange(row_list, dtype=jnp.int32)
    ends = jnp.cumsum(doc_lengths[0])
    q_start = jnp.max(jnp.where(ends[None, :] <= q_pos[:, None], ends[None, :], 0), axis=1)

    my_dest = dest[:, 0]
    same = my_dest[:, None] == my_dest[None, :]
    earlier = q_pos[None, :] < q_pos[:, None]
    rank = jnp.sum((same & earlier).astype(jnp.int32), axis=1)
    capacity = NSWAP * row_list // n_inner
    place = lax.rem(my_dest - me + n_inner, n_inner) * capacity + rank

    kv_parts = [part for pair in zip(rest_parts, listed_parts) for part in pair]
    arrived, first = [], 0
    for heads in HEAD_GROUPS:
        routed = attend(
            first,
            heads,
            order,
            key_pos,
            q_pos[:, None],
            q_start[:, None],
            place[None, :],
            queries,
            q_new,
            kv_parts,
            n_inner,
        )
        arrived.append(routed[0])
        for k in range(1, n_inner):
            arrived.append(lax.ppermute(routed[k], "inner", ring(k, n_inner)))
        first += heads
    return normalize(me, gain, arrived, n_inner)


def solution(mesh):
    return jax.shard_map(
        shards,
        mesh=mesh,
        in_specs=(
            P(("outer", "inner"), None),
            P(("outer", "inner"), None),
            P("outer", None),
            P(),
            P("outer", "inner", None),
            P(("outer", "inner"), None),
            P(),
        ),
        out_specs=P(("outer", "inner"), None),
        check_vma=False,
    )
```

time: 199 us -> 110 us (0.55); the launches traced: 195 us -> 109 us
  blocking collectives: 62.5 us -> 0 us
  waiting for transfers between devices: 85.6 us -> 64.5 us
  starting transfers between devices: 3.21 us -> 22.8 us
  local copies, waits for them, and re-layouts: 16 us -> 2.8 us
  Pallas kernels: 0 us -> 12.8 us
  between operations: 13.8 us -> 2.12 us
  matrix products: 7.46 us -> 0 us
  other arithmetic: 6.8 us -> 4.36 us
    all_to_all x1 -> x0, blocking collectives: 62.5 us -> none  [shards(): lax.all_to_all(buffer.reshape(n_inner, capacity, width), 'inner', split_a...]
    all_gather x1 -> x0, waiting for transfers between devices: 42.3 us -> none  [attend_sequence(): slice_part = lax.all_gather(key_value_sequence, 'inner', axis=0, tiled=True)]
    ppermute x3 -> x22, waiting for transfers between devices: 43.3 us -> 64.5 us  [the longest x6 43.3 us: shards(): arrived.append(lax.ppermute(routed[k], 'inner', ring(k, n_inner)))]
    ppermute x3 -> x22, starting transfers between devices: 3.21 us -> 22.8 us  [the longest x10 8.6 us: from_partner(): lax.ppermute(value, 'outer', [(i, i ^ 1 << level) for i in range(size)])]
    pallas_call x0 -> x4, Pallas kernels: none -> 12.8 us  [the longest x2 8.58 us: attend(): pl.pallas_call(functools.partial(attend_kernel, len(kv_parts), n_out), gr...]
    dot_general x2 -> x0, matrix products: 7.46 us -> none  [the longest x1 4.26 us: attend_sequence(): jnp.einsum('tkgd,rkd->kgtr', query_rank4, key_value_rank4[:, :, 0], prefe...]
    scatter x3 -> x0, local copies, waits for them, and re-layouts: 5.35 us -> none  [the longest x1 4.02 us: shards(): jnp.zeros((n_inner * capacity, width), jnp.bfloat16).at[place].set(attn)]
    all_gather x1 -> x0, local copies, waits for them, and re-layouts: 3.92 us -> none  [attend_sequence(): slice_part = lax.all_gather(key_value_sequence, 'inner', axis=0, tiled=True)]
  transfers between devices with their start and end apart: 4 -> 22, of which waited for: 4 -> 13; matrix products, arithmetic and copies ran while one was open for 2% -> 3% of each run, Pallas kernels for 0% -> 5%
where the time goes in v1:
time: 110 us; the launch traced here: 109 us
  waiting for transfers between devices  64.5 us (59%)
  starting transfers between devices  22.8 us (21%)
  Pallas kernels  12.8 us (12%)
  other arithmetic  4.36 us (4%)
  local copies, waits for them, and re-layouts  2.8 us (3%)
  between operations  2.12 us (2%)
    ppermute x6, waiting for transfers between devices, shards(): arrived.append(lax.ppermute(routed[k], 'inner', ring(k, n_inner)))  43.3 us
    ppermute x10, waiting for transfers between devices, from_partner(): lax.ppermute(value, 'outer', [(i, i ^ 1 << level) for i in range(size)])  19.9 us
    ppermute x10, starting transfers between devices, from_partner(): lax.ppermute(value, 'outer', [(i, i ^ 1 << level) for i in range(size)])  8.6 us
    pallas_call x2, Pallas kernels, attend(): pl.pallas_call(functools.partial(attend_kernel, len(kv_parts), n_out), gr...  8.58 us
    ppermute x6, starting transfers between devices, shards(): arrived.append(lax.ppermute(routed[k], 'inner', ring(k, n_inner)))  8.5 us
    pallas_call x1, Pallas kernels, normalize(): pl.pallas_call(functools.partial(norm_kernel, n_inner, n_groups), out_sha...  2.7 us
    unnamed x8, local copies, waits for them, and re-layouts  2.37 us
  transfers between devices with their start and end apart: 22, of which 13 were waited for; matrix products, arithmetic and copies ran while one was open for 3% of the time, Pallas kernels for 5%

profile of v1, /device:TPU:8, one launch (start us, length us, event | category | flops | bytes accessed | tf_op | source)
XLA Modules:
  0.0 109.3 jit_solution(16384836886811400015)
XLA Ops:
  0.0 0.8 fusion
  1.3 1.6 %collective-permute-start = (s32[4]{0:T(128)S(1)}, s32[4]{0:T(128)S(1)}, u32[]{:S(2)}, u32[]{:S(2)}) collective-permute-start(s32[4]{0:T(128)S(1)} %select_reduce_fusion.1.order), channel_id=1, source_target_pairs={{0,1},{1,2},{2,3},{3,0},{4,5},{5,6},{6,7},{7,4},{8,9},{9,10},{10,1... | collective-permute-start | bytes 56 | tf_op jit(solution)/shard_map/ppermute | solution.py:253
  2.9 1.3 %copy-done = bf16[128,5120]{1,0:T(8,128)(2,1)S(1)} copy-done((bf16[128,5120]{1,0:T(8,128)(2,1)S(1)}, bf16[128,5120]{1,0:T(8,128)(2,1)}, u32[]{:S(2)}) %copy-start) | copy-done | bytes 1310744
  4.2 1.0 copy-done.2
  5.3 1.5 %split_blocks.1 = (bf16[64,2048]{1,0:T(8,128)(2,1)S(1)}, bf16[64,2048]{1,0:T(8,128)(2,1)S(1)}, bf16[64,5120]{1,0:T(8,128)(2,1)S(1)}) custom-call(s32[4]{0:T(128)S(1)} %select_reduce_fusion.1.order, bf16[128,5120]{1,0:T(8,128)(2,1)S(1)} %copy-done, bf16[128,2048]{1,0:T(8,128)(2,1)S(1)} %copy-done.2), custom_call_target="tpu_custom_call" | custom-call | tf_op jit(solution)/shard_map/split_blocks/pallas_call | solution.py:69
  6.8 1.6 %collective-permute-start.12 = (bf16[64,2048]{1,0:T(8,128)(2,1)S(1)}, bf16[64,2048]{1,0:T(8,128)(2,1)S(1)}, u32[]{:S(2)}, u32[]{:S(2)}) collective-permute-start(bf16[64,2048]{1,0:T(8,128)(2,1)S(1)} %get-tuple-element.17.refs_2_), channel_id=1, source_target_pairs={{0,1},{1,2},{2,3},{3,0},{4,5},{5,6},{6,7},{7,4},{8,9},{9,10},{10,1... | collective-permute-start | bytes 786440 | tf_op jit(solution)/shard_map/ppermute | solution.py:252
  8.6 0.9 convert_reduce_fusion
  10.2 0.8 reduce-window.26
  13.4 1.6 %collective-permute-start.8 = (bf16[32,2048]{1,0:T(8,128)(2,1)S(1)}, bf16[32,2048]{1,0:T(8,128)(2,1)S(1)}, u32[]{:S(2)}, u32[]{:S(2)}) collective-permute-start(bf16[32,2048]{1,0:T(8,128)(2,1)S(1)} %get-tuple-element.33), channel_id=1, source_target_pairs={{0,8},{4,12},{8,0},{12,4},{16,24},{20,28},{24,16},{28,20},{1,9},{5... | collective-permute-start | bytes 393224 | tf_op jit(solution)/shard_map/ppermute | solution.py:32
  15.0 1.5 %collective-permute-start.10 = (bf16[32,2048]{1,0:T(8,128)(2,1)S(1)}, bf16[32,2048]{1,0:T(8,128)(2,1)S(1)}, u32[]{:S(2)}, u32[]{:S(2)}) collective-permute-start(bf16[32,2048]{1,0:T(8,128)(2,1)S(1)} %get-tuple-element.34), channel_id=1, source_target_pairs={{0,16},{4,20},{8,24},{12,28},{16,0},{20,4},{24,8},{28,12},{1,17},{... | collective-permute-start | bytes 393224 | tf_op jit(solution)/shard_map/ppermute | solution.py:32
  17.0 2.3 %collective-permute-done.8 = bf16[32,2048]{1,0:T(8,128)(2,1)S(1)} collective-permute-done((bf16[32,2048]{1,0:T(8,128)(2,1)S(1)}, bf16[32,2048]{1,0:T(8,128)(2,1)S(1)}, u32[]{:S(2)}, u32[]{:S(2)}) %collective-permute-start.8) | collective-permute-done | bytes 131104 | tf_op jit(solution)/shard_map/ppermute | solution.py:32
  19.3 1.2 %collective-permute-done.10 = bf16[32,2048]{1,0:T(8,128)(2,1)S(1)} collective-permute-done((bf16[32,2048]{1,0:T(8,128)(2,1)S(1)}, bf16[32,2048]{1,0:T(8,128)(2,1)S(1)}, u32[]{:S(2)}, u32[]{:S(2)}) %collective-permute-start.10) | collective-permute-done | bytes 131104 | tf_op jit(solution)/shard_map/ppermute | solution.py:32
  20.5 1.6 %collective-permute-start.9 = (bf16[32,2048]{1,0:T(8,128)(2,1)S(1)}, bf16[32,2048]{1,0:T(8,128)(2,1)S(1)}, u32[]{:S(2)}, u32[]{:S(2)}) collective-permute-start(bf16[32,2048]{1,0:T(8,128)(2,1)S(1)} %get-tuple-element.31), channel_id=1, source_target_pairs={{0,16},{4,20},{8,24},{12,28},{16,0},{20,4},{24,8},{28,12},{1,17},{... | collective-permute-start | bytes 393224 | tf_op jit(solution)/shard_map/ppermute | solution.py:32
  22.6 2.9 %collective-permute-done.9 = bf16[32,2048]{1,0:T(8,128)(2,1)S(1)} collective-permute-done((bf16[32,2048]{1,0:T(8,128)(2,1)S(1)}, bf16[32,2048]{1,0:T(8,128)(2,1)S(1)}, u32[]{:S(2)}, u32[]{:S(2)}) %collective-permute-start.9) | collective-permute-done | bytes 131104 | tf_op jit(solution)/shard_map/ppermute | solution.py:32
  25.7 1.6 %collective-permute-start.5 = (bf16[32,5120]{1,0:T(8,128)(2,1)S(1)}, bf16[32,5120]{1,0:T(8,128)(2,1)S(1)}, u32[]{:S(2)}, u32[]{:S(2)}) collective-permute-start(bf16[32,5120]{1,0:T(8,128)(2,1)S(1)} %get-tuple-element.29), channel_id=1, source_target_pairs={{0,16},{4,20},{8,24},{12,28},{16,0},{20,4},{24,8},{28,12},{1,17},{... | collective-permute-start | bytes 983048 | tf_op jit(solution)/shard_map/ppermute | solution.py:32
  28.2 5.3 %collective-permute-done.5 = bf16[32,5120]{1,0:T(8,128)(2,1)S(1)} collective-permute-done((bf16[32,5120]{1,0:T(8,128)(2,1)S(1)}, bf16[32,5120]{1,0:T(8,128)(2,1)S(1)}, u32[]{:S(2)}, u32[]{:S(2)}) %collective-permute-start.5) | collective-permute-done | bytes 327712 | tf_op jit(solution)/shard_map/ppermute | solution.py:32
  33.5 1.6 %collective-permute-done.3 = bf16[32,5120]{1,0:T(8,128)(2,1)S(1)} collective-permute-done((bf16[32,5120]{1,0:T(8,128)(2,1)S(1)}, bf16[32,5120]{1,0:T(8,128)(2,1)S(1)}, u32[]{:S(2)}, u32[]{:S(2)}) %collective-permute-start.3) | collective-permute-done | bytes 327712 | tf_op jit(solution)/shard_map/ppermute | solution.py:32
  36.2 1.6 %collective-permute-start.15 = (bf16[64,2048]{1,0:T(8,128)(2,1)S(1)}, bf16[64,2048]{1,0:T(8,128)(2,1)S(1)}, u32[]{:S(2)}, u32[]{:S(2)}) collective-permute-start(bf16[64,2048]{1,0:T(8,128)(2,1)S(1)} %collective-permute-done.13.refs_5_), channel_id=1, source_target_pairs={{0,1},{1,2},{2,3},{3,0},{4,5},{5,6},{6,7},{7,4},{8,9},{9,10},{10,1... | collective-permute-start | bytes 786440 | tf_op jit(solution)/shard_map/ppermute | solution.py:257
  38.2 4.1 %collective-permute-done.6 = bf16[32,5120]{1,0:T(8,128)(2,1)S(1)} collective-permute-done((bf16[32,5120]{1,0:T(8,128)(2,1)S(1)}, bf16[32,5120]{1,0:T(8,128)(2,1)S(1)}, u32[]{:S(2)}, u32[]{:S(2)}) %collective-permute-start.6) | collective-permute-done | bytes 327712 | tf_op jit(solution)/shard_map/ppermute | solution.py:32
  42.3 2.5 %collective-permute-done.4 = bf16[32,5120]{1,0:T(8,128)(2,1)S(1)} collective-permute-done((bf16[32,5120]{1,0:T(8,128)(2,1)S(1)}, bf16[32,5120]{1,0:T(8,128)(2,1)S(1)}, u32[]{:S(2)}, u32[]{:S(2)}) %collective-permute-start.4) | collective-permute-done | bytes 327712 | tf_op jit(solution)/shard_map/ppermute | solution.py:32
  44.9 1.3 %collective-permute-done.15.refs_7_ = bf16[64,2048]{1,0:T(8,128)(2,1)S(1)} collective-permute-done((bf16[64,2048]{1,0:T(8,128)(2,1)S(1)}, bf16[64,2048]{1,0:T(8,128)(2,1)S(1)}, u32[]{:S(2)}, u32[]{:S(2)}) %collective-permute-start.15) | collective-permute-done | bytes 262176 | tf_op jit(solution)/shard_map/ppermute | solution.py:257
  46.2 4.3 %attend.3 = (bf16[64,2560]{1,0:T(8,128)(2,1)S(1)}, bf16[64,2560]{1,0:T(8,128)(2,1)S(1)}, bf16[64,2560]{1,0:T(8,128)(2,1)S(1)}, bf16[64,2560]{1,0:T(8,128)(2,1)S(1)}) custom-call(s32[4]{0:T(128)S(1)} %select_reduce_fusion.1.order, s32[1,384]{1,0:T(1,128)S(1)} %broadcast_in_dim.35.key_pos, s32[128,1]{1,0:T(8,128)S(1)} %iota_add_fusion.q_pos, ...), custom_call_target="tpu_custom_call" | custom-call | flops 503316480 | bytes 3407872 | tf_op jit(solution)/shard_map/attend/pallas_call | solution.py:155
  50.9 4.3 %collective-permute-start.20 = (bf16[64,2560]{1,0:T(8,128)(2,1)S(1)}, bf16[64,2560]{1,0:T(8,128)(2,1)S(1)}, u32[]{:S(2)}, u32[]{:S(2)}) collective-permute-start(bf16[64,2560]{1,0:T(8,128)(2,1)S(1)} %get-tuple-element.25), channel_id=1, source_target_pairs={{0,2},{1,3},{2,0},{3,1},{4,6},{5,7},{6,4},{7,5},{8,10},{9,11},{10,... | collective-permute-start | bytes 983048 | tf_op jit(solution)/shard_map/ppermute | solution.py:295
  55.2 4.3 %attend.2 = (bf16[64,2560]{1,0:T(8,128)(2,1)S(1)}, bf16[64,2560]{1,0:T(8,128)(2,1)S(1)}, bf16[64,2560]{1,0:T(8,128)(2,1)S(1)}, bf16[64,2560]{1,0:T(8,128)(2,1)S(1)}) custom-call(s32[4]{0:T(128)S(1)} %select_reduce_fusion.1.order, s32[1,384]{1,0:T(1,128)S(1)} %broadcast_in_dim.35.key_pos, s32[128,1]{1,0:T(8,128)S(1)} %iota_add_fusion.q_pos, ...), custom_call_target="tpu_custom_call" | custom-call | flops 503316480 | bytes 3407872 | tf_op jit(solution)/shard_map/attend/pallas_call | solution.py:155
  59.5 2.1 %collective-permute-start.16 = (bf16[64,2560]{1,0:T(8,128)(2,1)S(1)}, bf16[64,2560]{1,0:T(8,128)(2,1)S(1)}, u32[]{:S(2)}, u32[]{:S(2)}) collective-permute-start(bf16[64,2560]{1,0:T(8,128)(2,1)S(1)} %get-tuple-element.20), channel_id=1, source_target_pairs={{0,1},{1,2},{2,3},{3,0},{4,5},{5,6},{6,7},{7,4},{8,9},{9,10},{10,1... | collective-permute-start | bytes 983048 | tf_op jit(solution)/shard_map/ppermute | solution.py:295
  61.5 1.8 %collective-permute-start.17 = (bf16[64,2560]{1,0:T(8,128)(2,1)S(1)}, bf16[64,2560]{1,0:T(8,128)(2,1)S(1)}, u32[]{:S(2)}, u32[]{:S(2)}) collective-permute-start(bf16[64,2560]{1,0:T(8,128)(2,1)S(1)} %get-tuple-element.21), channel_id=1, source_target_pairs={{0,2},{1,3},{2,0},{3,1},{4,6},{5,7},{6,4},{7,5},{8,10},{9,11},{10,... | collective-permute-start | bytes 983048 | tf_op jit(solution)/shard_map/ppermute | solution.py:295
  63.3 7.4 %collective-permute-done.19.refs_5_ = bf16[64,2560]{1,0:T(8,128)(2,1)S(1)} collective-permute-done((bf16[64,2560]{1,0:T(8,128)(2,1)S(1)}, bf16[64,2560]{1,0:T(8,128)(2,1)S(1)}, u32[]{:S(2)}, u32[]{:S(2)}) %collective-permute-start.19) | collective-permute-done | bytes 327712 | tf_op jit(solution)/shard_map/ppermute | solution.py:295
  70.7 23.2 %collective-permute-done.20.refs_6_ = bf16[64,2560]{1,0:T(8,128)(2,1)S(1)} collective-permute-done((bf16[64,2560]{1,0:T(8,128)(2,1)S(1)}, bf16[64,2560]{1,0:T(8,128)(2,1)S(1)}, u32[]{:S(2)}, u32[]{:S(2)}) %collective-permute-start.20) | collective-permute-done | bytes 327712 | tf_op jit(solution)/shard_map/ppermute | solution.py:295
  93.9 5.7 %collective-permute-done.16.refs_1_ = bf16[64,2560]{1,0:T(8,128)(2,1)S(1)} collective-permute-done((bf16[64,2560]{1,0:T(8,128)(2,1)S(1)}, bf16[64,2560]{1,0:T(8,128)(2,1)S(1)}, u32[]{:S(2)}, u32[]{:S(2)}) %collective-permute-start.16) | collective-permute-done | bytes 327712 | tf_op jit(solution)/shard_map/ppermute | solution.py:295
  99.6 3.5 %collective-permute-done.17.refs_2_ = bf16[64,2560]{1,0:T(8,128)(2,1)S(1)} collective-permute-done((bf16[64,2560]{1,0:T(8,128)(2,1)S(1)}, bf16[64,2560]{1,0:T(8,128)(2,1)S(1)}, u32[]{:S(2)}, u32[]{:S(2)}) %collective-permute-start.17) | collective-permute-done | bytes 327712 | tf_op jit(solution)/shard_map/ppermute | solution.py:295
  103.1 3.5 %collective-permute-done.18.refs_3_ = bf16[64,2560]{1,0:T(8,128)(2,1)S(1)} collective-permute-done((bf16[64,2560]{1,0:T(8,128)(2,1)S(1)}, bf16[64,2560]{1,0:T(8,128)(2,1)S(1)}, u32[]{:S(2)}, u32[]{:S(2)}) %collective-permute-start.18) | collective-permute-done | bytes 327712 | tf_op jit(solution)/shard_map/ppermute | solution.py:295
  106.6 2.7 %normalize.1 = bf16[256,5120]{1,0:T(8,128)(2,1)} custom-call(s32[1]{0:T(128)} %bitcast.me, f32[1,5120]{1,0:T(1,128)S(1)} %bitcast.23, bf16[64,2560]{1,0:T(8,128)(2,1)S(1)} %get-tuple-element.19.refs_0_, bf16[64,2560]{1,0:T(8,128)(2,1)S(1)} %collective-permute-done.16.refs_1_, bf16[64,2560]{1,0:T(8,128)(2,1)S(1)} %collective-permute-done.17.refs_2_, ...), custom_call_target="tpu_custom_call" | custom-call | tf_op jit(solution)/shard_map/normalize/pallas_call | solution.py:218
  (60 shorter events, 5.9 us)
Async XLA Ops:
  1.3 12.1 %collective-permute-start = (s32[4]{0:T(128)S(1)}, s32[4]{0:T(128)S(1)}, u32[]{:S(2)}, u32[]{:S(2)}) collective-permute-start(s32[4]{0:T(128)S(1)} %select_reduce_fusion.1.order), channel_id=1, source_target_pairs={{0,1},{1,2},{2,3},{3,0},{4,5},{5,6},{6,7},{7,4},{8,9},{9,10},{10,1... | collective-permute-start | bytes 56 | tf_op jit(solution)/shard_map/ppermute | solution.py:253
  2.9 1.3 %copy-start = (bf16[128,5120]{1,0:T(8,128)(2,1)S(1)}, bf16[128,5120]{1,0:T(8,128)(2,1)}, u32[]{:S(2)}) copy-start(bf16[128,5120]{1,0:T(8,128)(2,1)} %q_ref.5) | copy-start | bytes 3932164
  4.2 1.0 copy-start.2
  6.8 6.6 %collective-permute-start.7 = (bf16[64,2048]{1,0:T(8,128)(2,1)S(1)}, bf16[64,2048]{1,0:T(8,128)(2,1)S(1)}, u32[]{:S(2)}, u32[]{:S(2)}) collective-permute-start(bf16[64,2048]{1,0:T(8,128)(2,1)S(1)} %get-tuple-element.18), channel_id=1, source_target_pairs={{0,4},{4,0},{8,12},{12,8},{16,20},{20,16},{24,28},{28,24},{1,5},{5... | collective-permute-start | bytes 786440 | tf_op jit(solution)/shard_map/ppermute | solution.py:32
  6.8 29.1 %collective-permute-start.12 = (bf16[64,2048]{1,0:T(8,128)(2,1)S(1)}, bf16[64,2048]{1,0:T(8,128)(2,1)S(1)}, u32[]{:S(2)}, u32[]{:S(2)}) collective-permute-start(bf16[64,2048]{1,0:T(8,128)(2,1)S(1)} %get-tuple-element.17.refs_2_), channel_id=1, source_target_pairs={{0,1},{1,2},{2,3},{3,0},{4,5},{5,6},{6,7},{7,4},{8,9},{9,10},{10,1... | collective-permute-start | bytes 786440 | tf_op jit(solution)/shard_map/ppermute | solution.py:252
  8.5 17.1 %collective-permute-start.2 = (bf16[64,5120]{1,0:T(8,128)(2,1)S(1)}, bf16[64,5120]{1,0:T(8,128)(2,1)S(1)}, u32[]{:S(2)}, u32[]{:S(2)}) collective-permute-start(bf16[64,5120]{1,0:T(8,128)(2,1)S(1)} %get-tuple-element.16), channel_id=1, source_target_pairs={{0,4},{4,0},{8,12},{12,8},{16,20},{20,16},{24,28},{28,24},{1,5},{5... | collective-permute-start | bytes 1966088 | tf_op jit(solution)/shard_map/ppermute | solution.py:32
  13.4 5.8 %collective-permute-start.8 = (bf16[32,2048]{1,0:T(8,128)(2,1)S(1)}, bf16[32,2048]{1,0:T(8,128)(2,1)S(1)}, u32[]{:S(2)}, u32[]{:S(2)}) collective-permute-start(bf16[32,2048]{1,0:T(8,128)(2,1)S(1)} %get-tuple-element.33), channel_id=1, source_target_pairs={{0,8},{4,12},{8,0},{12,4},{16,24},{20,28},{24,16},{28,20},{1,9},{5... | collective-permute-start | bytes 393224 | tf_op jit(solution)/shard_map/ppermute | solution.py:32
  15.0 5.5 %collective-permute-start.10 = (bf16[32,2048]{1,0:T(8,128)(2,1)S(1)}, bf16[32,2048]{1,0:T(8,128)(2,1)S(1)}, u32[]{:S(2)}, u32[]{:S(2)}) collective-permute-start(bf16[32,2048]{1,0:T(8,128)(2,1)S(1)} %get-tuple-element.34), channel_id=1, source_target_pairs={{0,16},{4,20},{8,24},{12,28},{16,0},{20,4},{24,8},{28,12},{1,17},{... | collective-permute-start | bytes 393224 | tf_op jit(solution)/shard_map/ppermute | solution.py:32
  16.7 5.4 %collective-permute-start.1 = (s32[4]{0:T(128)S(1)}, s32[4]{0:T(128)S(1)}, u32[]{:S(2)}, u32[]{:S(2)}) collective-permute-start(s32[4]{0:T(128)S(1)} %collective-permute-done), channel_id=1, source_target_pairs={{0,1},{1,2},{2,3},{3,0},{4,5},{5,6},{6,7},{7,4},{8,9},{9,10},{10,1... | collective-permute-start | bytes 56 | tf_op jit(solution)/shard_map/ppermute | solution.py:253
  20.5 5.0 %collective-permute-start.9 = (bf16[32,2048]{1,0:T(8,128)(2,1)S(1)}, bf16[32,2048]{1,0:T(8,128)(2,1)S(1)}, u32[]{:S(2)}, u32[]{:S(2)}) collective-permute-start(bf16[32,2048]{1,0:T(8,128)(2,1)S(1)} %get-tuple-element.31), channel_id=1, source_target_pairs={{0,16},{4,20},{8,24},{12,28},{16,0},{20,4},{24,8},{28,12},{1,17},{... | collective-permute-start | bytes 393224 | tf_op jit(solution)/shard_map/ppermute | solution.py:32
  22.1 5.7 %collective-permute-start.11 = (bf16[32,2048]{1,0:T(8,128)(2,1)S(1)}, bf16[32,2048]{1,0:T(8,128)(2,1)S(1)}, u32[]{:S(2)}, u32[]{:S(2)}) collective-permute-start(bf16[32,2048]{1,0:T(8,128)(2,1)S(1)} %get-tuple-element.32), channel_id=1, source_target_pairs={{0,8},{4,12},{8,0},{12,4},{16,24},{20,28},{24,16},{28,20},{1,9},{5... | collective-permute-start | bytes 393224 | tf_op jit(solution)/shard_map/ppermute | solution.py:32
  25.7 20.5 %copy-start.1 = (bf16[128,5120]{1,0:T(8,128)(2,1)S(1)}, bf16[128,5120]{1,0:T(8,128)(2,1)}, u32[]{:S(2)}) copy-start(bf16[128,5120]{1,0:T(8,128)(2,1)} %q_ref.5) | copy-start | bytes 3932164
  25.7 7.8 %collective-permute-start.5 = (bf16[32,5120]{1,0:T(8,128)(2,1)S(1)}, bf16[32,5120]{1,0:T(8,128)(2,1)S(1)}, u32[]{:S(2)}, u32[]{:S(2)}) collective-permute-start(bf16[32,5120]{1,0:T(8,128)(2,1)S(1)} %get-tuple-element.29), channel_id=1, source_target_pairs={{0,16},{4,20},{8,24},{12,28},{16,0},{20,4},{24,8},{28,12},{1,17},{... | collective-permute-start | bytes 983048 | tf_op jit(solution)/shard_map/ppermute | solution.py:32
  27.3 7.7 %collective-permute-start.3 = (bf16[32,5120]{1,0:T(8,128)(2,1)S(1)}, bf16[32,5120]{1,0:T(8,128)(2,1)S(1)}, u32[]{:S(2)}, u32[]{:S(2)}) collective-permute-start(bf16[32,5120]{1,0:T(8,128)(2,1)S(1)} %get-tuple-element.30), channel_id=1, source_target_pairs={{0,8},{4,12},{8,0},{12,4},{16,24},{20,28},{24,16},{28,20},{1,9},{5... | collective-permute-start | bytes 983048 | tf_op jit(solution)/shard_map/ppermute | solution.py:32
  27.9 8.3 %collective-permute-start.13 = (bf16[64,2048]{1,0:T(8,128)(2,1)S(1)}, bf16[64,2048]{1,0:T(8,128)(2,1)S(1)}, u32[]{:S(2)}, u32[]{:S(2)}) collective-permute-start(bf16[64,2048]{1,0:T(8,128)(2,1)S(1)} %pad_maximum_fusion.refs_3_), channel_id=1, source_target_pairs={{0,1},{1,2},{2,3},{3,0},{4,5},{5,6},{6,7},{7,4},{8,9},{9,10},{10,1... | collective-permute-start | bytes 786440 | tf_op jit(solution)/shard_map/ppermute | solution.py:257
  35.1 7.1 %collective-permute-start.6 = (bf16[32,5120]{1,0:T(8,128)(2,1)S(1)}, bf16[32,5120]{1,0:T(8,128)(2,1)S(1)}, u32[]{:S(2)}, u32[]{:S(2)}) collective-permute-start(bf16[32,5120]{1,0:T(8,128)(2,1)S(1)} %get-tuple-element.27), channel_id=1, source_target_pairs={{0,8},{4,12},{8,0},{12,4},{16,24},{20,28},{24,16},{28,20},{1,9},{5... | collective-permute-start | bytes 983048 | tf_op jit(solution)/shard_map/ppermute | solution.py:32
  35.9 9.0 %collective-permute-start.14 = (bf16[64,2048]{1,0:T(8,128)(2,1)S(1)}, bf16[64,2048]{1,0:T(8,128)(2,1)S(1)}, u32[]{:S(2)}, u32[]{:S(2)}) collective-permute-start(bf16[64,2048]{1,0:T(8,128)(2,1)S(1)} %collective-permute-done.12.refs_4_), channel_id=1, source_target_pairs={{0,1},{1,2},{2,3},{3,0},{4,5},{5,6},{6,7},{7,4},{8,9},{9,10},{10,1... | collective-permute-start | bytes 786440 | tf_op jit(solution)/shard_map/ppermute | solution.py:252
  36.2 10.0 %collective-permute-start.15 = (bf16[64,2048]{1,0:T(8,128)(2,1)S(1)}, bf16[64,2048]{1,0:T(8,128)(2,1)S(1)}, u32[]{:S(2)}, u32[]{:S(2)}) collective-permute-start(bf16[64,2048]{1,0:T(8,128)(2,1)S(1)} %collective-permute-done.13.refs_5_), channel_id=1, source_target_pairs={{0,1},{1,2},{2,3},{3,0},{4,5},{5,6},{6,7},{7,4},{8,9},{9,10},{10,1... | collective-permute-start | bytes 786440 | tf_op jit(solution)/shard_map/ppermute | solution.py:257
  37.8 7.1 %collective-permute-start.4 = (bf16[32,5120]{1,0:T(8,128)(2,1)S(1)}, bf16[32,5120]{1,0:T(8,128)(2,1)S(1)}, u32[]{:S(2)}, u32[]{:S(2)}) collective-permute-start(bf16[32,5120]{1,0:T(8,128)(2,1)S(1)} %get-tuple-element.28), channel_id=1, source_target_pairs={{0,16},{4,20},{8,24},{12,28},{16,0},{20,4},{24,8},{28,12},{1,17},{... | collective-permute-start | bytes 983048 | tf_op jit(solution)/shard_map/ppermute | solution.py:32
  50.5 56.1 %copy-start.3 = (f32[5120]{0:T(1024)S(1)}, f32[5120]{0:T(1024)}, u32[]{:S(2)}) copy-start(f32[5120]{0:T(1024)} %param.13) | copy-start | bytes 61444
  50.5 20.2 %collective-permute-start.19 = (bf16[64,2560]{1,0:T(8,128)(2,1)S(1)}, bf16[64,2560]{1,0:T(8,128)(2,1)S(1)}, u32[]{:S(2)}, u32[]{:S(2)}) collective-permute-start(bf16[64,2560]{1,0:T(8,128)(2,1)S(1)} %get-tuple-element.24), channel_id=1, source_target_pairs={{0,1},{1,2},{2,3},{3,0},{4,5},{5,6},{6,7},{7,4},{8,9},{9,10},{10,1... | collective-permute-start | bytes 983048 | tf_op jit(solution)/shard_map/ppermute | solution.py:295
  50.9 43.0 %collective-permute-start.20 = (bf16[64,2560]{1,0:T(8,128)(2,1)S(1)}, bf16[64,2560]{1,0:T(8,128)(2,1)S(1)}, u32[]{:S(2)}, u32[]{:S(2)}) collective-permute-start(bf16[64,2560]{1,0:T(8,128)(2,1)S(1)} %get-tuple-element.25), channel_id=1, source_target_pairs={{0,2},{1,3},{2,0},{3,1},{4,6},{5,7},{6,4},{7,5},{8,10},{9,11},{10,... | collective-permute-start | bytes 983048 | tf_op jit(solution)/shard_map/ppermute | solution.py:295
  55.2 38.7 %collective-permute-start.21 = (bf16[64,2560]{1,0:T(8,128)(2,1)S(1)}, bf16[64,2560]{1,0:T(8,128)(2,1)S(1)}, u32[]{:S(2)}, u32[]{:S(2)}) collective-permute-start(bf16[64,2560]{1,0:T(8,128)(2,1)S(1)} %get-tuple-element.26), channel_id=1, source_target_pairs={{0,3},{1,0},{2,1},{3,2},{4,7},{5,4},{6,5},{7,6},{8,11},{9,8},{10,9... | collective-permute-start | bytes 983048 | tf_op jit(solution)/shard_map/ppermute | solution.py:295
  59.5 40.1 %collective-permute-start.16 = (bf16[64,2560]{1,0:T(8,128)(2,1)S(1)}, bf16[64,2560]{1,0:T(8,128)(2,1)S(1)}, u32[]{:S(2)}, u32[]{:S(2)}) collective-permute-start(bf16[64,2560]{1,0:T(8,128)(2,1)S(1)} %get-tuple-element.20), channel_id=1, source_target_pairs={{0,1},{1,2},{2,3},{3,0},{4,5},{5,6},{6,7},{7,4},{8,9},{9,10},{10,1... | collective-permute-start | bytes 983048 | tf_op jit(solution)/shard_map/ppermute | solution.py:295
  61.5 41.6 %collective-permute-start.17 = (bf16[64,2560]{1,0:T(8,128)(2,1)S(1)}, bf16[64,2560]{1,0:T(8,128)(2,1)S(1)}, u32[]{:S(2)}, u32[]{:S(2)}) collective-permute-start(bf16[64,2560]{1,0:T(8,128)(2,1)S(1)} %get-tuple-element.21), channel_id=1, source_target_pairs={{0,2},{1,3},{2,0},{3,1},{4,6},{5,7},{6,4},{7,5},{8,10},{9,11},{10,... | collective-permute-start | bytes 983048 | tf_op jit(solution)/shard_map/ppermute | solution.py:295
  70.7 35.9 %collective-permute-start.18 = (bf16[64,2560]{1,0:T(8,128)(2,1)S(1)}, bf16[64,2560]{1,0:T(8,128)(2,1)S(1)}, u32[]{:S(2)}, u32[]{:S(2)}) collective-permute-start(bf16[64,2560]{1,0:T(8,128)(2,1)S(1)} %get-tuple-element.22), channel_id=1, source_target_pairs={{0,3},{1,0},{2,1},{3,2},{4,7},{5,4},{6,5},{7,6},{8,11},{9,8},{10,9... | collective-permute-start | bytes 983048 | tf_op jit(solution)/shard_map/ppermute | solution.py:295

commit v2 on v1

v2 whole, which is shorter than its diff:
```python
import functools
import math

import jax
import jax.numpy as jnp
from jax import lax
from jax.experimental import pallas as pl
from jax.experimental.pallas import tpu as pltpu
from jax.sharding import PartitionSpec as P

QUERY_HEADS = 40
KEY_VALUE_HEADS = 8
PORTION = QUERY_HEADS // KEY_VALUE_HEADS
HEAD_SIZE = 128
BLK = 32
NSWAP = 2
LANES = 128

NEGATIVE_LARGE = -1e30
HEAD_GROUPS = (4, 4)
MIB = 1024 * 1024


def params(mib=60):
    return pltpu.CompilerParams(vmem_limit_bytes=mib * MIB)


def ring(step, size):
    return [(i, (i + step) % size) for i in range(size)]


def block_order(listed, n_blocks):
    low, high = listed
    first = jnp.where(low > 0, 0, jnp.where(high > 1, 1, 2))
    return [first, n_blocks * (n_blocks - 1) // 2 - first - low - high, low, high]


def split_kernel(ids, q_ref, kv_ref, kv_rest, kv_listed, q_listed, kv_held, q_held, held_pos, sems):
    n_blocks = kv_ref.shape[0] // BLK
    n_rest = n_blocks - NSWAP
    kv_width = kv_ref.shape[1]
    order = block_order((ids[0, 0, 0], ids[0, 0, 1]), n_blocks)
    moves = []
    for b, block in enumerate(order):
        here = pl.ds(pl.multiple_of(block * BLK, BLK), BLK)
        held = pl.ds(b * BLK, BLK)
        if b < n_rest:
            target = kv_rest.at[held, pl.ds(0, kv_width)]
            moves.append((kv_ref.at[here], kv_held.at[held], target))
        else:
            there = pl.ds((b - n_rest) * BLK, BLK)
            moves.append((kv_ref.at[here], kv_held.at[held], kv_listed.at[there]))
            moves.append((q_ref.at[here], q_held.at[there], q_listed.at[there]))
    loads, stores = [], []
    for i, (source, middle, target) in enumerate(moves):
        loads.append(pltpu.make_async_copy(source, middle, sems.at[0, i]))
        stores.append(pltpu.make_async_copy(middle, target, sems.at[1, i]))
    for load in loads:
        load.start()
    shape = held_pos.shape
    row = lax.broadcasted_iota(jnp.int32, shape, 0)
    lane = lax.broadcasted_iota(jnp.int32, shape, 1)
    pos = jnp.zeros(shape, jnp.int32)
    for b, block in enumerate(order):
        at = b % n_rest * BLK
        here = (row >= at) & (row < at + BLK) & (lane == b // n_rest)
        pos = jnp.where(here, row - at + block * BLK, pos)
    held_pos[...] = pos.astype(jnp.bfloat16)
    tail = kv_rest.at[:, pl.ds(kv_width, LANES)]
    stores.append(pltpu.make_async_copy(held_pos, tail, sems.at[1, len(moves)]))
    stores[-1].start()
    for load, store in zip(loads, stores):
        load.wait()
        store.start()
    for store in stores:
        store.wait()


def split_blocks(swap_ids, queries, key_values):
    row_list, width = queries.shape
    kv_width = key_values.shape[1]
    some = NSWAP * BLK
    far = pl.BlockSpec(memory_space=pl.ANY)
    return pl.pallas_call(
        split_kernel,
        out_shape=(
            jax.ShapeDtypeStruct((row_list - some, kv_width + LANES), jnp.bfloat16),
            jax.ShapeDtypeStruct((some, kv_width), jnp.bfloat16),
            jax.ShapeDtypeStruct((some, width), jnp.bfloat16),
        ),
        in_specs=[pl.BlockSpec(memory_space=pltpu.SMEM), far, far],
        out_specs=(far,) * 3,
        scratch_shapes=[
            pltpu.VMEM((row_list, kv_width), jnp.bfloat16),
            pltpu.VMEM((some, width), jnp.bfloat16),
            pltpu.VMEM((row_list - some, LANES), jnp.bfloat16),
            pltpu.SemaphoreType.DMA((2, row_list // BLK + NSWAP + 1)),
        ],
        compiler_params=params(60),
        name="split_blocks",
    )(swap_ids, queries, key_values)


def back(value, n_inner):
    return lax.ppermute(value, "inner", ring(1, n_inner))


def gather_keys(mask, n_outer, n_inner, n_back, kv_rest, kv_listed, q_listed):
    def swap(value):
        return lax.ppermute(value, "outer", [(i, i ^ mask) for i in range(n_outer)])

    def reach_back(value):
        parts = [value]
        for _ in range(n_back):
            parts.append(back(parts[-1], n_inner))
        return parts

    rest = reach_back(kv_rest)
    listed = reach_back(swap(kv_listed))
    return swap(q_listed), rest[1:], listed


def fill_tables(n_out, lengths, dest, pos_refs, bias, chosen):
    row_list, n_all = bias.shape
    me = lax.axis_index("inner")
    lane = lax.broadcasted_iota(jnp.int32, (1, LANES), 1)
    key_pos = []
    for back, ref in enumerate(pos_refs):
        for which in range(2):
            pick = (lane == which).astype(jnp.bfloat16)
            pos = lax.dot_general(
                pick, ref[...], (((1,), (1,)), ((), ())), preferred_element_type=jnp.float32
            ).astype(jnp.int32)
            key_pos.append(jnp.where(me >= back, pos + (me - back) * row_list, -1))
    key_pos = jnp.concatenate(key_pos, axis=1)
    q_pos = me * row_list + lax.broadcasted_iota(jnp.int32, (row_list, 1), 0)
    end, start = 0, jnp.zeros((row_list, 1), jnp.int32)
    for k in range(lengths.shape[1]):
        end = end + lengths[0, k]
        start = jnp.where(q_pos >= end, end, start)
    bias[...] = jnp.where((key_pos <= q_pos) & (key_pos >= start), 0.0, NEGATIVE_LARGE)

    capacity = chosen.shape[0] // n_out
    square = (row_list, row_list)
    named = lax.broadcasted_iota(jnp.int32, square, 0) == dest[...]
    earlier = lax.broadcasted_iota(jnp.int32, square, 0) < lax.broadcasted_iota(jnp.int32, square, 1)
    before = jnp.dot(
        named.astype(jnp.bfloat16), earlier.astype(jnp.bfloat16), preferred_element_type=jnp.float32
    )
    rank = jnp.sum(jnp.where(named, before, 0.0), axis=0, keepdims=True).astype(jnp.int32)
    place = lax.rem(dest[...] - me + n_out, n_out) * capacity + rank
    slots = lax.broadcasted_iota(jnp.int32, chosen.shape, 0)
    chosen[...] = (slots == place).astype(jnp.bfloat16)


def attend_kernel(n_keys, n_out, ids, lengths, dest, q_ref, q_new, *refs):
    pos_refs = refs[: n_keys // 2]
    kv_refs = refs[n_keys // 2 : n_keys // 2 + n_keys]
    outs = refs[-3 - n_out : -3]
    q_all, bias, chosen = refs[-3:]
    row_list = q_ref.shape[0]
    capacity = outs[0].shape[0]

    @pl.when(pl.program_id(0) == 0)
    def _():
        fill_tables(n_out, lengths, dest, pos_refs, bias, chosen)

    q_all[...] = q_ref[...]
    for part in range(NSWAP):
        at = pl.multiple_of(ids[0, 0, part] * BLK, BLK)
        q_all[pl.ds(at, BLK), :] = q_new[part * BLK : (part + 1) * BLK, :]

    key = jnp.concatenate([ref[:, :HEAD_SIZE] for ref in kv_refs], axis=0)
    value = jnp.concatenate([ref[:, HEAD_SIZE:] for ref in kv_refs], axis=0)
    query = jnp.concatenate(
        [q_all[:, h * HEAD_SIZE : (h + 1) * HEAD_SIZE] for h in range(PORTION)], axis=0
    )
    scores = lax.dot_general(
        query, key, (((1,), (1,)), ((), ())), preferred_element_type=jnp.float32
    )
    scores = scores + jnp.concatenate([bias[...]] * PORTION, axis=0)
    top = jnp.max(scores, axis=1, keepdims=True)
    expo = jnp.exp2((scores - top) * (math.log2(math.e) / math.sqrt(HEAD_SIZE)))
    total = jnp.sum(expo, axis=1, keepdims=True)
    attn = jnp.dot(expo.astype(jnp.bfloat16), value, preferred_element_type=jnp.float32)
    attn = (attn / total).astype(jnp.bfloat16)
    attn = jnp.concatenate(
        [attn[h * row_list : (h + 1) * row_list] for h in range(PORTION)], axis=1
    )
    routed = jnp.dot(chosen[...], attn, preferred_element_type=jnp.float32).astype(jnp.bfloat16)
    for k in range(n_out):
        outs[k][...] = routed[k * capacity : (k + 1) * capacity]


def attend(first, heads, swap_ids, doc_lengths, dest, queries, q_new, kv_parts, n_out, before):
    row_list = queries.shape[0]
    capacity = NSWAP * row_list // n_out
    wide = PORTION * HEAD_SIZE
    tail = KEY_VALUE_HEADS * 2 * HEAD_SIZE // LANES
    n_all = sum(part.shape[0] for part in kv_parts)

    def columns(rows, width):
        return pl.BlockSpec((rows, width), lambda s: (0, first + s))

    return pl.pallas_call(
        functools.partial(attend_kernel, len(kv_parts), n_out),
        grid=(heads,),
        out_shape=[jax.ShapeDtypeStruct((capacity, heads * wide), jnp.bfloat16)] * n_out,
        in_specs=[
            pl.BlockSpec(memory_space=pltpu.SMEM),
            pl.BlockSpec(memory_space=pltpu.SMEM),
            pl.BlockSpec((1, row_list), lambda s: (0, 0)),
            columns(row_list, wide),
            columns(NSWAP * BLK, wide),
        ]
        + [pl.BlockSpec((kv_parts[0].shape[0], LANES), lambda s: (0, tail))] * (len(kv_parts) // 2)
        + [columns(part.shape[0], 2 * HEAD_SIZE) for part in kv_parts]
        + [pl.BlockSpec(memory_space=pl.ANY)] * len(before),
        out_specs=[pl.BlockSpec((capacity, wide), lambda s: (0, s))] * n_out,
        scratch_shapes=[
            pltpu.VMEM((row_list, wide), jnp.bfloat16),
            pltpu.VMEM((row_list, n_all), jnp.float32),
            pltpu.VMEM((n_out * capacity, row_list), jnp.bfloat16),
        ],
        compiler_params=params(16 if before else 60),
        cost_estimate=pl.CostEstimate(
            flops=heads * PORTION * row_list * n_all * HEAD_SIZE * 4,
            bytes_accessed=heads * (4 * wide * row_list * 2 + n_all * 512),
            transcendentals=heads * PORTION * row_list * n_all,
        ),
        name="attend",
    )(swap_ids, doc_lengths, dest, queries, q_new, *kv_parts[::2], *kv_parts, *before)


def norm_kernel(n_inner, n_groups, me, gain, *refs):
    parts = refs[: n_inner * n_groups]
    out = refs[n_inner * n_groups]
    held, ready, in_sems, out_sems = refs[n_inner * n_groups + 1 :]
    capacity, width = parts[0].shape[0], held.shape[2]
    loads = []
    for k in range(n_inner):
        column = 0
        for g in range(n_groups):
            ref = parts[g * n_inner + k]
            wide = ref.shape[1]
            loads.append(
                pltpu.make_async_copy(
                    ref, held.at[k, :, pl.ds(column, wide)], in_sems.at[k, g]
                )
            )
            loads[-1].start()
            column += wide
    stores = []
    for k in range(n_inner):
        for g in range(n_groups):
            loads[k * n_groups + g].wait()
        value = held[k].astype(jnp.float32)
        factor = lax.rsqrt(jnp.sum(value * value, axis=1, keepdims=True) / width + 1e-06)
        ready[k] = (value * factor * gain[...]).astype(jnp.bfloat16)
        source = lax.rem(me[0] - k + n_inner, n_inner)
        there = pl.ds(pl.multiple_of(source * capacity, capacity), capacity)
        stores.append(pltpu.make_async_copy(ready.at[k], out.at[there], out_sems.at[k]))
        stores[-1].start()
    for store in stores:
        store.wait()


def normalize(me, gain, parts, n_inner):
    n_groups = len(parts) // n_inner
    capacity = parts[0].shape[0]
    width = gain.shape[0]
    return pl.pallas_call(
        functools.partial(norm_kernel, n_inner, n_groups),
        out_shape=jax.ShapeDtypeStruct((n_inner * capacity, width), jnp.bfloat16),
        in_specs=[
            pl.BlockSpec(memory_space=pltpu.SMEM),
            pl.BlockSpec((1, width), lambda: (0, 0)),
        ]
        + [pl.BlockSpec(memory_space=pl.ANY)] * len(parts),
        out_specs=pl.BlockSpec(memory_space=pl.ANY),
        scratch_shapes=[
            pltpu.VMEM((n_inner, capacity, width), jnp.bfloat16),
            pltpu.VMEM((n_inner, capacity, width), jnp.bfloat16),
            pltpu.SemaphoreType.DMA((n_inner, n_groups)),
            pltpu.SemaphoreType.DMA((n_inner,)),
        ],
        compiler_params=params(16),
        name="normalize",
    )(me.reshape(1), gain.reshape(1, width), *parts)


def shards(queries, key_values, doc_lengths, pairing, swap_ids, dest, gain):
    n_inner = lax.axis_size("inner")
    n_outer = lax.axis_size("outer")
    me = lax.axis_index("inner")
    n_back = n_inner // 2

    kv_rest, kv_listed, q_listed = split_blocks(swap_ids, queries, key_values)
    branches = [
        functools.partial(gather_keys, mask, n_outer, n_inner, n_back)
        for mask in range(1, n_outer)
    ]
    q_new, rest, listed = lax.switch(pairing[0] - 1, branches, kv_rest, kv_listed, q_listed)
    kv_parts = [part for pair in zip([kv_rest] + rest, listed) for part in pair]

    dest_row = dest.reshape(1, -1)
    arrived, first, before = [], 0, []
    for heads in HEAD_GROUPS:
        routed = attend(
            first, heads, swap_ids, doc_lengths, dest_row, queries, q_new, kv_parts, n_inner, before
        )
        before = [routed[0]]
        arrived.append(routed[0])
        for k in range(1, n_inner):
            arrived.append(lax.ppermute(routed[k], "inner", ring(k, n_inner)))
        first += heads
    return normalize(me, gain, arrived, n_inner)


def solution(mesh):
    return jax.shard_map(
        shards,
        mesh=mesh,
        in_specs=(
            P(("outer", "inner"), None),
            P(("outer", "inner"), None),
            P("outer", None),
            P(),
            P("outer", "inner", None),
            P(("outer", "inner"), None),
            P(),
        ),
        out_specs=P(("outer", "inner"), None),
        check_vma=False,
    )
```

time: 110 us -> 99.9 us (0.908); the launches traced: 109 us -> 101 us
  starting transfers between devices: 22.8 us -> 16.7 us
  other arithmetic: 4.36 us -> 0 us
  Pallas kernels: 12.8 us -> 15.8 us
  waiting for transfers between devices: 64.5 us -> 66.8 us
  local copies, waits for them, and re-layouts: 2.8 us -> 1 us
  between operations: 2.12 us -> 0.75 us
    ppermute x16 -> x6, starting transfers between devices: 14.3 us -> 8.12 us  [the longest x4 6.31 us: back(): return lax.ppermute(value, 'inner', ring(1, n_inner))]
    ppermute x6, waiting for transfers between devices: 43.3 us -> 45.8 us  [shards(): arrived.append(lax.ppermute(routed[k], 'inner', ring(k, n_inner)))]
    pallas_call x2, Pallas kernels: 8.58 us -> 10.7 us  [attend(): pl.pallas_call(functools.partial(attend_kernel, len(kv_parts), n_out), gr...]
    unnamed x8 -> x16, local copies, waits for them, and re-layouts: 2.37 us -> 1 us
    another operation x3 -> x0, other arithmetic: 1.18 us -> none
    ppermute x16 -> x6, waiting for transfers between devices: 21.2 us -> 21 us  [the longest x4 15.6 us: back(): return lax.ppermute(value, 'inner', ring(1, n_inner))]
  transfers between devices with their start and end apart: 22 -> 12, of which waited for: 13 -> 11; matrix products, arithmetic and copies ran while one was open for 3% -> 0% of each run, Pallas kernels for 5% -> 5%
where the time goes in v2:
time: 99.9 us; the launch traced here: 101 us
  waiting for transfers between devices  66.8 us (67%)
  starting transfers between devices  16.7 us (17%)
  Pallas kernels  15.8 us (16%)
  local copies, waits for them, and re-layouts  1 us (1%)
    ppermute x6, waiting for transfers between devices, shards(): arrived.append(lax.ppermute(routed[k], 'inner', ring(k, n_inner)))  45.8 us
    ppermute x4, waiting for transfers between devices, back(): return lax.ppermute(value, 'inner', ring(1, n_inner))  15.6 us
    pallas_call x2, Pallas kernels, attend(): pl.pallas_call(functools.partial(attend_kernel, len(kv_parts), n_out), gr...  10.7 us
    ppermute x6, starting transfers between devices, shards(): arrived.append(lax.ppermute(routed[k], 'inner', ring(k, n_inner)))  8.59 us
    ppermute x4, starting transfers between devices, back(): return lax.ppermute(value, 'inner', ring(1, n_inner))  6.31 us
    ppermute x2, waiting for transfers between devices, swap(): return lax.ppermute(value, 'outer', [(i, i ^ mask) for i in range(n_outer)])  5.31 us
    pallas_call x1, Pallas kernels, normalize(): pl.pallas_call(functools.partial(norm_kernel, n_inner, n_groups), out_sha...  2.71 us
    pallas_call x1, Pallas kernels, split_blocks(): pl.pallas_call(split_kernel, out_shape=(jax.ShapeDtypeStruct((row_list -...  2.35 us
  transfers between devices with their start and end apart: 12, of which 11 were waited for; matrix products, arithmetic and copies ran while one was open for 0% of the time, Pallas kernels for 5%

profile of v2, /device:TPU:8, one launch (start us, length us, event | category | flops | bytes accessed | tf_op | source)
XLA Modules:
  0.0 101.0 jit_solution(7446624750151547970)
XLA Ops:
  0.7 2.4 %split_blocks.1 = (bf16[64,2176]{1,0:T(8,128)(2,1)S(1)}, bf16[64,2048]{1,0:T(8,128)(2,1)S(1)}, bf16[64,5120]{1,0:T(8,128)(2,1)S(1)}) custom-call(s32[1,1,2]{2,1,0:T(1,128)} %ids.5, bf16[128,5120]{1,0:T(8,128)(2,1)} %q_ref.5, bf16[128,2048]{1,0:T(8,128)(2,1)} %kv_ref.1), custom_call_target="tpu_custom_call" | custom-call | tf_op jit(solution)/shard_map/split_blocks/pallas_call | solution.py:84
  3.0 0.0 copy-start
  3.0 0.0 copy-start.4
  3.0 0.0 copy-start.5
  3.1 0.0 copy-start.6
  3.1 29.1 %conditional.1 = (bf16[64,5120]{1,0:T(8,128)(2,1)}, bf16[64,2176]{1,0:T(8,128)(2,1)}, bf16[64,2176]{1,0:T(8,128)(2,1)}, bf16[64,2048]{1,0:T(8,128)(2,1)}, bf16[6...) conditional(s32[]{:T(128)} %bitcast.3, (bf16[64,5120]{1,0:T(8,128)(2,1)S(1)}, ...), branch_computations={%region_0.0_spmd, %region_1.0_spmd, %region_2.0_spmd, %region_3.0_... | conditional | bytes 7995680 | solution.py:303
  3.1 1.0 %collective-permute-start.27 = (bf16[64,2048]{1,0:T(8,128)(2,1)S(1)}, bf16[64,2048]{1,0:T(8,128)(2,1)}, u32[]{:S(2)}, u32[]{:S(2)}) collective-permute-start(bf16[64,2048]{1,0:T(8,128)(2,1)S(1)} %get-tuple-element.61), channel_id=1, source_target_pairs={{0,20},{4,16},{8,28},{12,24},{16,4},{20,0},{24,12},{28,8},{1,21},{... | collective-permute-start | bytes 786440 | tf_op jit(solution)/shard_map/cond/branch_4_fun/ppermute | solution.py:110
  4.1 0.8 collective-permute-start.24
  4.9 1.6 %collective-permute-start.25 = (bf16[64,2176]{1,0:T(8,128)(2,1)S(1)}, bf16[64,2176]{1,0:T(8,128)(2,1)}, u32[]{:S(2)}, u32[]{:S(2)}) collective-permute-start(bf16[64,2176]{1,0:T(8,128)(2,1)S(1)} %get-tuple-element.60), channel_id=1, source_target_pairs={{0,1},{1,2},{2,3},{3,0},{4,5},{5,6},{6,7},{7,4},{8,9},{9,10},{10,1... | collective-permute-start | bytes 835592 | tf_op jit(solution)/shard_map/cond/branch_4_fun/ppermute | solution.py:105
  6.5 5.3 %collective-permute-done.27 = bf16[64,2048]{1,0:T(8,128)(2,1)} collective-permute-done((bf16[64,2048]{1,0:T(8,128)(2,1)S(1)}, bf16[64,2048]{1,0:T(8,128)(2,1)}, u32[]{:S(2)}, u32[]{:S(2)}) %collective-permute-start.27) | collective-permute-done | bytes 262176 | tf_op jit(solution)/shard_map/cond/branch_4_fun/ppermute | solution.py:110
  11.8 1.6 %collective-permute-start.28 = (bf16[64,2048]{1,0:T(8,128)(2,1)}, bf16[64,2048]{1,0:T(8,128)(2,1)}, u32[]{:S(2)}, u32[]{:S(2)}) collective-permute-start(bf16[64,2048]{1,0:T(8,128)(2,1)} %collective-permute-done.27), channel_id=1, source_target_pairs={{0,1},{1,2},{2,3},{3,0},{4,5},{5,6},{6,7},{7,4},{8,9},{9,10},{10,1... | collective-permute-start | bytes 786440 | tf_op jit(solution)/shard_map/cond/branch_4_fun/ppermute | solution.py:105
  13.4 0.2 collective-permute-done.25
  13.5 1.6 %collective-permute-start.26 = (bf16[64,2176]{1,0:T(8,128)(2,1)}, bf16[64,2176]{1,0:T(8,128)(2,1)}, u32[]{:S(2)}, u32[]{:S(2)}) collective-permute-start(bf16[64,2176]{1,0:T(8,128)(2,1)} %collective-permute-done.25), channel_id=1, source_target_pairs={{0,1},{1,2},{2,3},{3,0},{4,5},{5,6},{6,7},{7,4},{8,9},{9,10},{10,1... | collective-permute-start | bytes 835592 | tf_op jit(solution)/shard_map/cond/branch_4_fun/ppermute | solution.py:105
  15.1 6.1 %collective-permute-done.28 = bf16[64,2048]{1,0:T(8,128)(2,1)} collective-permute-done((bf16[64,2048]{1,0:T(8,128)(2,1)}, bf16[64,2048]{1,0:T(8,128)(2,1)}, u32[]{:S(2)}, u32[]{:S(2)}) %collective-permute-start.28) | collective-permute-done | bytes 262176 | tf_op jit(solution)/shard_map/cond/branch_4_fun/ppermute | solution.py:105
  21.2 1.6 %collective-permute-start.29 = (bf16[64,2048]{1,0:T(8,128)(2,1)}, bf16[64,2048]{1,0:T(8,128)(2,1)}, u32[]{:S(2)}, u32[]{:S(2)}) collective-permute-start(bf16[64,2048]{1,0:T(8,128)(2,1)} %collective-permute-done.28), channel_id=1, source_target_pairs={{0,1},{1,2},{2,3},{3,0},{4,5},{5,6},{6,7},{7,4},{8,9},{9,10},{10,1... | collective-permute-start | bytes 786440 | tf_op jit(solution)/shard_map/cond/branch_4_fun/ppermute | solution.py:105
  22.8 4.4 %collective-permute-done.26 = bf16[64,2176]{1,0:T(8,128)(2,1)} collective-permute-done((bf16[64,2176]{1,0:T(8,128)(2,1)}, bf16[64,2176]{1,0:T(8,128)(2,1)}, u32[]{:S(2)}, u32[]{:S(2)}) %collective-permute-start.26) | collective-permute-done | bytes 278560 | tf_op jit(solution)/shard_map/cond/branch_4_fun/ppermute | solution.py:105
  27.2 5.0 %collective-permute-done.29 = bf16[64,2048]{1,0:T(8,128)(2,1)} collective-permute-done((bf16[64,2048]{1,0:T(8,128)(2,1)}, bf16[64,2048]{1,0:T(8,128)(2,1)}, u32[]{:S(2)}, u32[]{:S(2)}) %collective-permute-start.29) | collective-permute-done | bytes 262176 | tf_op jit(solution)/shard_map/cond/branch_4_fun/ppermute | solution.py:105
  32.2 5.4 %attend.2 = (bf16[64,2560]{1,0:T(8,128)(2,1)}, bf16[64,2560]{1,0:T(8,128)(2,1)}, bf16[64,2560]{1,0:T(8,128)(2,1)}, bf16[64,2560]{1,0:T(8,128)(2,1)}) custom-call(s32[1,1,2]{2,1,0:T(1,128)} %ids.5, s32[1,8]{1,0:T(1,128)} %lengths.3, s32[1,128]{1,0:T(1,128)} %bitcast.6, bf16[128,5120]{1,0:T(8,128)(2,1)} %q_ref.5, bf16[64,5120]{1,0:T(8,128)(2,1)} %get-tuple-element.88.q_new, ...), custom_call_target="tpu_custom_call" | custom-call | flops 503316480 | bytes 3407872 | tf_op jit(solution)/shard_map/attend/pallas_call | solution.py:205
  37.6 1.6 %collective-permute-start.42 = (bf16[64,2560]{1,0:T(8,128)(2,1)}, bf16[64,2560]{1,0:T(8,128)(2,1)S(1)}, u32[]{:S(2)}, u32[]{:S(2)}) collective-permute-start(bf16[64,2560]{1,0:T(8,128)(2,1)} %get-tuple-element.95), channel_id=1, source_target_pairs={{0,1},{1,2},{2,3},{3,0},{4,5},{5,6},{6,7},{7,4},{8,9},{9,10},{10,1... | collective-permute-start | bytes 983048 | tf_op jit(solution)/shard_map/ppermute | solution.py:315
  39.2 3.1 %collective-permute-start.43 = (bf16[64,2560]{1,0:T(8,128)(2,1)}, bf16[64,2560]{1,0:T(8,128)(2,1)S(1)}, u32[]{:S(2)}, u32[]{:S(2)}) collective-permute-start(bf16[64,2560]{1,0:T(8,128)(2,1)} %get-tuple-element.96), channel_id=1, source_target_pairs={{0,2},{1,3},{2,0},{3,1},{4,6},{5,7},{6,4},{7,5},{8,10},{9,11},{10,... | collective-permute-start | bytes 983048 | tf_op jit(solution)/shard_map/ppermute | solution.py:315
  42.4 0.0 copy-start.1
  42.4 1.0 copy-done.1
  43.4 5.3 %attend.3 = (bf16[64,2560]{1,0:T(8,128)(2,1)S(1)}, bf16[64,2560]{1,0:T(8,128)(2,1)}, bf16[64,2560]{1,0:T(8,128)(2,1)}, bf16[64,2560]{1,0:T(8,128)(2,1)S(1)}) custom-call(s32[1,1,2]{2,1,0:T(1,128)S(1)} %copy-done.4, s32[1,8]{1,0:T(1,128)S(1)} %copy-done.5, s32[1,128]{1,0:T(1,128)S(1)} %bitcast.7, bf16[128,5120]{1,0:T(8,128)(2,1)S(1)} %copy-done, ...), custom_call_target="tpu_custom_call" | custom-call | flops 503316480 | bytes 3407872 | tf_op jit(solution)/shard_map/attend/pallas_call | solution.py:205
  48.6 2.1 %collective-permute-start.45 = (bf16[64,2560]{1,0:T(8,128)(2,1)}, bf16[64,2560]{1,0:T(8,128)(2,1)S(1)}, u32[]{:S(2)}, u32[]{:S(2)}) collective-permute-start(bf16[64,2560]{1,0:T(8,128)(2,1)} %get-tuple-element.99), channel_id=1, source_target_pairs={{0,1},{1,2},{2,3},{3,0},{4,5},{5,6},{6,7},{7,4},{8,9},{9,10},{10,1... | collective-permute-start | bytes 983048 | tf_op jit(solution)/shard_map/ppermute | solution.py:315
  50.7 1.8 %collective-permute-start.46 = (bf16[64,2560]{1,0:T(8,128)(2,1)}, bf16[64,2560]{1,0:T(8,128)(2,1)S(1)}, u32[]{:S(2)}, u32[]{:S(2)}) collective-permute-start(bf16[64,2560]{1,0:T(8,128)(2,1)} %get-tuple-element.100), channel_id=1, source_target_pairs={{0,2},{1,3},{2,0},{3,1},{4,6},{5,7},{6,4},{7,5},{8,10},{9,11},{10,... | collective-permute-start | bytes 983048 | tf_op jit(solution)/shard_map/ppermute | solution.py:315
  52.5 8.7 %collective-permute-done.42.refs_1_ = bf16[64,2560]{1,0:T(8,128)(2,1)S(1)} collective-permute-done((bf16[64,2560]{1,0:T(8,128)(2,1)}, bf16[64,2560]{1,0:T(8,128)(2,1)S(1)}, u32[]{:S(2)}, u32[]{:S(2)}) %collective-permute-start.42) | collective-permute-done | bytes 327712 | tf_op jit(solution)/shard_map/ppermute | solution.py:315
  61.2 21.6 %collective-permute-done.43.refs_2_ = bf16[64,2560]{1,0:T(8,128)(2,1)S(1)} collective-permute-done((bf16[64,2560]{1,0:T(8,128)(2,1)}, bf16[64,2560]{1,0:T(8,128)(2,1)S(1)}, u32[]{:S(2)}, u32[]{:S(2)}) %collective-permute-start.43) | collective-permute-done | bytes 327712 | tf_op jit(solution)/shard_map/ppermute | solution.py:315
  82.7 2.5 %collective-permute-done.44.refs_3_ = bf16[64,2560]{1,0:T(8,128)(2,1)S(1)} collective-permute-done((bf16[64,2560]{1,0:T(8,128)(2,1)}, bf16[64,2560]{1,0:T(8,128)(2,1)S(1)}, u32[]{:S(2)}, u32[]{:S(2)}) %collective-permute-start.44) | collective-permute-done | bytes 327712 | tf_op jit(solution)/shard_map/ppermute | solution.py:315
  85.2 4.7 %collective-permute-done.45.refs_5_ = bf16[64,2560]{1,0:T(8,128)(2,1)S(1)} collective-permute-done((bf16[64,2560]{1,0:T(8,128)(2,1)}, bf16[64,2560]{1,0:T(8,128)(2,1)S(1)}, u32[]{:S(2)}, u32[]{:S(2)}) %collective-permute-start.45) | collective-permute-done | bytes 327712 | tf_op jit(solution)/shard_map/ppermute | solution.py:315
  89.9 5.4 %collective-permute-done.46.refs_6_ = bf16[64,2560]{1,0:T(8,128)(2,1)S(1)} collective-permute-done((bf16[64,2560]{1,0:T(8,128)(2,1)}, bf16[64,2560]{1,0:T(8,128)(2,1)S(1)}, u32[]{:S(2)}, u32[]{:S(2)}) %collective-permute-start.46) | collective-permute-done | bytes 327712 | tf_op jit(solution)/shard_map/ppermute | solution.py:315
  95.3 3.0 %collective-permute-done.47.refs_7_ = bf16[64,2560]{1,0:T(8,128)(2,1)S(1)} collective-permute-done((bf16[64,2560]{1,0:T(8,128)(2,1)S(1)}, bf16[64,2560]{1,0:T(8,128)(2,1)S(1)}, u32[]{:S(2)}, u32[]{:S(2)}) %collective-permute-start.47) | collective-permute-done | bytes 327712 | tf_op jit(solution)/shard_map/ppermute | solution.py:315
  98.3 2.7 %normalize.1 = bf16[256,5120]{1,0:T(8,128)(2,1)} custom-call(s32[1]{0:T(128)} %bitcast.me, f32[1,5120]{1,0:T(1,128)S(1)} %bitcast.5, bf16[64,2560]{1,0:T(8,128)(2,1)S(1)} %copy-done.2, bf16[64,2560]{1,0:T(8,128)(2,1)S(1)} %collective-permute-done.42.refs_1_, bf16[64,2560]{1,0:T(8,128)(2,1)S(1)} %collective-permute-done.43.refs_2_, ...), custom_call_target="tpu_custom_call" | custom-call | tf_op jit(solution)/shard_map/normalize/pallas_call | solution.py:272
  (13 shorter events, 0.0 us)
Async XLA Ops:
  3.0 34.6 %copy-start.7 = (bf16[64,2176]{1,0:T(8,128)(2,1)}, bf16[64,2176]{1,0:T(8,128)(2,1)S(1)}, u32[]{:S(2)}) copy-start(bf16[64,2176]{1,0:T(8,128)(2,1)S(1)} %get-tuple-element.86.refs_0_.refs_3_) | copy-start | bytes 835588
  3.0 39.3 %copy-start = (bf16[128,5120]{1,0:T(8,128)(2,1)S(1)}, bf16[128,5120]{1,0:T(8,128)(2,1)}, u32[]{:S(2)}) copy-start(bf16[128,5120]{1,0:T(8,128)(2,1)} %q_ref.5) | copy-start | bytes 3932164
  3.0 39.3 %copy-start.4 = (s32[1,1,2]{2,1,0:T(1,128)S(1)}, s32[1,1,2]{2,1,0:T(1,128)}, u32[]{:S(2)}) copy-start(s32[1,1,2]{2,1,0:T(1,128)} %ids.5) | copy-start | bytes 28
  3.0 39.3 %copy-start.5 = (s32[1,8]{1,0:T(1,128)S(1)}, s32[1,8]{1,0:T(1,128)}, u32[]{:S(2)}) copy-start(s32[1,8]{1,0:T(1,128)} %lengths.3) | copy-start | bytes 100
  3.1 39.3 %copy-start.6 = (s32[128,1]{0,1:T(1,128)S(1)}, s32[128,1]{0,1:T(1,128)}, u32[]{:S(2)}) copy-start(s32[128,1]{0,1:T(1,128)} %param.19) | copy-start | bytes 1540
  3.1 8.7 %collective-permute-start.27 = (bf16[64,2048]{1,0:T(8,128)(2,1)S(1)}, bf16[64,2048]{1,0:T(8,128)(2,1)}, u32[]{:S(2)}, u32[]{:S(2)}) collective-permute-start(bf16[64,2048]{1,0:T(8,128)(2,1)S(1)} %get-tuple-element.61), channel_id=1, source_target_pairs={{0,20},{4,16},{8,28},{12,24},{16,4},{20,0},{24,12},{28,8},{1,21},{... | collective-permute-start | bytes 786440 | tf_op jit(solution)/shard_map/cond/branch_4_fun/ppermute | solution.py:110
  4.1 23.1 %collective-permute-start.24 = (bf16[64,5120]{1,0:T(8,128)(2,1)S(1)}, bf16[64,5120]{1,0:T(8,128)(2,1)}, u32[]{:S(2)}, u32[]{:S(2)}) collective-permute-start(bf16[64,5120]{1,0:T(8,128)(2,1)S(1)} %get-tuple-element.59), channel_id=1, source_target_pairs={{0,20},{4,16},{8,28},{12,24},{16,4},{20,0},{24,12},{28,8},{1,21},{... | collective-permute-start | bytes 1966088 | tf_op jit(solution)/shard_map/cond/branch_4_fun/ppermute | solution.py:110
  4.9 8.6 %collective-permute-start.25 = (bf16[64,2176]{1,0:T(8,128)(2,1)S(1)}, bf16[64,2176]{1,0:T(8,128)(2,1)}, u32[]{:S(2)}, u32[]{:S(2)}) collective-permute-start(bf16[64,2176]{1,0:T(8,128)(2,1)S(1)} %get-tuple-element.60), channel_id=1, source_target_pairs={{0,1},{1,2},{2,3},{3,0},{4,5},{5,6},{6,7},{7,4},{8,9},{9,10},{10,1... | collective-permute-start | bytes 835592 | tf_op jit(solution)/shard_map/cond/branch_4_fun/ppermute | solution.py:105
  11.8 9.4 %collective-permute-start.28 = (bf16[64,2048]{1,0:T(8,128)(2,1)}, bf16[64,2048]{1,0:T(8,128)(2,1)}, u32[]{:S(2)}, u32[]{:S(2)}) collective-permute-start(bf16[64,2048]{1,0:T(8,128)(2,1)} %collective-permute-done.27), channel_id=1, source_target_pairs={{0,1},{1,2},{2,3},{3,0},{4,5},{5,6},{6,7},{7,4},{8,9},{9,10},{10,1... | collective-permute-start | bytes 786440 | tf_op jit(solution)/shard_map/cond/branch_4_fun/ppermute | solution.py:105
  13.5 13.7 %collective-permute-start.26 = (bf16[64,2176]{1,0:T(8,128)(2,1)}, bf16[64,2176]{1,0:T(8,128)(2,1)}, u32[]{:S(2)}, u32[]{:S(2)}) collective-permute-start(bf16[64,2176]{1,0:T(8,128)(2,1)} %collective-permute-done.25), channel_id=1, source_target_pairs={{0,1},{1,2},{2,3},{3,0},{4,5},{5,6},{6,7},{7,4},{8,9},{9,10},{10,1... | collective-permute-start | bytes 835592 | tf_op jit(solution)/shard_map/cond/branch_4_fun/ppermute | solution.py:105
  21.2 10.9 %collective-permute-start.29 = (bf16[64,2048]{1,0:T(8,128)(2,1)}, bf16[64,2048]{1,0:T(8,128)(2,1)}, u32[]{:S(2)}, u32[]{:S(2)}) collective-permute-start(bf16[64,2048]{1,0:T(8,128)(2,1)} %collective-permute-done.28), channel_id=1, source_target_pairs={{0,1},{1,2},{2,3},{3,0},{4,5},{5,6},{6,7},{7,4},{8,9},{9,10},{10,1... | collective-permute-start | bytes 786440 | tf_op jit(solution)/shard_map/cond/branch_4_fun/ppermute | solution.py:105
  32.2 66.2 %copy-start.3 = (f32[5120]{0:T(1024)S(1)}, f32[5120]{0:T(1024)}, u32[]{:S(2)}) copy-start(f32[5120]{0:T(1024)} %param.20) | copy-start | bytes 61444
  37.6 23.6 %collective-permute-start.42 = (bf16[64,2560]{1,0:T(8,128)(2,1)}, bf16[64,2560]{1,0:T(8,128)(2,1)S(1)}, u32[]{:S(2)}, u32[]{:S(2)}) collective-permute-start(bf16[64,2560]{1,0:T(8,128)(2,1)} %get-tuple-element.95), channel_id=1, source_target_pairs={{0,1},{1,2},{2,3},{3,0},{4,5},{5,6},{6,7},{7,4},{8,9},{9,10},{10,1... | collective-permute-start | bytes 983048 | tf_op jit(solution)/shard_map/ppermute | solution.py:315
  39.2 43.5 %collective-permute-start.43 = (bf16[64,2560]{1,0:T(8,128)(2,1)}, bf16[64,2560]{1,0:T(8,128)(2,1)S(1)}, u32[]{:S(2)}, u32[]{:S(2)}) collective-permute-start(bf16[64,2560]{1,0:T(8,128)(2,1)} %get-tuple-element.96), channel_id=1, source_target_pairs={{0,2},{1,3},{2,0},{3,1},{4,6},{5,7},{6,4},{7,5},{8,10},{9,11},{10,... | collective-permute-start | bytes 983048 | tf_op jit(solution)/shard_map/ppermute | solution.py:315
  42.3 42.9 %collective-permute-start.44 = (bf16[64,2560]{1,0:T(8,128)(2,1)}, bf16[64,2560]{1,0:T(8,128)(2,1)S(1)}, u32[]{:S(2)}, u32[]{:S(2)}) collective-permute-start(bf16[64,2560]{1,0:T(8,128)(2,1)} %get-tuple-element.97), channel_id=1, source_target_pairs={{0,3},{1,0},{2,1},{3,2},{4,7},{5,4},{6,5},{7,6},{8,11},{9,8},{10,9... | collective-permute-start | bytes 983048 | tf_op jit(solution)/shard_map/ppermute | solution.py:315
  42.4 1.0 copy-start.1
  43.3 55.0 %copy-start.2 = (bf16[64,2560]{1,0:T(8,128)(2,1)S(1)}, bf16[64,2560]{1,0:T(8,128)(2,1)}, u32[]{:S(2)}) copy-start(bf16[64,2560]{1,0:T(8,128)(2,1)} %get-tuple-element.94.refs_9_.refs_0_) | copy-start | bytes 983044
  48.6 41.3 %collective-permute-start.45 = (bf16[64,2560]{1,0:T(8,128)(2,1)}, bf16[64,2560]{1,0:T(8,128)(2,1)S(1)}, u32[]{:S(2)}, u32[]{:S(2)}) collective-permute-start(bf16[64,2560]{1,0:T(8,128)(2,1)} %get-tuple-element.99), channel_id=1, source_target_pairs={{0,1},{1,2},{2,3},{3,0},{4,5},{5,6},{6,7},{7,4},{8,9},{9,10},{10,1... | collective-permute-start | bytes 983048 | tf_op jit(solution)/shard_map/ppermute | solution.py:315
  50.7 44.7 %collective-permute-start.46 = (bf16[64,2560]{1,0:T(8,128)(2,1)}, bf16[64,2560]{1,0:T(8,128)(2,1)S(1)}, u32[]{:S(2)}, u32[]{:S(2)}) collective-permute-start(bf16[64,2560]{1,0:T(8,128)(2,1)} %get-tuple-element.100), channel_id=1, source_target_pairs={{0,2},{1,3},{2,0},{3,1},{4,6},{5,7},{6,4},{7,5},{8,10},{9,11},{10,... | collective-permute-start | bytes 983048 | tf_op jit(solution)/shard_map/ppermute | solution.py:315
  61.2 37.2 %collective-permute-start.47 = (bf16[64,2560]{1,0:T(8,128)(2,1)S(1)}, bf16[64,2560]{1,0:T(8,128)(2,1)S(1)}, u32[]{:S(2)}, u32[]{:S(2)}) collective-permute-start(bf16[64,2560]{1,0:T(8,128)(2,1)S(1)} %get-tuple-element.101), channel_id=1, source_target_pairs={{0,3},{1,0},{2,1},{3,2},{4,7},{5,4},{6,5},{7,6},{8,11},{9,8},{10,9... | collective-permute-start | bytes 983048 | tf_op jit(solution)/shard_map/ppermute | solution.py:315

commit v3 on v2

v3 whole, which is shorter than its diff:
```python
import functools
import math

import jax
import jax.numpy as jnp
from jax import lax
from jax.experimental import pallas as pl
from jax.experimental.pallas import tpu as pltpu
from jax.sharding import PartitionSpec as P

QUERY_HEADS = 40
KEY_VALUE_HEADS = 8
PORTION = QUERY_HEADS // KEY_VALUE_HEADS
HEAD_SIZE = 128
BLK = 32
NSWAP = 2
LANES = 128

NEGATIVE_LARGE = -1e30
HEAD_GROUPS = (2, 6)
PLACE_EARLY = 30_000_000_000
PER_STEP = 2
MIB = 1024 * 1024


def params(mib=60):
    return pltpu.CompilerParams(vmem_limit_bytes=mib * MIB)


def ring(step, size):
    return [(i, (i + step) % size) for i in range(size)]


def block_order(listed, n_blocks):
    low, high = listed
    first = jnp.where(low > 0, 0, jnp.where(high > 1, 1, 2))
    return [first, n_blocks * (n_blocks - 1) // 2 - first - low - high, low, high]


def split_kernel(ids, q_ref, kv_ref, kv_rest, kv_listed, q_listed, sems):
    n_blocks = kv_ref.shape[0] // BLK
    n_rest = n_blocks - NSWAP
    kv_width = kv_ref.shape[1]
    order = block_order((ids[0, 0, 0], ids[0, 0, 1]), n_blocks)
    copies = []
    for b, block in enumerate(order):
        here = pl.ds(pl.multiple_of(block * BLK, BLK), BLK)
        there = pl.ds(b % n_rest * BLK, BLK)
        if b < n_rest:
            pairs = [(kv_ref, kv_rest.at[there, pl.ds(0, kv_width)])]
        else:
            pairs = [(kv_ref, kv_listed.at[there]), (q_ref, q_listed.at[there])]
        for source, target in pairs:
            copies.append(pltpu.make_async_copy(source.at[here], target, sems.at[len(copies)]))
            copies[-1].start()
    shape = (kv_rest.shape[0], LANES)
    row = lax.broadcasted_iota(jnp.int32, shape, 0)
    lane = lax.broadcasted_iota(jnp.int32, shape, 1)
    pos = jnp.zeros(shape, jnp.int32)
    for b, block in enumerate(order):
        at = b % n_rest * BLK
        here = (row >= at) & (row < at + BLK) & (lane == b // n_rest)
        pos = jnp.where(here, row - at + block * BLK, pos)
    kv_rest[:, kv_width:] = pos.astype(jnp.bfloat16)
    for copy in copies:
        copy.wait()


def split_blocks(swap_ids, queries, key_values):
    row_list, width = queries.shape
    kv_width = key_values.shape[1]
    some = NSWAP * BLK
    far = pl.BlockSpec(memory_space=pltpu.HBM)
    near = pl.BlockSpec(memory_space=pltpu.VMEM)
    return pl.pallas_call(
        split_kernel,
        out_shape=(
            pltpu.VMEM((row_list - some, kv_width + LANES), jnp.bfloat16),
            pltpu.VMEM((some, kv_width), jnp.bfloat16),
            pltpu.VMEM((some, width), jnp.bfloat16),
        ),
        in_specs=[pl.BlockSpec(memory_space=pltpu.SMEM), far, far],
        out_specs=(near,) * 3,
        scratch_shapes=[pltpu.SemaphoreType.DMA((row_list // BLK + NSWAP,))],
        compiler_params=params(16),
        name="split_blocks",
    )(
        pltpu.with_memory_space_constraint(swap_ids, pltpu.HBM),
        pltpu.with_memory_space_constraint(queries, pltpu.HBM),
        pltpu.with_memory_space_constraint(key_values, pltpu.HBM),
    )


def back(value, n_inner):
    return lax.ppermute(value, "inner", ring(1, n_inner))


def gather_keys(mask, n_outer, n_inner, n_back, doc_lengths, dest, kv_rest, kv_listed, q_listed):
    def swap(value):
        return lax.ppermute(value, "outer", [(i, i ^ mask) for i in range(n_outer)])

    def reach_back(value):
        parts = [value]
        for _ in range(n_back):
            parts.append(back(parts[-1], n_inner))
        return parts

    rest = reach_back(kv_rest)
    listed = reach_back(swap(kv_listed))
    row_list = dest.shape[1]
    n_all = (n_back + 1) * row_list
    bias, chosen = tables(doc_lengths, dest, rest, row_list, n_all, n_inner)
    return swap(q_listed), rest[1:], listed, bias, chosen


def fill_tables(n_out, lengths, dest, pos_refs, bias, chosen):
    row_list, n_all = bias.shape
    me = lax.axis_index("inner")
    lane = lax.broadcasted_iota(jnp.int32, (1, LANES), 1)
    key_pos = []
    for back, ref in enumerate(pos_refs):
        for which in range(2):
            pick = (lane == which).astype(jnp.bfloat16)
            pos = lax.dot_general(
                pick, ref[...], (((1,), (1,)), ((), ())), preferred_element_type=jnp.float32
            ).astype(jnp.int32)
            key_pos.append(jnp.where(me >= back, pos + (me - back) * row_list, -1))
    key_pos = jnp.concatenate(key_pos, axis=1)
    q_pos = me * row_list + lax.broadcasted_iota(jnp.int32, (row_list, 1), 0)
    end, start = 0, jnp.zeros((row_list, 1), jnp.int32)
    for k in range(lengths.shape[1]):
        end = end + lengths[0, k]
        start = jnp.where(q_pos >= end, end, start)
    bias[...] = jnp.where((key_pos <= q_pos) & (key_pos >= start), 0.0, NEGATIVE_LARGE)

    capacity = chosen.shape[0] // n_out
    square = (row_list, row_list)
    named = lax.broadcasted_iota(jnp.int32, square, 0) == dest[...]
    earlier = lax.broadcasted_iota(jnp.int32, square, 0) < lax.broadcasted_iota(jnp.int32, square, 1)
    before = jnp.dot(
        named.astype(jnp.bfloat16), earlier.astype(jnp.bfloat16), preferred_element_type=jnp.float32
    )
    rank = jnp.sum(jnp.where(named, before, 0.0), axis=0, keepdims=True).astype(jnp.int32)
    place = lax.rem(dest[...] - me + n_out, n_out) * capacity + rank
    slots = lax.broadcasted_iota(jnp.int32, chosen.shape, 0)
    chosen[...] = (slots == place).astype(jnp.bfloat16)


def tables_kernel(n_ranges, n_out, lengths, dest, *refs):
    fill_tables(n_out, lengths, dest, refs[:n_ranges], *refs[n_ranges:])


def tables(doc_lengths, dest, rest, row_list, n_all, n_out):
    capacity = NSWAP * row_list // n_out
    tail = rest[0].shape[1] // LANES - 1
    shapes = ((row_list, n_all), (n_out * capacity, row_list))
    return pl.pallas_call(
        functools.partial(tables_kernel, len(rest), n_out),
        grid=(1,),
        out_shape=(
            jax.ShapeDtypeStruct(shapes[0], jnp.float32),
            jax.ShapeDtypeStruct(shapes[1], jnp.bfloat16),
        ),
        in_specs=[
            pl.BlockSpec(memory_space=pltpu.SMEM),
            pl.BlockSpec((1, row_list), lambda s: (0, 0)),
        ]
        + [pl.BlockSpec((part.shape[0], LANES), lambda s: (0, tail)) for part in rest],
        out_specs=[pl.BlockSpec(shape, lambda s: (0, 0)) for shape in shapes],
        compiler_params=params(16),
        name="tables",
    )(doc_lengths, dest, *rest)


def attend_kernel(n_keys, n_out, ids, q_ref, q_new, bias, chosen, *refs):
    kv_refs = refs[:n_keys]
    outs = refs[-1 - n_out : -1]
    q_all = refs[-1]
    row_list = q_ref.shape[0]
    capacity = outs[0].shape[0]

    q_all[...] = q_ref[...]
    for part in range(NSWAP):
        at = pl.multiple_of(ids[0, 0, part] * BLK, BLK)
        q_all[pl.ds(at, BLK), :] = q_new[part * BLK : (part + 1) * BLK, :]

    for j in range(PER_STEP):
        wide = PORTION * HEAD_SIZE
        at = slice(j * 2 * HEAD_SIZE, (j + 1) * 2 * HEAD_SIZE)
        key = jnp.concatenate([ref[:, at.start : at.start + HEAD_SIZE] for ref in kv_refs], axis=0)
        value = jnp.concatenate([ref[:, at.start + HEAD_SIZE : at.stop] for ref in kv_refs], axis=0)
        first = j * PORTION
        query = jnp.concatenate(
            [
                q_all[:, (first + h) * HEAD_SIZE : (first + h + 1) * HEAD_SIZE]
                for h in range(PORTION)
            ],
            axis=0,
        )
        scores = lax.dot_general(
            query, key, (((1,), (1,)), ((), ())), preferred_element_type=jnp.float32
        )
        scores = scores + jnp.concatenate([bias[...]] * PORTION, axis=0)
        top = jnp.max(scores, axis=1, keepdims=True)
        expo = jnp.exp2((scores - top) * (math.log2(math.e) / math.sqrt(HEAD_SIZE)))
        total = jnp.sum(expo, axis=1, keepdims=True)
        attn = jnp.dot(expo.astype(jnp.bfloat16), value, preferred_element_type=jnp.float32)
        attn = (attn / total).astype(jnp.bfloat16)
        attn = jnp.concatenate(
            [attn[h * row_list : (h + 1) * row_list] for h in range(PORTION)], axis=1
        )
        routed = jnp.dot(chosen[...], attn, preferred_element_type=jnp.float32).astype(jnp.bfloat16)
        for k in range(n_out):
            outs[k][:, j * wide : (j + 1) * wide] = routed[k * capacity : (k + 1) * capacity]


def attend(first, heads, swap_ids, queries, q_new, bias, chosen, kv_parts, before):
    row_list, n_all = bias.shape
    n_out = lax.axis_size("inner")
    capacity = NSWAP * row_list // n_out
    wide = PORTION * HEAD_SIZE

    def columns(rows, width):
        return pl.BlockSpec((rows, width), lambda s: (0, first // PER_STEP + s))

    def whole(array):
        return pl.BlockSpec(array.shape, lambda s: (0, 0))

    return pl.pallas_call(
        functools.partial(attend_kernel, len(kv_parts), n_out),
        grid=(heads // PER_STEP,),
        out_shape=[jax.ShapeDtypeStruct((capacity, heads * wide), jnp.bfloat16)] * n_out,
        in_specs=[
            pl.BlockSpec(memory_space=pltpu.SMEM),
            columns(row_list, PER_STEP * wide),
            columns(NSWAP * BLK, PER_STEP * wide),
            whole(bias),
            whole(chosen),
        ]
        + [columns(part.shape[0], PER_STEP * 2 * HEAD_SIZE) for part in kv_parts]
        + [pl.BlockSpec(memory_space=pl.ANY)] * len(before),
        out_specs=[pl.BlockSpec((capacity, PER_STEP * wide), lambda s: (0, s))] * n_out,
        scratch_shapes=[pltpu.VMEM((row_list, PER_STEP * wide), jnp.bfloat16)],
        compiler_params=params(16 if before else 60),
        cost_estimate=pl.CostEstimate(
            flops=heads * PORTION * row_list * n_all * HEAD_SIZE * 4,
            bytes_accessed=heads * (4 * wide * row_list * 2 + n_all * 512),
            transcendentals=heads * PORTION * row_list * n_all,
        ),
        name="attend",
    )(swap_ids, queries, q_new, bias, chosen, *kv_parts, *before)


def squares_kernel(*refs):
    n_parts = len(refs) // 2
    for ref, out in zip(refs[:n_parts], refs[n_parts:]):
        value = ref[...].astype(jnp.float32)
        out[...] = jnp.broadcast_to(jnp.sum(value * value, axis=1, keepdims=True), out.shape)


def squares(parts):
    capacity, wide = parts[0].shape
    return pl.pallas_call(
        squares_kernel,
        out_shape=[jax.ShapeDtypeStruct((capacity, LANES), jnp.float32)] * len(parts),
        compiler_params=params(16),
        cost_estimate=pl.CostEstimate(
            flops=PLACE_EARLY,
            bytes_accessed=len(parts) * capacity * wide * 2,
            transcendentals=0,
        ),
        name="squares",
    )(*parts)


def norm_kernel(me, gain, early, first, others, *refs):
    out = refs[-1]
    first, others = first[...].astype(jnp.float32), others[...].astype(jnp.float32)
    cut, width = first.shape[1], out.shape[1]
    total = early[...][:, :1] + jnp.sum(others * others, axis=1, keepdims=True)
    factor = lax.rsqrt(total / width + 1e-06)
    out[:, :cut] = (first * factor * gain[:, :cut]).astype(jnp.bfloat16)
    out[:, cut:] = (others * factor * gain[:, cut:]).astype(jnp.bfloat16)


def normalize(source, gain, early, first, others, n_inner, result):
    capacity, cut = first.shape
    width = gain.shape[0]
    steps = 2
    rows = capacity // steps
    held = [] if result is None else [result]
    return pl.pallas_call(
        norm_kernel,
        out_shape=jax.ShapeDtypeStruct((n_inner * capacity, width), jnp.bfloat16),
        grid_spec=pltpu.PrefetchScalarGridSpec(
            num_scalar_prefetch=1,
            grid=(steps,),
            in_specs=[
                pl.BlockSpec((1, width), lambda s, at: (0, 0)),
                pl.BlockSpec((rows, LANES), lambda s, at: (s, 0)),
                pl.BlockSpec((rows, cut), lambda s, at: (s, 0)),
                pl.BlockSpec((rows, width - cut), lambda s, at: (s, 0)),
            ]
            + [pl.BlockSpec(memory_space=pl.ANY)] * len(held),
            out_specs=pl.BlockSpec((rows, width), lambda s, at: (at[0] * steps + s, 0)),
        ),
        input_output_aliases={5: 0} if held else {},
        compiler_params=params(16),
        name="normalize",
    )(source.reshape(1), gain.reshape(1, width), early, first, others, *held)


def shards(queries, key_values, doc_lengths, pairing, swap_ids, dest, gain):
    n_inner = lax.axis_size("inner")
    n_outer = lax.axis_size("outer")
    me = lax.axis_index("inner")
    n_back = n_inner // 2

    kv_rest, kv_listed, q_listed = split_blocks(swap_ids, queries, key_values)
    branches = [
        functools.partial(gather_keys, mask, n_outer, n_inner, n_back)
        for mask in range(1, n_outer)
    ]
    q_new, rest, listed, bias, chosen = lax.switch(
        pairing[0] - 1, branches, doc_lengths, dest.reshape(1, -1), kv_rest, kv_listed, q_listed
    )
    kv_parts = [part for pair in zip([kv_rest] + rest, listed) for part in pair]

    arrived, first, before = [], 0, []
    for heads in HEAD_GROUPS:
        routed = attend(
            first, heads, swap_ids, queries, q_new, bias, chosen, kv_parts, before
        )
        before = [routed[0]]
        arrived.append(routed[0])
        for k in range(1, n_inner):
            arrived.append(lax.ppermute(routed[k], "inner", ring(k, n_inner)))
        first += heads
    early = squares(arrived[:n_inner])
    result = None
    for k in range(n_inner):
        source = lax.rem(me - k + n_inner, n_inner)
        result = normalize(
            source, gain, early[k], arrived[k], arrived[n_inner + k], n_inner, result
        )
    return result


def solution(mesh):
    return jax.shard_map(
        shards,
        mesh=mesh,
        in_specs=(
            P(("outer", "inner"), None),
            P(("outer", "inner"), None),
            P("outer", None),
            P(),
            P("outer", "inner", None),
            P(("outer", "inner"), None),
            P(),
        ),
        out_specs=P(("outer", "inner"), None),
        check_vma=False,
    )
```

time: 99.9 us -> 93.4 us (0.935); the launches traced: 101 us -> 93.1 us
  waiting for transfers between devices: 66.8 us -> 56.9 us
  Pallas kernels: 15.8 us -> 17.6 us
    ppermute x6, waiting for transfers between devices: 45.8 us -> 39.1 us  [shards(): arrived.append(lax.ppermute(routed[k], 'inner', ring(k, n_inner)))]
    ppermute x4, waiting for transfers between devices: 15.6 us -> 12.1 us  [back(): return lax.ppermute(value, 'inner', ring(1, n_inner))]
    pallas_call x2 -> x7, Pallas kernels: 5.06 us -> 8.33 us  [the longest x4 5.03 us: normalize(): pl.pallas_call(norm_kernel, out_shape=jax.ShapeDtypeStruct((n_inner * cap...]
    pallas_call x2, Pallas kernels: 10.7 us -> 9.26 us  [attend(): pl.pallas_call(functools.partial(attend_kernel, len(kv_parts), n_out), gr...]
  transfers between devices with their start and end apart: 12 -> 12, of which waited for: 11 -> 9; matrix products, arithmetic and copies ran while one was open for 0% -> 0% of each run, Pallas kernels for 5% -> 12%
where the time goes in v3:
time: 93.4 us; the launch traced here: 93.1 us
  waiting for transfers between devices  56.9 us (61%)
  Pallas kernels  17.6 us (19%)
  starting transfers between devices  16.9 us (18%)
    ppermute x6, waiting for transfers between devices, shards(): arrived.append(lax.ppermute(routed[k], 'inner', ring(k, n_inner)))  39.1 us
    ppermute x4, waiting for transfers between devices, back(): return lax.ppermute(value, 'inner', ring(1, n_inner))  12.1 us
    pallas_call x2, Pallas kernels, attend(): pl.pallas_call(functools.partial(attend_kernel, len(kv_parts), n_out), gr...  9.26 us
    ppermute x6, starting transfers between devices, shards(): arrived.append(lax.ppermute(routed[k], 'inner', ring(k, n_inner)))  8.55 us
    ppermute x4, starting transfers between devices, back(): return lax.ppermute(value, 'inner', ring(1, n_inner))  6.31 us
    ppermute x2, waiting for transfers between devices, swap(): return lax.ppermute(value, 'outer', [(i, i ^ mask) for i in range(n_outer)])  5.7 us
    pallas_call x4, Pallas kernels, normalize(): pl.pallas_call(norm_kernel, out_shape=jax.ShapeDtypeStruct((n_inner * cap...  5.03 us
    ppermute x2, starting transfers between devices, swap(): return lax.ppermute(value, 'outer', [(i, i ^ mask) for i in range(n_outer)])  2.09 us
  transfers between devices with their start and end apart: 12, of which 9 were waited for; matrix products, arithmetic and copies ran while one was open for 0% of the time, Pallas kernels for 12%

profile of v3, /device:TPU:8, one launch (start us, length us, event | category | flops | bytes accessed | tf_op | source)
XLA Modules:
  0.0 93.1 jit_solution(8829611778514476849)
XLA Ops:
  0.7 2.0 %split_blocks.1 = (bf16[64,2176]{1,0:T(8,128)(2,1)S(1)}, bf16[64,2048]{1,0:T(8,128)(2,1)S(1)}, bf16[64,5120]{1,0:T(8,128)(2,1)S(1)}) custom-call(s32[1,1,2]{2,1,0:T(1,128)} %ids.5, bf16[128,5120]{1,0:T(8,128)(2,1)} %q_ref.5, bf16[128,2048]{1,0:T(8,128)(2,1)} %kv_ref.1), custom_call_target="tpu_custom_call" | custom-call | tf_op jit(solution)/shard_map/split_blocks/pallas_call | solution.py:75
  2.7 27.3 %conditional.1 = (bf16[64,5120]{1,0:T(8,128)(2,1)}, bf16[64,2176]{1,0:T(8,128)(2,1)}, bf16[64,2176]{1,0:T(8,128)(2,1)}, bf16[64,2048]{1,0:T(8,128)(2,1)}, bf16[6...) conditional(s32[]{:T(128)} %bitcast.2, ...), branch_computations={%region_0.0_spmd, %region_1.0_spmd, %region_2.0_spmd, %region_3.0_... | conditional | bytes 7995696 | solution.py:324
  2.7 1.6 %collective-permute-start.9 = (bf16[64,2048]{1,0:T(8,128)(2,1)S(1)}, bf16[64,2048]{1,0:T(8,128)(2,1)}, u32[]{:S(2)}, u32[]{:S(2)}) collective-permute-start(bf16[64,2048]{1,0:T(8,128)(2,1)S(1)} %get-tuple-element.84), channel_id=1, source_target_pairs={{0,8},{4,12},{8,0},{12,4},{16,24},{20,28},{24,16},{28,20},{1,9},{5... | collective-permute-start | bytes 786440 | tf_op jit(solution)/shard_map/cond/branch_1_fun/ppermute | solution.py:100
  4.3 0.5 collective-permute-start.6
  4.8 1.6 %collective-permute-start.7 = (bf16[64,2176]{1,0:T(8,128)(2,1)S(1)}, bf16[64,2176]{1,0:T(8,128)(2,1)}, u32[]{:S(2)}, u32[]{:S(2)}) collective-permute-start(bf16[64,2176]{1,0:T(8,128)(2,1)S(1)} %get-tuple-element.83.refs_0_), channel_id=1, source_target_pairs={{0,1},{1,2},{2,3},{3,0},{4,5},{5,6},{6,7},{7,4},{8,9},{9,10},{10,1... | collective-permute-start | bytes 835592 | tf_op jit(solution)/shard_map/cond/branch_1_fun/ppermute | solution.py:95
  6.4 5.7 %collective-permute-done.9 = bf16[64,2048]{1,0:T(8,128)(2,1)} collective-permute-done((bf16[64,2048]{1,0:T(8,128)(2,1)S(1)}, bf16[64,2048]{1,0:T(8,128)(2,1)}, u32[]{:S(2)}, u32[]{:S(2)}) %collective-permute-start.9) | collective-permute-done | bytes 262176 | tf_op jit(solution)/shard_map/cond/branch_1_fun/ppermute | solution.py:100
  12.1 1.6 %collective-permute-start.10 = (bf16[64,2048]{1,0:T(8,128)(2,1)}, bf16[64,2048]{1,0:T(8,128)(2,1)}, u32[]{:S(2)}, u32[]{:S(2)}) collective-permute-start(bf16[64,2048]{1,0:T(8,128)(2,1)} %collective-permute-done.9), channel_id=1, source_target_pairs={{0,1},{1,2},{2,3},{3,0},{4,5},{5,6},{6,7},{7,4},{8,9},{9,10},{10,1... | collective-permute-start | bytes 786440 | tf_op jit(solution)/shard_map/cond/branch_1_fun/ppermute | solution.py:95
  13.7 1.6 %collective-permute-start.8 = (bf16[64,2176]{1,0:T(8,128)(2,1)}, bf16[64,2176]{1,0:T(8,128)(2,1)}, u32[]{:S(2)}, u32[]{:S(2)}) collective-permute-start(bf16[64,2176]{1,0:T(8,128)(2,1)} %collective-permute-done.7.refs_1_), channel_id=1, source_target_pairs={{0,1},{1,2},{2,3},{3,0},{4,5},{5,6},{6,7},{7,4},{8,9},{9,10},{10,1... | collective-permute-start | bytes 835592 | tf_op jit(solution)/shard_map/cond/branch_1_fun/ppermute | solution.py:95
  15.2 6.4 %collective-permute-done.10 = bf16[64,2048]{1,0:T(8,128)(2,1)} collective-permute-done((bf16[64,2048]{1,0:T(8,128)(2,1)}, bf16[64,2048]{1,0:T(8,128)(2,1)}, u32[]{:S(2)}, u32[]{:S(2)}) %collective-permute-start.10) | collective-permute-done | bytes 262176 | tf_op jit(solution)/shard_map/cond/branch_1_fun/ppermute | solution.py:95
  21.7 1.6 %collective-permute-start.11 = (bf16[64,2048]{1,0:T(8,128)(2,1)}, bf16[64,2048]{1,0:T(8,128)(2,1)}, u32[]{:S(2)}, u32[]{:S(2)}) collective-permute-start(bf16[64,2048]{1,0:T(8,128)(2,1)} %collective-permute-done.10), channel_id=1, source_target_pairs={{0,1},{1,2},{2,3},{3,0},{4,5},{5,6},{6,7},{7,4},{8,9},{9,10},{10,1... | collective-permute-start | bytes 786440 | tf_op jit(solution)/shard_map/cond/branch_1_fun/ppermute | solution.py:95
  23.2 4.0 %collective-permute-done.8.refs_2_ = bf16[64,2176]{1,0:T(8,128)(2,1)} collective-permute-done((bf16[64,2176]{1,0:T(8,128)(2,1)}, bf16[64,2176]{1,0:T(8,128)(2,1)}, u32[]{:S(2)}, u32[]{:S(2)}) %collective-permute-start.8) | collective-permute-done | bytes 278560 | tf_op jit(solution)/shard_map/cond/branch_1_fun/ppermute | solution.py:95
  27.2 1.1 %tables.8 = (f32[128,384]{1,0:T(8,128)S(1)}, bf16[256,128]{1,0:T(8,128)(2,1)S(1)}) custom-call(s32[1,8]{1,0:T(1,128)} %get-tuple-element.85.lengths, s32[1,128]{1,0:T(1,128)} %get-tuple-element.86.dest, bf16[64,2176]{1,0:T(8,128)(2,1)S(1)} %get-tuple-element.83.refs_0_, bf16[64,2176]{1,0:T(8,128)(2,1)} %collective-permute-done.7.refs_1_, ...), custom_call_target="tpu_custom_call" | custom-call | tf_op jit(solution)/shard_map/cond/branch_1_fun/tables/pallas_call | solution.py:157
  28.3 0.0 collective-permute-done.6
  28.3 1.7 %collective-permute-done.11 = bf16[64,2048]{1,0:T(8,128)(2,1)} collective-permute-done((bf16[64,2048]{1,0:T(8,128)(2,1)}, bf16[64,2048]{1,0:T(8,128)(2,1)}, u32[]{:S(2)}, u32[]{:S(2)}) %collective-permute-start.11) | collective-permute-done | bytes 262176 | tf_op jit(solution)/shard_map/cond/branch_1_fun/ppermute | solution.py:95
  30.0 3.3 %attend.2 = (bf16[64,1280]{1,0:T(8,128)(2,1)}, bf16[64,1280]{1,0:T(8,128)(2,1)}, bf16[64,1280]{1,0:T(8,128)(2,1)}, bf16[64,1280]{1,0:T(8,128)(2,1)}) custom-call(s32[1,1,2]{2,1,0:T(1,128)} %ids.5, bf16[128,5120]{1,0:T(8,128)(2,1)} %q_ref.5, bf16[64,5120]{1,0:T(8,128)(2,1)} %get-tuple-element.150.q_new, f32[128,384]{1,0:T(8,128)S(1)} %get-tuple-element.151.bias, ...), custom_call_target="tpu_custom_call" | custom-call | flops 251658240 | bytes 1703936 | tf_op jit(solution)/shard_map/attend/pallas_call | solution.py:229
  33.3 1.6 %collective-permute-start.42 = (bf16[64,1280]{1,0:T(8,128)(2,1)}, bf16[64,1280]{1,0:T(8,128)(2,1)S(1)}, u32[]{:S(2)}, u32[]{:S(2)}) collective-permute-start(bf16[64,1280]{1,0:T(8,128)(2,1)} %get-tuple-element.159), channel_id=1, source_target_pairs={{0,1},{1,2},{2,3},{3,0},{4,5},{5,6},{6,7},{7,4},{8,9},{9,10},{10,1... | collective-permute-start | bytes 491528 | tf_op jit(solution)/shard_map/ppermute | solution.py:337
  34.9 3.2 %collective-permute-start.43 = (bf16[64,1280]{1,0:T(8,128)(2,1)}, bf16[64,1280]{1,0:T(8,128)(2,1)S(1)}, u32[]{:S(2)}, u32[]{:S(2)}) collective-permute-start(bf16[64,1280]{1,0:T(8,128)(2,1)} %get-tuple-element.160), channel_id=1, source_target_pairs={{0,2},{1,3},{2,0},{3,1},{4,6},{5,7},{6,4},{7,5},{8,10},{9,11},{10,... | collective-permute-start | bytes 491528 | tf_op jit(solution)/shard_map/ppermute | solution.py:337
  38.1 0.0 copy-start.1
  38.1 0.9 copy-done.1
  39.0 5.9 %attend.3 = (bf16[64,3840]{1,0:T(8,128)(2,1)S(1)}, bf16[64,3840]{1,0:T(8,128)(2,1)}, bf16[64,3840]{1,0:T(8,128)(2,1)}, bf16[64,3840]{1,0:T(8,128)(2,1)S(1)}) custom-call(s32[1,1,2]{2,1,0:T(1,128)S(1)} %copy-done.4, bf16[128,5120]{1,0:T(8,128)(2,1)S(1)} %copy-done, bf16[64,5120]{1,0:T(8,128)(2,1)} %get-tuple-element.150.q_new, ...), custom_call_target="tpu_custom_call" | custom-call | flops 754974720 | bytes 5111808 | tf_op jit(solution)/shard_map/attend/pallas_call | solution.py:229
  45.0 2.0 %collective-permute-start.47 = (bf16[64,3840]{1,0:T(8,128)(2,1)}, bf16[64,3840]{1,0:T(8,128)(2,1)S(1)}, u32[]{:S(2)}, u32[]{:S(2)}) collective-permute-start(bf16[64,3840]{1,0:T(8,128)(2,1)} %get-tuple-element.167), channel_id=1, source_target_pairs={{0,1},{1,2},{2,3},{3,0},{4,5},{5,6},{6,7},{7,4},{8,9},{9,10},{10,1... | collective-permute-start | bytes 1474568 | tf_op jit(solution)/shard_map/ppermute | solution.py:337
  47.0 1.8 %collective-permute-start.46 = (bf16[64,3840]{1,0:T(8,128)(2,1)}, bf16[64,3840]{1,0:T(8,128)(2,1)S(1)}, u32[]{:S(2)}, u32[]{:S(2)}) collective-permute-start(bf16[64,3840]{1,0:T(8,128)(2,1)} %get-tuple-element.165), channel_id=1, source_target_pairs={{0,2},{1,3},{2,0},{3,1},{4,6},{5,7},{6,4},{7,5},{8,10},{9,11},{10,... | collective-permute-start | bytes 1474568 | tf_op jit(solution)/shard_map/ppermute | solution.py:337
  48.8 0.6 collective-permute-done.43.refs_2_.first
  49.3 22.5 %collective-permute-done.44.refs_3_.first = bf16[64,1280]{1,0:T(8,128)(2,1)S(1)} collective-permute-done((bf16[64,1280]{1,0:T(8,128)(2,1)}, bf16[64,1280]{1,0:T(8,128)(2,1)S(1)}, u32[]{:S(2)}, u32[]{:S(2)}) %collective-permute-start.44) | collective-permute-done | bytes 163872 | tf_op jit(solution)/shard_map/ppermute | solution.py:337
  71.8 0.2 squares.1
  72.0 1.3 %normalize.4.refs_0_ = bf16[256,5120]{1,0:T(8,128)(2,1)} custom-call(s32[1]{0:T(128)} %bitcast.6.me, f32[1,5120]{1,0:T(1,128)S(1)} %bitcast.8, f32[64,128]{1,0:T(8,128)S(1)} %get-tuple-element.168.early, bf16[64,1280]{1,0:T(8,128)(2,1)S(1)} %copy-done.2, bf16[64,3840]{1,0:T(8,128)(2,1)S(1)} %get-tuple-element.169.others), custom_call_target="tpu_custom_call" | custom-call | tf_op jit(solution)/shard_map/normalize/pallas_call | solution.py:292
  73.3 7.6 %collective-permute-done.47.others = bf16[64,3840]{1,0:T(8,128)(2,1)S(1)} collective-permute-done((bf16[64,3840]{1,0:T(8,128)(2,1)}, bf16[64,3840]{1,0:T(8,128)(2,1)S(1)}, u32[]{:S(2)}, u32[]{:S(2)}) %collective-permute-start.47) | collective-permute-done | bytes 491552 | tf_op jit(solution)/shard_map/ppermute | solution.py:337
  80.9 1.3 %normalize.5.refs_0_ = bf16[256,5120]{1,0:T(8,128)(2,1)} custom-call(s32[1]{0:T(128)} %bitcast.5.me, f32[1,5120]{1,0:T(1,128)S(1)} %bitcast.9, f32[64,128]{1,0:T(8,128)S(1)} %get-tuple-element.166.early, bf16[64,1280]{1,0:T(8,128)(2,1)S(1)} %collective-permute-done.42.refs_1_.first, ...), custom_call_target="tpu_custom_call", output_to_operand_aliasing={{}: (5, {})} | custom-call | tf_op jit(solution)/shard_map/normalize/pallas_call | solution.py:292
  82.2 7.5 %collective-permute-done.46.others = bf16[64,3840]{1,0:T(8,128)(2,1)S(1)} collective-permute-done((bf16[64,3840]{1,0:T(8,128)(2,1)}, bf16[64,3840]{1,0:T(8,128)(2,1)S(1)}, u32[]{:S(2)}, u32[]{:S(2)}) %collective-permute-start.46) | collective-permute-done | bytes 491552 | tf_op jit(solution)/shard_map/ppermute | solution.py:337
  89.7 1.3 %normalize.6.refs_0_ = bf16[256,5120]{1,0:T(8,128)(2,1)} custom-call(s32[1]{0:T(128)} %bitcast.4.me, f32[1,5120]{1,0:T(1,128)S(1)} %bitcast.10, f32[64,128]{1,0:T(8,128)S(1)} %get-tuple-element.164.early, bf16[64,1280]{1,0:T(8,128)(2,1)S(1)} %collective-permute-done.43.refs_2_.first, ...), custom_call_target="tpu_custom_call", output_to_operand_aliasing={{}: (5, {})} | custom-call | tf_op jit(solution)/shard_map/normalize/pallas_call | solution.py:292
  90.9 0.9 collective-permute-done.45.others
  91.9 1.3 %normalize.7 = bf16[256,5120]{1,0:T(8,128)(2,1)} custom-call(s32[1]{0:T(128)} %bitcast.me, f32[1,5120]{1,0:T(1,128)S(1)} %bitcast.11, f32[64,128]{1,0:T(8,128)S(1)} %get-tuple-element.162.early, bf16[64,1280]{1,0:T(8,128)(2,1)S(1)} %collective-permute-done.44.refs_3_.first, ...), custom_call_target="tpu_custom_call", output_to_operand_aliasing={{}: (5, {})} | custom-call | tf_op jit(solution)/shard_map/normalize/pallas_call | solution.py:292
  (12 shorter events, 0.0 us)
Async XLA Ops:
  2.7 9.4 %collective-permute-start.9 = (bf16[64,2048]{1,0:T(8,128)(2,1)S(1)}, bf16[64,2048]{1,0:T(8,128)(2,1)}, u32[]{:S(2)}, u32[]{:S(2)}) collective-permute-start(bf16[64,2048]{1,0:T(8,128)(2,1)S(1)} %get-tuple-element.84), channel_id=1, source_target_pairs={{0,8},{4,12},{8,0},{12,4},{16,24},{20,28},{24,16},{28,20},{1,9},{5... | collective-permute-start | bytes 786440 | tf_op jit(solution)/shard_map/cond/branch_1_fun/ppermute | solution.py:100
  4.3 24.0 %collective-permute-start.6 = (bf16[64,5120]{1,0:T(8,128)(2,1)S(1)}, bf16[64,5120]{1,0:T(8,128)(2,1)}, u32[]{:S(2)}, u32[]{:S(2)}) collective-permute-start(bf16[64,5120]{1,0:T(8,128)(2,1)S(1)} %get-tuple-element.82), channel_id=1, source_target_pairs={{0,8},{4,12},{8,0},{12,4},{16,24},{20,28},{24,16},{28,20},{1,9},{5... | collective-permute-start | bytes 1966088 | tf_op jit(solution)/shard_map/cond/branch_1_fun/ppermute | solution.py:100
  4.8 8.9 %collective-permute-start.7 = (bf16[64,2176]{1,0:T(8,128)(2,1)S(1)}, bf16[64,2176]{1,0:T(8,128)(2,1)}, u32[]{:S(2)}, u32[]{:S(2)}) collective-permute-start(bf16[64,2176]{1,0:T(8,128)(2,1)S(1)} %get-tuple-element.83.refs_0_), channel_id=1, source_target_pairs={{0,1},{1,2},{2,3},{3,0},{4,5},{5,6},{6,7},{7,4},{8,9},{9,10},{10,1... | collective-permute-start | bytes 835592 | tf_op jit(solution)/shard_map/cond/branch_1_fun/ppermute | solution.py:95
  12.1 9.6 %collective-permute-start.10 = (bf16[64,2048]{1,0:T(8,128)(2,1)}, bf16[64,2048]{1,0:T(8,128)(2,1)}, u32[]{:S(2)}, u32[]{:S(2)}) collective-permute-start(bf16[64,2048]{1,0:T(8,128)(2,1)} %collective-permute-done.9), channel_id=1, source_target_pairs={{0,1},{1,2},{2,3},{3,0},{4,5},{5,6},{6,7},{7,4},{8,9},{9,10},{10,1... | collective-permute-start | bytes 786440 | tf_op jit(solution)/shard_map/cond/branch_1_fun/ppermute | solution.py:95
  13.7 13.5 %collective-permute-start.8 = (bf16[64,2176]{1,0:T(8,128)(2,1)}, bf16[64,2176]{1,0:T(8,128)(2,1)}, u32[]{:S(2)}, u32[]{:S(2)}) collective-permute-start(bf16[64,2176]{1,0:T(8,128)(2,1)} %collective-permute-done.7.refs_1_), channel_id=1, source_target_pairs={{0,1},{1,2},{2,3},{3,0},{4,5},{5,6},{6,7},{7,4},{8,9},{9,10},{10,1... | collective-permute-start | bytes 835592 | tf_op jit(solution)/shard_map/cond/branch_1_fun/ppermute | solution.py:95
  21.7 8.4 %collective-permute-start.11 = (bf16[64,2048]{1,0:T(8,128)(2,1)}, bf16[64,2048]{1,0:T(8,128)(2,1)}, u32[]{:S(2)}, u32[]{:S(2)}) collective-permute-start(bf16[64,2048]{1,0:T(8,128)(2,1)} %collective-permute-done.10), channel_id=1, source_target_pairs={{0,1},{1,2},{2,3},{3,0},{4,5},{5,6},{6,7},{7,4},{8,9},{9,10},{10,1... | collective-permute-start | bytes 786440 | tf_op jit(solution)/shard_map/cond/branch_1_fun/ppermute | solution.py:95
  30.0 8.1 %copy-start = (bf16[128,5120]{1,0:T(8,128)(2,1)S(1)}, bf16[128,5120]{1,0:T(8,128)(2,1)}, u32[]{:S(2)}) copy-start(bf16[128,5120]{1,0:T(8,128)(2,1)} %q_ref.5) | copy-start | bytes 3932164
  30.0 8.1 %copy-start.4 = (s32[1,1,2]{2,1,0:T(1,128)S(1)}, s32[1,1,2]{2,1,0:T(1,128)}, u32[]{:S(2)}) copy-start(s32[1,1,2]{2,1,0:T(1,128)} %ids.5) | copy-start | bytes 28
  33.3 15.4 %collective-permute-start.42 = (bf16[64,1280]{1,0:T(8,128)(2,1)}, bf16[64,1280]{1,0:T(8,128)(2,1)S(1)}, u32[]{:S(2)}, u32[]{:S(2)}) collective-permute-start(bf16[64,1280]{1,0:T(8,128)(2,1)} %get-tuple-element.159), channel_id=1, source_target_pairs={{0,1},{1,2},{2,3},{3,0},{4,5},{5,6},{6,7},{7,4},{8,9},{9,10},{10,1... | collective-permute-start | bytes 491528 | tf_op jit(solution)/shard_map/ppermute | solution.py:337
  34.9 14.4 %collective-permute-start.43 = (bf16[64,1280]{1,0:T(8,128)(2,1)}, bf16[64,1280]{1,0:T(8,128)(2,1)S(1)}, u32[]{:S(2)}, u32[]{:S(2)}) collective-permute-start(bf16[64,1280]{1,0:T(8,128)(2,1)} %get-tuple-element.160), channel_id=1, source_target_pairs={{0,2},{1,3},{2,0},{3,1},{4,6},{5,7},{6,4},{7,5},{8,10},{9,11},{10,... | collective-permute-start | bytes 491528 | tf_op jit(solution)/shard_map/ppermute | solution.py:337
  38.1 33.7 %collective-permute-start.44 = (bf16[64,1280]{1,0:T(8,128)(2,1)}, bf16[64,1280]{1,0:T(8,128)(2,1)S(1)}, u32[]{:S(2)}, u32[]{:S(2)}) collective-permute-start(bf16[64,1280]{1,0:T(8,128)(2,1)} %get-tuple-element.161), channel_id=1, source_target_pairs={{0,3},{1,0},{2,1},{3,2},{4,7},{5,4},{6,5},{7,6},{8,11},{9,8},{10,9... | collective-permute-start | bytes 491528 | tf_op jit(solution)/shard_map/ppermute | solution.py:337
  38.1 0.9 copy-start.1
  39.0 32.8 %copy-start.2 = (bf16[64,1280]{1,0:T(8,128)(2,1)S(1)}, bf16[64,1280]{1,0:T(8,128)(2,1)}, u32[]{:S(2)}) copy-start(bf16[64,1280]{1,0:T(8,128)(2,1)} %get-tuple-element.158.refs_0_.refs_6_.first) | copy-start | bytes 491524
  45.0 36.0 %collective-permute-start.47 = (bf16[64,3840]{1,0:T(8,128)(2,1)}, bf16[64,3840]{1,0:T(8,128)(2,1)S(1)}, u32[]{:S(2)}, u32[]{:S(2)}) collective-permute-start(bf16[64,3840]{1,0:T(8,128)(2,1)} %get-tuple-element.167), channel_id=1, source_target_pairs={{0,1},{1,2},{2,3},{3,0},{4,5},{5,6},{6,7},{7,4},{8,9},{9,10},{10,1... | collective-permute-start | bytes 1474568 | tf_op jit(solution)/shard_map/ppermute | solution.py:337
  47.0 42.7 %collective-permute-start.46 = (bf16[64,3840]{1,0:T(8,128)(2,1)}, bf16[64,3840]{1,0:T(8,128)(2,1)S(1)}, u32[]{:S(2)}, u32[]{:S(2)}) collective-permute-start(bf16[64,3840]{1,0:T(8,128)(2,1)} %get-tuple-element.165), channel_id=1, source_target_pairs={{0,2},{1,3},{2,0},{3,1},{4,6},{5,7},{6,4},{7,5},{8,10},{9,11},{10,... | collective-permute-start | bytes 1474568 | tf_op jit(solution)/shard_map/ppermute | solution.py:337
  48.8 23.3 %copy-start.3 = (f32[5120]{0:T(1024)S(1)}, f32[5120]{0:T(1024)}, u32[]{:S(2)}) copy-start(f32[5120]{0:T(1024)} %param.20) | copy-start | bytes 61444
  48.8 43.1 %collective-permute-start.45 = (bf16[64,3840]{1,0:T(8,128)(2,1)S(1)}, bf16[64,3840]{1,0:T(8,128)(2,1)S(1)}, u32[]{:S(2)}, u32[]{:S(2)}) collective-permute-start(bf16[64,3840]{1,0:T(8,128)(2,1)S(1)} %get-tuple-element.163), channel_id=1, source_target_pairs={{0,3},{1,0},{2,1},{3,2},{4,7},{5,4},{6,5},{7,6},{8,11},{9,8},{10,9... | collective-permute-start | bytes 1474568 | tf_op jit(solution)/shard_map/ppermute | solution.py:337

commit v4 on v3

--- a/solution.py
+++ b/solution.py
@@ -91,18 +91,24 @@
     )
 
 
-def back(value, n_inner):
-    return lax.ppermute(value, "inner", ring(1, n_inner))
+def back(value, n_inner, step):
+    pairs = ring(1, n_inner) if step == 1 else [(i, i + 1) for i in range(step - 1, n_inner - 1)]
+    return lax.ppermute(value, "inner", pairs)
 
 
 def gather_keys(mask, n_outer, n_inner, n_back, doc_lengths, dest, kv_rest, kv_listed, q_listed):
+    def cross(value, bits):
+        return lax.ppermute(value, "outer", [(i, i ^ bits) for i in range(n_outer)])
+
     def swap(value):
-        return lax.ppermute(value, "outer", [(i, i ^ mask) for i in range(n_outer)])
+        if mask & 1 and mask > 1:
+            return cross(cross(value, 1), mask - 1)
+        return cross(value, mask)
 
     def reach_back(value):
         parts = [value]
         for _ in range(n_back):
-            parts.append(back(parts[-1], n_inner))
+            parts.append(back(parts[-1], n_inner, len(parts)))
         return parts
 
     rest = reach_back(kv_rest)

time: 93.4 us -> 94.5 us (1.012); the launches traced: 93.1 us -> 92.7 us
  waiting for transfers between devices: 56.9 us -> 51.2 us
  starting transfers between devices: 16.9 us -> 22.2 us
    ppermute x6, waiting for transfers between devices: 17.8 us -> 11.6 us  [the longest x4 11.6 us: back(): return lax.ppermute(value, 'inner', pairs)]
    ppermute x6, starting transfers between devices: 8.4 us -> 13 us  [the longest x4 12.4 us: back(): return lax.ppermute(value, 'inner', pairs)]
where the time goes in v4:
time: 94.5 us; the launch traced here: 92.7 us
  waiting for transfers between devices  51.2 us (54%)
  starting transfers between devices  22.2 us (23%)
  Pallas kernels  17.6 us (19%)
    ppermute x6, waiting for transfers between devices, shards(): arrived.append(lax.ppermute(routed[k], 'inner', ring(k, n_inner)))  39.7 us
    ppermute x4, starting transfers between devices, back(): return lax.ppermute(value, 'inner', pairs)  12.4 us
    ppermute x4, waiting for transfers between devices, back(): return lax.ppermute(value, 'inner', pairs)  11.6 us
    pallas_call x2, Pallas kernels, attend(): pl.pallas_call(functools.partial(attend_kernel, len(kv_parts), n_out), gr...  9.27 us
    ppermute x6, starting transfers between devices, shards(): arrived.append(lax.ppermute(routed[k], 'inner', ring(k, n_inner)))  9.22 us
    pallas_call x4, Pallas kernels, normalize(): pl.pallas_call(norm_kernel, out_shape=jax.ShapeDtypeStruct((n_inner * cap...  5.03 us
    pallas_call x1, Pallas kernels, split_blocks(): pl.pallas_call(split_kernel, out_shape=(pltpu.VMEM((row_list - some, kv_w...  2.03 us
  transfers between devices with their start and end apart: 12, of which 9 were waited for; matrix products, arithmetic and copies ran while one was open for 0% of the time, Pallas kernels for 12%

profile of v4, /device:TPU:8, one launch (start us, length us, event | category | flops | bytes accessed | tf_op | source)
XLA Modules:
  0.0 92.7 jit_solution(17690813584335900330)
XLA Ops:
  0.7 2.0 %split_blocks.1 = (bf16[64,2176]{1,0:T(8,128)(2,1)S(1)}, bf16[64,2048]{1,0:T(8,128)(2,1)S(1)}, bf16[64,5120]{1,0:T(8,128)(2,1)S(1)}) custom-call(s32[1,1,2]{2,1,0:T(1,128)} %ids.5, bf16[128,5120]{1,0:T(8,128)(2,1)} %q_ref.5, bf16[128,2048]{1,0:T(8,128)(2,1)} %kv_ref.1), custom_call_target="tpu_custom_call" | custom-call | tf_op jit(solution)/shard_map/split_blocks/pallas_call | solution.py:75
  2.7 25.6 %conditional.1 = (bf16[64,5120]{1,0:T(8,128)(2,1)}, bf16[64,2176]{1,0:T(8,128)(2,1)}, bf16[64,2176]{1,0:T(8,128)(2,1)}, bf16[64,2048]{1,0:T(8,128)(2,1)}, bf16[6...) conditional(s32[]{:T(128)} %bitcast.2, ...), branch_computations={%region_0.0_spmd, %region_1.0_spmd, %region_2.0_spmd, %region_3.0_... | conditional | bytes 11665792 | solution.py:330
  2.7 0.1 collective-permute-start.3
  2.8 0.5 collective-permute-start
  3.3 1.6 %collective-permute-start.1 = (bf16[64,2176]{1,0:T(8,128)(2,1)S(1)}, bf16[64,2176]{1,0:T(8,128)(2,1)}, u32[]{:S(2)}, u32[]{:S(2)}) collective-permute-start(bf16[64,2176]{1,0:T(8,128)(2,1)S(1)} %get-tuple-element.76.refs_0_), channel_id=1, source_target_pairs={{0,1},{1,2},{2,3},{3,0},{4,5},{5,6},{6,7},{7,4},{8,9},{9,10},{10,1... | collective-permute-start | bytes 835592 | tf_op jit(solution)/shard_map/cond/branch_0_fun/ppermute | solution.py:96
  4.9 0.0 collective-permute-done.3
  4.9 1.6 %collective-permute-start.4 = (bf16[64,2048]{1,0:T(8,128)(2,1)}, bf16[64,2048]{1,0:T(8,128)(2,1)}, u32[]{:S(2)}, u32[]{:S(2)}) collective-permute-start(bf16[64,2048]{1,0:T(8,128)(2,1)} %collective-permute-done.3), channel_id=1, source_target_pairs={{0,1},{1,2},{2,3},{3,0},{4,5},{5,6},{6,7},{7,4},{8,9},{9,10},{10,1... | collective-permute-start | bytes 786440 | tf_op jit(solution)/shard_map/cond/branch_0_fun/ppermute | solution.py:96
  6.5 6.5 %collective-permute-done.1.refs_1_ = bf16[64,2176]{1,0:T(8,128)(2,1)} collective-permute-done((bf16[64,2176]{1,0:T(8,128)(2,1)S(1)}, bf16[64,2176]{1,0:T(8,128)(2,1)}, u32[]{:S(2)}, u32[]{:S(2)}) %collective-permute-start.1) | collective-permute-done | bytes 278560 | tf_op jit(solution)/shard_map/cond/branch_0_fun/ppermute | solution.py:96
  12.9 4.2 %collective-permute-start.2 = (bf16[64,2176]{1,0:T(8,128)(2,1)}, bf16[64,2176]{1,0:T(8,128)(2,1)}, u32[]{:S(2)}, u32[]{:S(2)}) collective-permute-start(bf16[64,2176]{1,0:T(8,128)(2,1)} %collective-permute-done.1.refs_1_), channel_id=1, source_target_pairs={{1,2},{2,3},{5,6},{6,7},{9,10},{10,11},{13,14},{14,15},{17,18},{18... | collective-permute-start | bytes 835592 | tf_op jit(solution)/shard_map/cond/branch_0_fun/ppermute | solution.py:96
  17.1 0.6 collective-permute-done.4
  17.7 5.1 %collective-permute-start.5 = (bf16[64,2048]{1,0:T(8,128)(2,1)}, bf16[64,2048]{1,0:T(8,128)(2,1)}, u32[]{:S(2)}, u32[]{:S(2)}) collective-permute-start(bf16[64,2048]{1,0:T(8,128)(2,1)} %collective-permute-done.4), channel_id=1, source_target_pairs={{1,2},{2,3},{5,6},{6,7},{9,10},{10,11},{13,14},{14,15},{17,18},{18... | collective-permute-start | bytes 786440 | tf_op jit(solution)/shard_map/cond/branch_0_fun/ppermute | solution.py:96
  22.7 1.1 %collective-permute-done.2.refs_2_ = bf16[64,2176]{1,0:T(8,128)(2,1)} collective-permute-done((bf16[64,2176]{1,0:T(8,128)(2,1)}, bf16[64,2176]{1,0:T(8,128)(2,1)}, u32[]{:S(2)}, u32[]{:S(2)}) %collective-permute-start.2) | collective-permute-done | bytes 278560 | tf_op jit(solution)/shard_map/cond/branch_0_fun/ppermute | solution.py:96
  23.8 1.1 %tables.7 = (f32[128,384]{1,0:T(8,128)S(1)}, bf16[256,128]{1,0:T(8,128)(2,1)S(1)}) custom-call(s32[1,8]{1,0:T(1,128)} %get-tuple-element.78.lengths, s32[1,128]{1,0:T(1,128)} %get-tuple-element.79.dest, bf16[64,2176]{1,0:T(8,128)(2,1)S(1)} %get-tuple-element.76.refs_0_, bf16[64,2176]{1,0:T(8,128)(2,1)} %collective-permute-done.1.refs_1_, ...), custom_call_target="tpu_custom_call" | custom-call | tf_op jit(solution)/shard_map/cond/branch_0_fun/tables/pallas_call | solution.py:163
  24.9 3.5 %collective-permute-done.5 = bf16[64,2048]{1,0:T(8,128)(2,1)} collective-permute-done((bf16[64,2048]{1,0:T(8,128)(2,1)}, bf16[64,2048]{1,0:T(8,128)(2,1)}, u32[]{:S(2)}, u32[]{:S(2)}) %collective-permute-start.5) | collective-permute-done | bytes 262176 | tf_op jit(solution)/shard_map/cond/branch_0_fun/ppermute | solution.py:96
  28.3 3.3 %attend.2 = (bf16[64,1280]{1,0:T(8,128)(2,1)}, bf16[64,1280]{1,0:T(8,128)(2,1)}, bf16[64,1280]{1,0:T(8,128)(2,1)}, bf16[64,1280]{1,0:T(8,128)(2,1)}) custom-call(s32[1,1,2]{2,1,0:T(1,128)} %ids.5, bf16[128,5120]{1,0:T(8,128)(2,1)} %q_ref.5, bf16[64,5120]{1,0:T(8,128)(2,1)} %get-tuple-element.150.q_new, f32[128,384]{1,0:T(8,128)S(1)} %get-tuple-element.151.bias, ...), custom_call_target="tpu_custom_call" | custom-call | flops 251658240 | bytes 1703936 | tf_op jit(solution)/shard_map/attend/pallas_call | solution.py:235
  31.7 2.5 %collective-permute-start.48 = (bf16[64,1280]{1,0:T(8,128)(2,1)}, bf16[64,1280]{1,0:T(8,128)(2,1)S(1)}, u32[]{:S(2)}, u32[]{:S(2)}) collective-permute-start(bf16[64,1280]{1,0:T(8,128)(2,1)} %get-tuple-element.159), channel_id=1, source_target_pairs={{0,1},{1,2},{2,3},{3,0},{4,5},{5,6},{6,7},{7,4},{8,9},{9,10},{10,1... | collective-permute-start | bytes 491528 | tf_op jit(solution)/shard_map/ppermute | solution.py:343
  34.1 1.0 %collective-permute-start.49 = (bf16[64,1280]{1,0:T(8,128)(2,1)}, bf16[64,1280]{1,0:T(8,128)(2,1)S(1)}, u32[]{:S(2)}, u32[]{:S(2)}) collective-permute-start(bf16[64,1280]{1,0:T(8,128)(2,1)} %get-tuple-element.160), channel_id=1, source_target_pairs={{0,2},{1,3},{2,0},{3,1},{4,6},{5,7},{6,4},{7,5},{8,10},{9,11},{10,... | collective-permute-start | bytes 491528 | tf_op jit(solution)/shard_map/ppermute | solution.py:343
  35.2 2.0 %collective-permute-start.50 = (bf16[64,1280]{1,0:T(8,128)(2,1)}, bf16[64,1280]{1,0:T(8,128)(2,1)S(1)}, u32[]{:S(2)}, u32[]{:S(2)}) collective-permute-start(bf16[64,1280]{1,0:T(8,128)(2,1)} %get-tuple-element.161), channel_id=1, source_target_pairs={{0,3},{1,0},{2,1},{3,2},{4,7},{5,4},{6,5},{7,6},{8,11},{9,8},{10,9... | collective-permute-start | bytes 491528 | tf_op jit(solution)/shard_map/ppermute | solution.py:343
  37.2 0.9 copy-done.1
  38.1 6.0 %attend.3 = (bf16[64,3840]{1,0:T(8,128)(2,1)S(1)}, bf16[64,3840]{1,0:T(8,128)(2,1)}, bf16[64,3840]{1,0:T(8,128)(2,1)}, bf16[64,3840]{1,0:T(8,128)(2,1)S(1)}) custom-call(s32[1,1,2]{2,1,0:T(1,128)S(1)} %copy-done.4, bf16[128,5120]{1,0:T(8,128)(2,1)S(1)} %copy-done, bf16[64,5120]{1,0:T(8,128)(2,1)} %get-tuple-element.150.q_new, ...), custom_call_target="tpu_custom_call" | custom-call | flops 754974720 | bytes 5111808 | tf_op jit(solution)/shard_map/attend/pallas_call | solution.py:235
  44.1 0.0 collective-permute-start.53
  44.1 3.7 %collective-permute-start.52 = (bf16[64,3840]{1,0:T(8,128)(2,1)}, bf16[64,3840]{1,0:T(8,128)(2,1)S(1)}, u32[]{:S(2)}, u32[]{:S(2)}) collective-permute-start(bf16[64,3840]{1,0:T(8,128)(2,1)} %get-tuple-element.165), channel_id=1, source_target_pairs={{0,2},{1,3},{2,0},{3,1},{4,6},{5,7},{6,4},{7,5},{8,10},{9,11},{10,... | collective-permute-start | bytes 1474568 | tf_op jit(solution)/shard_map/ppermute | solution.py:343
  47.8 1.9 %collective-permute-done.49.refs_2_.first = bf16[64,1280]{1,0:T(8,128)(2,1)S(1)} collective-permute-done((bf16[64,1280]{1,0:T(8,128)(2,1)}, bf16[64,1280]{1,0:T(8,128)(2,1)S(1)}, u32[]{:S(2)}, u32[]{:S(2)}) %collective-permute-start.49) | collective-permute-done | bytes 163872 | tf_op jit(solution)/shard_map/ppermute | solution.py:343
  49.7 20.6 %collective-permute-done.50.refs_3_.first = bf16[64,1280]{1,0:T(8,128)(2,1)S(1)} collective-permute-done((bf16[64,1280]{1,0:T(8,128)(2,1)}, bf16[64,1280]{1,0:T(8,128)(2,1)S(1)}, u32[]{:S(2)}, u32[]{:S(2)}) %collective-permute-start.50) | collective-permute-done | bytes 163872 | tf_op jit(solution)/shard_map/ppermute | solution.py:343
  70.3 0.2 squares.1
  70.5 1.3 %normalize.4.refs_0_ = bf16[256,5120]{1,0:T(8,128)(2,1)} custom-call(s32[1]{0:T(128)} %bitcast.6.me, f32[1,5120]{1,0:T(1,128)S(1)} %bitcast.8, f32[64,128]{1,0:T(8,128)S(1)} %get-tuple-element.168.early, bf16[64,1280]{1,0:T(8,128)(2,1)S(1)} %copy-done.2, bf16[64,3840]{1,0:T(8,128)(2,1)S(1)} %get-tuple-element.169.others), custom_call_target="tpu_custom_call" | custom-call | tf_op jit(solution)/shard_map/normalize/pallas_call | solution.py:298
  71.7 9.5 %collective-permute-done.53.others = bf16[64,3840]{1,0:T(8,128)(2,1)S(1)} collective-permute-done((bf16[64,3840]{1,0:T(8,128)(2,1)}, bf16[64,3840]{1,0:T(8,128)(2,1)S(1)}, u32[]{:S(2)}, u32[]{:S(2)}) %collective-permute-start.53) | collective-permute-done | bytes 491552 | tf_op jit(solution)/shard_map/ppermute | solution.py:343
  81.3 1.3 %normalize.5.refs_0_ = bf16[256,5120]{1,0:T(8,128)(2,1)} custom-call(s32[1]{0:T(128)} %bitcast.5.me, f32[1,5120]{1,0:T(1,128)S(1)} %bitcast.9, f32[64,128]{1,0:T(8,128)S(1)} %get-tuple-element.166.early, bf16[64,1280]{1,0:T(8,128)(2,1)S(1)} %collective-permute-done.48.refs_1_.first, ...), custom_call_target="tpu_custom_call", output_to_operand_aliasing={{}: (5, {})} | custom-call | tf_op jit(solution)/shard_map/normalize/pallas_call | solution.py:298
  82.5 7.3 %collective-permute-done.52.others = bf16[64,3840]{1,0:T(8,128)(2,1)S(1)} collective-permute-done((bf16[64,3840]{1,0:T(8,128)(2,1)}, bf16[64,3840]{1,0:T(8,128)(2,1)S(1)}, u32[]{:S(2)}, u32[]{:S(2)}) %collective-permute-start.52) | collective-permute-done | bytes 491552 | tf_op jit(solution)/shard_map/ppermute | solution.py:343
  89.8 1.3 %normalize.6.refs_0_ = bf16[256,5120]{1,0:T(8,128)(2,1)} custom-call(s32[1]{0:T(128)} %bitcast.4.me, f32[1,5120]{1,0:T(1,128)S(1)} %bitcast.10, f32[64,128]{1,0:T(8,128)S(1)} %get-tuple-element.164.early, bf16[64,1280]{1,0:T(8,128)(2,1)S(1)} %collective-permute-done.49.refs_2_.first, ...), custom_call_target="tpu_custom_call", output_to_operand_aliasing={{}: (5, {})} | custom-call | tf_op jit(solution)/shard_map/normalize/pallas_call | solution.py:298
  91.0 0.4 collective-permute-done.51.others
  91.4 1.3 %normalize.7 = bf16[256,5120]{1,0:T(8,128)(2,1)} custom-call(s32[1]{0:T(128)} %bitcast.me, f32[1,5120]{1,0:T(1,128)S(1)} %bitcast.11, f32[64,128]{1,0:T(8,128)S(1)} %get-tuple-element.162.early, bf16[64,1280]{1,0:T(8,128)(2,1)S(1)} %collective-permute-done.50.refs_3_.first, ...), custom_call_target="tpu_custom_call", output_to_operand_aliasing={{}: (5, {})} | custom-call | tf_op jit(solution)/shard_map/normalize/pallas_call | solution.py:298
  (12 shorter events, 0.0 us)
Async XLA Ops:
  2.7 2.2 %collective-permute-start.3 = (bf16[64,2048]{1,0:T(8,128)(2,1)S(1)}, bf16[64,2048]{1,0:T(8,128)(2,1)}, u32[]{:S(2)}, u32[]{:S(2)}) collective-permute-start(bf16[64,2048]{1,0:T(8,128)(2,1)S(1)} %get-tuple-element.77), channel_id=1, source_target_pairs={{0,4},{4,0},{8,12},{12,8},{16,20},{20,16},{24,28},{28,24},{1,5},{5... | collective-permute-start | bytes 786440 | tf_op jit(solution)/shard_map/cond/branch_0_fun/ppermute | solution.py:101
  2.8 22.1 %collective-permute-start = (bf16[64,5120]{1,0:T(8,128)(2,1)S(1)}, bf16[64,5120]{1,0:T(8,128)(2,1)}, u32[]{:S(2)}, u32[]{:S(2)}) collective-permute-start(bf16[64,5120]{1,0:T(8,128)(2,1)S(1)} %get-tuple-element.75), channel_id=1, source_target_pairs={{0,4},{4,0},{8,12},{12,8},{16,20},{20,16},{24,28},{28,24},{1,5},{5... | collective-permute-start | bytes 1966088 | tf_op jit(solution)/shard_map/cond/branch_0_fun/ppermute | solution.py:101
  3.3 9.6 %collective-permute-start.1 = (bf16[64,2176]{1,0:T(8,128)(2,1)S(1)}, bf16[64,2176]{1,0:T(8,128)(2,1)}, u32[]{:S(2)}, u32[]{:S(2)}) collective-permute-start(bf16[64,2176]{1,0:T(8,128)(2,1)S(1)} %get-tuple-element.76.refs_0_), channel_id=1, source_target_pairs={{0,1},{1,2},{2,3},{3,0},{4,5},{5,6},{6,7},{7,4},{8,9},{9,10},{10,1... | collective-permute-start | bytes 835592 | tf_op jit(solution)/shard_map/cond/branch_0_fun/ppermute | solution.py:96
  4.9 12.8 %collective-permute-start.4 = (bf16[64,2048]{1,0:T(8,128)(2,1)}, bf16[64,2048]{1,0:T(8,128)(2,1)}, u32[]{:S(2)}, u32[]{:S(2)}) collective-permute-start(bf16[64,2048]{1,0:T(8,128)(2,1)} %collective-permute-done.3), channel_id=1, source_target_pairs={{0,1},{1,2},{2,3},{3,0},{4,5},{5,6},{6,7},{7,4},{8,9},{9,10},{10,1... | collective-permute-start | bytes 786440 | tf_op jit(solution)/shard_map/cond/branch_0_fun/ppermute | solution.py:96
  12.9 10.9 %collective-permute-start.2 = (bf16[64,2176]{1,0:T(8,128)(2,1)}, bf16[64,2176]{1,0:T(8,128)(2,1)}, u32[]{:S(2)}, u32[]{:S(2)}) collective-permute-start(bf16[64,2176]{1,0:T(8,128)(2,1)} %collective-permute-done.1.refs_1_), channel_id=1, source_target_pairs={{1,2},{2,3},{5,6},{6,7},{9,10},{10,11},{13,14},{14,15},{17,18},{18... | collective-permute-start | bytes 835592 | tf_op jit(solution)/shard_map/cond/branch_0_fun/ppermute | solution.py:96
  17.7 10.7 %collective-permute-start.5 = (bf16[64,2048]{1,0:T(8,128)(2,1)}, bf16[64,2048]{1,0:T(8,128)(2,1)}, u32[]{:S(2)}, u32[]{:S(2)}) collective-permute-start(bf16[64,2048]{1,0:T(8,128)(2,1)} %collective-permute-done.4), channel_id=1, source_target_pairs={{1,2},{2,3},{5,6},{6,7},{9,10},{10,11},{13,14},{14,15},{17,18},{18... | collective-permute-start | bytes 786440 | tf_op jit(solution)/shard_map/cond/branch_0_fun/ppermute | solution.py:96
  28.3 8.8 %copy-start = (bf16[128,5120]{1,0:T(8,128)(2,1)S(1)}, bf16[128,5120]{1,0:T(8,128)(2,1)}, u32[]{:S(2)}) copy-start(bf16[128,5120]{1,0:T(8,128)(2,1)} %q_ref.5) | copy-start | bytes 3932164
  28.3 8.8 %copy-start.4 = (s32[1,1,2]{2,1,0:T(1,128)S(1)}, s32[1,1,2]{2,1,0:T(1,128)}, u32[]{:S(2)}) copy-start(s32[1,1,2]{2,1,0:T(1,128)} %ids.5) | copy-start | bytes 28
  31.7 16.1 %collective-permute-start.48 = (bf16[64,1280]{1,0:T(8,128)(2,1)}, bf16[64,1280]{1,0:T(8,128)(2,1)S(1)}, u32[]{:S(2)}, u32[]{:S(2)}) collective-permute-start(bf16[64,1280]{1,0:T(8,128)(2,1)} %get-tuple-element.159), channel_id=1, source_target_pairs={{0,1},{1,2},{2,3},{3,0},{4,5},{5,6},{6,7},{7,4},{8,9},{9,10},{10,1... | collective-permute-start | bytes 491528 | tf_op jit(solution)/shard_map/ppermute | solution.py:343
  34.1 15.5 %collective-permute-start.49 = (bf16[64,1280]{1,0:T(8,128)(2,1)}, bf16[64,1280]{1,0:T(8,128)(2,1)S(1)}, u32[]{:S(2)}, u32[]{:S(2)}) collective-permute-start(bf16[64,1280]{1,0:T(8,128)(2,1)} %get-tuple-element.160), channel_id=1, source_target_pairs={{0,2},{1,3},{2,0},{3,1},{4,6},{5,7},{6,4},{7,5},{8,10},{9,11},{10,... | collective-permute-start | bytes 491528 | tf_op jit(solution)/shard_map/ppermute | solution.py:343
  35.2 35.1 %collective-permute-start.50 = (bf16[64,1280]{1,0:T(8,128)(2,1)}, bf16[64,1280]{1,0:T(8,128)(2,1)S(1)}, u32[]{:S(2)}, u32[]{:S(2)}) collective-permute-start(bf16[64,1280]{1,0:T(8,128)(2,1)} %get-tuple-element.161), channel_id=1, source_target_pairs={{0,3},{1,0},{2,1},{3,2},{4,7},{5,4},{6,5},{7,6},{8,11},{9,8},{10,9... | collective-permute-start | bytes 491528 | tf_op jit(solution)/shard_map/ppermute | solution.py:343
  37.2 0.9 copy-start.1
  38.1 32.1 %copy-start.2 = (bf16[64,1280]{1,0:T(8,128)(2,1)S(1)}, bf16[64,1280]{1,0:T(8,128)(2,1)}, u32[]{:S(2)}) copy-start(bf16[64,1280]{1,0:T(8,128)(2,1)} %get-tuple-element.158.refs_0_.refs_6_.first) | copy-start | bytes 491524
  44.1 37.2 %collective-permute-start.53 = (bf16[64,3840]{1,0:T(8,128)(2,1)}, bf16[64,3840]{1,0:T(8,128)(2,1)S(1)}, u32[]{:S(2)}, u32[]{:S(2)}) collective-permute-start(bf16[64,3840]{1,0:T(8,128)(2,1)} %get-tuple-element.167), channel_id=1, source_target_pairs={{0,1},{1,2},{2,3},{3,0},{4,5},{5,6},{6,7},{7,4},{8,9},{9,10},{10,1... | collective-permute-start | bytes 1474568 | tf_op jit(solution)/shard_map/ppermute | solution.py:343
  44.1 45.7 %collective-permute-start.52 = (bf16[64,3840]{1,0:T(8,128)(2,1)}, bf16[64,3840]{1,0:T(8,128)(2,1)S(1)}, u32[]{:S(2)}, u32[]{:S(2)}) collective-permute-start(bf16[64,3840]{1,0:T(8,128)(2,1)} %get-tuple-element.165), channel_id=1, source_target_pairs={{0,2},{1,3},{2,0},{3,1},{4,6},{5,7},{6,4},{7,5},{8,10},{9,11},{10,... | collective-permute-start | bytes 1474568 | tf_op jit(solution)/shard_map/ppermute | solution.py:343
  47.8 22.7 %copy-start.3 = (f32[5120]{0:T(1024)S(1)}, f32[5120]{0:T(1024)}, u32[]{:S(2)}) copy-start(f32[5120]{0:T(1024)} %param.20) | copy-start | bytes 61444
  47.8 43.7 %collective-permute-start.51 = (bf16[64,3840]{1,0:T(8,128)(2,1)S(1)}, bf16[64,3840]{1,0:T(8,128)(2,1)S(1)}, u32[]{:S(2)}, u32[]{:S(2)}) collective-permute-start(bf16[64,3840]{1,0:T(8,128)(2,1)S(1)} %get-tuple-element.163), channel_id=1, source_target_pairs={{0,3},{1,0},{2,1},{3,2},{4,7},{5,4},{6,5},{7,6},{8,11},{9,8},{10,9... | collective-permute-start | bytes 1474568 | tf_op jit(solution)/shard_map/ppermute | solution.py:343

commit v5 on v4

--- a/solution.py
+++ b/solution.py
@@ -105,14 +105,14 @@
             return cross(cross(value, 1), mask - 1)
         return cross(value, mask)
 
-    def reach_back(value):
+    def reach_back(value, whole_ring):
         parts = [value]
         for _ in range(n_back):
-            parts.append(back(parts[-1], n_inner, len(parts)))
+            parts.append(back(parts[-1], n_inner, 1 if whole_ring else len(parts)))
         return parts
 
-    rest = reach_back(kv_rest)
-    listed = reach_back(swap(kv_listed))
+    rest = reach_back(kv_rest, True)
+    listed = reach_back(swap(kv_listed), False)
     row_list = dest.shape[1]
     n_all = (n_back + 1) * row_list
     bias, chosen = tables(doc_lengths, dest, rest, row_list, n_all, n_inner)

time: 94.5 us -> 92.7 us (0.981); the launches traced: 92.7 us -> 92.9 us
  waiting for transfers between devices: 51.2 us -> 54.9 us
  starting transfers between devices: 22.2 us -> 18.7 us
    ppermute x4, starting transfers between devices: 12.4 us -> 8.91 us  [back(): return lax.ppermute(value, 'inner', pairs)]
    ppermute x4, waiting for transfers between devices: 11.6 us -> 15 us  [back(): return lax.ppermute(value, 'inner', pairs)]
where the time goes in v5:
time: 92.7 us; the launch traced here: 92.9 us
  waiting for transfers between devices  54.9 us (59%)
  starting transfers between devices  18.7 us (20%)
  Pallas kernels  17.6 us (19%)
  local copies, waits for them, and re-layouts  0.93 us (1%)
    ppermute x6, waiting for transfers between devices, shards(): arrived.append(lax.ppermute(routed[k], 'inner', ring(k, n_inner)))  39.9 us
    ppermute x4, waiting for transfers between devices, back(): return lax.ppermute(value, 'inner', pairs)  15 us
    pallas_call x2, Pallas kernels, attend(): pl.pallas_call(functools.partial(attend_kernel, len(kv_parts), n_out), gr...  9.27 us
    ppermute x6, starting transfers between devices, shards(): arrived.append(lax.ppermute(routed[k], 'inner', ring(k, n_inner)))  9.22 us
    ppermute x4, starting transfers between devices, back(): return lax.ppermute(value, 'inner', pairs)  8.91 us
    pallas_call x4, Pallas kernels, normalize(): pl.pallas_call(norm_kernel, out_shape=jax.ShapeDtypeStruct((n_inner * cap...  5.03 us
    pallas_call x1, Pallas kernels, split_blocks(): pl.pallas_call(split_kernel, out_shape=(pltpu.VMEM((row_list - some, kv_w...  2.03 us
  transfers between devices with their start and end apart: 12, of which 9 were waited for; matrix products, arithmetic and copies ran while one was open for 0% of the time, Pallas kernels for 12%

profile of v5, /device:TPU:8, one launch (start us, length us, event | category | flops | bytes accessed | tf_op | source)
XLA Modules:
  0.0 92.9 jit_solution(1326110924932549497)
XLA Ops:
  0.7 2.0 %split_blocks.1 = (bf16[64,2176]{1,0:T(8,128)(2,1)S(1)}, bf16[64,2048]{1,0:T(8,128)(2,1)S(1)}, bf16[64,5120]{1,0:T(8,128)(2,1)S(1)}) custom-call(s32[1,1,2]{2,1,0:T(1,128)} %ids.5, bf16[128,5120]{1,0:T(8,128)(2,1)} %q_ref.5, bf16[128,2048]{1,0:T(8,128)(2,1)} %kv_ref.1), custom_call_target="tpu_custom_call" | custom-call | tf_op jit(solution)/shard_map/split_blocks/pallas_call | solution.py:75
  2.7 25.6 %conditional.1 = (bf16[64,5120]{1,0:T(8,128)(2,1)}, bf16[64,2176]{1,0:T(8,128)(2,1)}, bf16[64,2176]{1,0:T(8,128)(2,1)}, bf16[64,2048]{1,0:T(8,128)(2,1)}, bf16[6...) conditional(s32[]{:T(128)} %bitcast.2, ...), branch_computations={%region_0.0_spmd, %region_1.0_spmd, %region_2.0_spmd, %region_3.0_... | conditional | bytes 11665792 | solution.py:330
  2.7 0.1 collective-permute-start.3
  2.8 0.5 collective-permute-start
  3.3 1.6 %collective-permute-start.1 = (bf16[64,2176]{1,0:T(8,128)(2,1)S(1)}, bf16[64,2176]{1,0:T(8,128)(2,1)}, u32[]{:S(2)}, u32[]{:S(2)}) collective-permute-start(bf16[64,2176]{1,0:T(8,128)(2,1)S(1)} %get-tuple-element.76.refs_0_), channel_id=1, source_target_pairs={{0,1},{1,2},{2,3},{3,0},{4,5},{5,6},{6,7},{7,4},{8,9},{9,10},{10,1... | collective-permute-start | bytes 835592 | tf_op jit(solution)/shard_map/cond/branch_0_fun/ppermute | solution.py:96
  4.9 0.0 collective-permute-done.3
  4.9 1.6 %collective-permute-start.4 = (bf16[64,2048]{1,0:T(8,128)(2,1)}, bf16[64,2048]{1,0:T(8,128)(2,1)}, u32[]{:S(2)}, u32[]{:S(2)}) collective-permute-start(bf16[64,2048]{1,0:T(8,128)(2,1)} %collective-permute-done.3), channel_id=1, source_target_pairs={{0,1},{1,2},{2,3},{3,0},{4,5},{5,6},{6,7},{7,4},{8,9},{9,10},{10,1... | collective-permute-start | bytes 786440 | tf_op jit(solution)/shard_map/cond/branch_0_fun/ppermute | solution.py:96
  6.5 6.5 %collective-permute-done.1.refs_1_ = bf16[64,2176]{1,0:T(8,128)(2,1)} collective-permute-done((bf16[64,2176]{1,0:T(8,128)(2,1)S(1)}, bf16[64,2176]{1,0:T(8,128)(2,1)}, u32[]{:S(2)}, u32[]{:S(2)}) %collective-permute-start.1) | collective-permute-done | bytes 278560 | tf_op jit(solution)/shard_map/cond/branch_0_fun/ppermute | solution.py:96
  12.9 1.6 %collective-permute-start.2 = (bf16[64,2176]{1,0:T(8,128)(2,1)}, bf16[64,2176]{1,0:T(8,128)(2,1)}, u32[]{:S(2)}, u32[]{:S(2)}) collective-permute-start(bf16[64,2176]{1,0:T(8,128)(2,1)} %collective-permute-done.1.refs_1_), channel_id=1, source_target_pairs={{0,1},{1,2},{2,3},{3,0},{4,5},{5,6},{6,7},{7,4},{8,9},{9,10},{10,1... | collective-permute-start | bytes 835592 | tf_op jit(solution)/shard_map/cond/branch_0_fun/ppermute | solution.py:96
  14.5 4.0 %collective-permute-done.4 = bf16[64,2048]{1,0:T(8,128)(2,1)} collective-permute-done((bf16[64,2048]{1,0:T(8,128)(2,1)}, bf16[64,2048]{1,0:T(8,128)(2,1)}, u32[]{:S(2)}, u32[]{:S(2)}) %collective-permute-start.4) | collective-permute-done | bytes 262176 | tf_op jit(solution)/shard_map/cond/branch_0_fun/ppermute | solution.py:96
  18.5 4.2 %collective-permute-start.5 = (bf16[64,2048]{1,0:T(8,128)(2,1)}, bf16[64,2048]{1,0:T(8,128)(2,1)}, u32[]{:S(2)}, u32[]{:S(2)}) collective-permute-start(bf16[64,2048]{1,0:T(8,128)(2,1)} %collective-permute-done.4), channel_id=1, source_target_pairs={{1,2},{2,3},{5,6},{6,7},{9,10},{10,11},{13,14},{14,15},{17,18},{18... | collective-permute-start | bytes 786440 | tf_op jit(solution)/shard_map/cond/branch_0_fun/ppermute | solution.py:96
  22.7 0.9 collective-permute-done.2.refs_2_
  23.6 1.1 %tables.7 = (f32[128,384]{1,0:T(8,128)S(1)}, bf16[256,128]{1,0:T(8,128)(2,1)S(1)}) custom-call(s32[1,8]{1,0:T(1,128)} %get-tuple-element.78.lengths, s32[1,128]{1,0:T(1,128)} %get-tuple-element.79.dest, bf16[64,2176]{1,0:T(8,128)(2,1)S(1)} %get-tuple-element.76.refs_0_, bf16[64,2176]{1,0:T(8,128)(2,1)} %collective-permute-done.1.refs_1_, ...), custom_call_target="tpu_custom_call" | custom-call | tf_op jit(solution)/shard_map/cond/branch_0_fun/tables/pallas_call | solution.py:163
  24.7 3.6 %collective-permute-done.5 = bf16[64,2048]{1,0:T(8,128)(2,1)} collective-permute-done((bf16[64,2048]{1,0:T(8,128)(2,1)}, bf16[64,2048]{1,0:T(8,128)(2,1)}, u32[]{:S(2)}, u32[]{:S(2)}) %collective-permute-start.5) | collective-permute-done | bytes 262176 | tf_op jit(solution)/shard_map/cond/branch_0_fun/ppermute | solution.py:96
  28.3 3.3 %attend.2 = (bf16[64,1280]{1,0:T(8,128)(2,1)}, bf16[64,1280]{1,0:T(8,128)(2,1)}, bf16[64,1280]{1,0:T(8,128)(2,1)}, bf16[64,1280]{1,0:T(8,128)(2,1)}) custom-call(s32[1,1,2]{2,1,0:T(1,128)} %ids.5, bf16[128,5120]{1,0:T(8,128)(2,1)} %q_ref.5, bf16[64,5120]{1,0:T(8,128)(2,1)} %get-tuple-element.150.q_new, f32[128,384]{1,0:T(8,128)S(1)} %get-tuple-element.151.bias, ...), custom_call_target="tpu_custom_call" | custom-call | flops 251658240 | bytes 1703936 | tf_op jit(solution)/shard_map/attend/pallas_call | solution.py:235
  31.7 2.5 %collective-permute-start.48 = (bf16[64,1280]{1,0:T(8,128)(2,1)}, bf16[64,1280]{1,0:T(8,128)(2,1)S(1)}, u32[]{:S(2)}, u32[]{:S(2)}) collective-permute-start(bf16[64,1280]{1,0:T(8,128)(2,1)} %get-tuple-element.159), channel_id=1, source_target_pairs={{0,1},{1,2},{2,3},{3,0},{4,5},{5,6},{6,7},{7,4},{8,9},{9,10},{10,1... | collective-permute-start | bytes 491528 | tf_op jit(solution)/shard_map/ppermute | solution.py:343
  34.1 1.0 %collective-permute-start.49 = (bf16[64,1280]{1,0:T(8,128)(2,1)}, bf16[64,1280]{1,0:T(8,128)(2,1)S(1)}, u32[]{:S(2)}, u32[]{:S(2)}) collective-permute-start(bf16[64,1280]{1,0:T(8,128)(2,1)} %get-tuple-element.160), channel_id=1, source_target_pairs={{0,2},{1,3},{2,0},{3,1},{4,6},{5,7},{6,4},{7,5},{8,10},{9,11},{10,... | collective-permute-start | bytes 491528 | tf_op jit(solution)/shard_map/ppermute | solution.py:343
  35.2 2.0 %collective-permute-start.50 = (bf16[64,1280]{1,0:T(8,128)(2,1)}, bf16[64,1280]{1,0:T(8,128)(2,1)S(1)}, u32[]{:S(2)}, u32[]{:S(2)}) collective-permute-start(bf16[64,1280]{1,0:T(8,128)(2,1)} %get-tuple-element.161), channel_id=1, source_target_pairs={{0,3},{1,0},{2,1},{3,2},{4,7},{5,4},{6,5},{7,6},{8,11},{9,8},{10,9... | collective-permute-start | bytes 491528 | tf_op jit(solution)/shard_map/ppermute | solution.py:343
  37.2 0.9 copy-done.1
  38.1 6.0 %attend.3 = (bf16[64,3840]{1,0:T(8,128)(2,1)S(1)}, bf16[64,3840]{1,0:T(8,128)(2,1)}, bf16[64,3840]{1,0:T(8,128)(2,1)}, bf16[64,3840]{1,0:T(8,128)(2,1)S(1)}) custom-call(s32[1,1,2]{2,1,0:T(1,128)S(1)} %copy-done.4, bf16[128,5120]{1,0:T(8,128)(2,1)S(1)} %copy-done, bf16[64,5120]{1,0:T(8,128)(2,1)} %get-tuple-element.150.q_new, ...), custom_call_target="tpu_custom_call" | custom-call | flops 754974720 | bytes 5111808 | tf_op jit(solution)/shard_map/attend/pallas_call | solution.py:235
  44.1 0.0 collective-permute-start.53
  44.1 3.7 %collective-permute-start.52 = (bf16[64,3840]{1,0:T(8,128)(2,1)}, bf16[64,3840]{1,0:T(8,128)(2,1)S(1)}, u32[]{:S(2)}, u32[]{:S(2)}) collective-permute-start(bf16[64,3840]{1,0:T(8,128)(2,1)} %get-tuple-element.165), channel_id=1, source_target_pairs={{0,2},{1,3},{2,0},{3,1},{4,6},{5,7},{6,4},{7,5},{8,10},{9,11},{10,... | collective-permute-start | bytes 1474568 | tf_op jit(solution)/shard_map/ppermute | solution.py:343
  47.8 1.9 %collective-permute-done.49.refs_2_.first = bf16[64,1280]{1,0:T(8,128)(2,1)S(1)} collective-permute-done((bf16[64,1280]{1,0:T(8,128)(2,1)}, bf16[64,1280]{1,0:T(8,128)(2,1)S(1)}, u32[]{:S(2)}, u32[]{:S(2)}) %collective-permute-start.49) | collective-permute-done | bytes 163872 | tf_op jit(solution)/shard_map/ppermute | solution.py:343
  49.6 21.0 %collective-permute-done.50.refs_3_.first = bf16[64,1280]{1,0:T(8,128)(2,1)S(1)} collective-permute-done((bf16[64,1280]{1,0:T(8,128)(2,1)}, bf16[64,1280]{1,0:T(8,128)(2,1)S(1)}, u32[]{:S(2)}, u32[]{:S(2)}) %collective-permute-start.50) | collective-permute-done | bytes 163872 | tf_op jit(solution)/shard_map/ppermute | solution.py:343
  70.7 0.2 squares.1
  70.9 1.3 %normalize.4.refs_0_ = bf16[256,5120]{1,0:T(8,128)(2,1)} custom-call(s32[1]{0:T(128)} %bitcast.6.me, f32[1,5120]{1,0:T(1,128)S(1)} %bitcast.8, f32[64,128]{1,0:T(8,128)S(1)} %get-tuple-element.168.early, bf16[64,1280]{1,0:T(8,128)(2,1)S(1)} %copy-done.2, bf16[64,3840]{1,0:T(8,128)(2,1)S(1)} %get-tuple-element.169.others), custom_call_target="tpu_custom_call" | custom-call | tf_op jit(solution)/shard_map/normalize/pallas_call | solution.py:298
  72.1 9.1 %collective-permute-done.53.others = bf16[64,3840]{1,0:T(8,128)(2,1)S(1)} collective-permute-done((bf16[64,3840]{1,0:T(8,128)(2,1)}, bf16[64,3840]{1,0:T(8,128)(2,1)S(1)}, u32[]{:S(2)}, u32[]{:S(2)}) %collective-permute-start.53) | collective-permute-done | bytes 491552 | tf_op jit(solution)/shard_map/ppermute | solution.py:343
  81.2 1.3 %normalize.5.refs_0_ = bf16[256,5120]{1,0:T(8,128)(2,1)} custom-call(s32[1]{0:T(128)} %bitcast.5.me, f32[1,5120]{1,0:T(1,128)S(1)} %bitcast.9, f32[64,128]{1,0:T(8,128)S(1)} %get-tuple-element.166.early, bf16[64,1280]{1,0:T(8,128)(2,1)S(1)} %collective-permute-done.48.refs_1_.first, ...), custom_call_target="tpu_custom_call", output_to_operand_aliasing={{}: (5, {})} | custom-call | tf_op jit(solution)/shard_map/normalize/pallas_call | solution.py:298
  82.5 7.5 %collective-permute-done.52.others = bf16[64,3840]{1,0:T(8,128)(2,1)S(1)} collective-permute-done((bf16[64,3840]{1,0:T(8,128)(2,1)}, bf16[64,3840]{1,0:T(8,128)(2,1)S(1)}, u32[]{:S(2)}, u32[]{:S(2)}) %collective-permute-start.52) | collective-permute-done | bytes 491552 | tf_op jit(solution)/shard_map/ppermute | solution.py:343
  90.0 1.3 %normalize.6.refs_0_ = bf16[256,5120]{1,0:T(8,128)(2,1)} custom-call(s32[1]{0:T(128)} %bitcast.4.me, f32[1,5120]{1,0:T(1,128)S(1)} %bitcast.10, f32[64,128]{1,0:T(8,128)S(1)} %get-tuple-element.164.early, bf16[64,1280]{1,0:T(8,128)(2,1)S(1)} %collective-permute-done.49.refs_2_.first, ...), custom_call_target="tpu_custom_call", output_to_operand_aliasing={{}: (5, {})} | custom-call | tf_op jit(solution)/shard_map/normalize/pallas_call | solution.py:298
  91.2 0.4 collective-permute-done.51.others
  91.6 1.3 %normalize.7 = bf16[256,5120]{1,0:T(8,128)(2,1)} custom-call(s32[1]{0:T(128)} %bitcast.me, f32[1,5120]{1,0:T(1,128)S(1)} %bitcast.11, f32[64,128]{1,0:T(8,128)S(1)} %get-tuple-element.162.early, bf16[64,1280]{1,0:T(8,128)(2,1)S(1)} %collective-permute-done.50.refs_3_.first, ...), custom_call_target="tpu_custom_call", output_to_operand_aliasing={{}: (5, {})} | custom-call | tf_op jit(solution)/shard_map/normalize/pallas_call | solution.py:298
  (12 shorter events, 0.0 us)
Async XLA Ops:
  2.7 2.2 %collective-permute-start.3 = (bf16[64,2048]{1,0:T(8,128)(2,1)S(1)}, bf16[64,2048]{1,0:T(8,128)(2,1)}, u32[]{:S(2)}, u32[]{:S(2)}) collective-permute-start(bf16[64,2048]{1,0:T(8,128)(2,1)S(1)} %get-tuple-element.77), channel_id=1, source_target_pairs={{0,4},{4,0},{8,12},{12,8},{16,20},{20,16},{24,28},{28,24},{1,5},{5... | collective-permute-start | bytes 786440 | tf_op jit(solution)/shard_map/cond/branch_0_fun/ppermute | solution.py:101
  2.8 21.9 %collective-permute-start = (bf16[64,5120]{1,0:T(8,128)(2,1)S(1)}, bf16[64,5120]{1,0:T(8,128)(2,1)}, u32[]{:S(2)}, u32[]{:S(2)}) collective-permute-start(bf16[64,5120]{1,0:T(8,128)(2,1)S(1)} %get-tuple-element.75), channel_id=1, source_target_pairs={{0,4},{4,0},{8,12},{12,8},{16,20},{20,16},{24,28},{28,24},{1,5},{5... | collective-permute-start | bytes 1966088 | tf_op jit(solution)/shard_map/cond/branch_0_fun/ppermute | solution.py:101
  3.3 9.6 %collective-permute-start.1 = (bf16[64,2176]{1,0:T(8,128)(2,1)S(1)}, bf16[64,2176]{1,0:T(8,128)(2,1)}, u32[]{:S(2)}, u32[]{:S(2)}) collective-permute-start(bf16[64,2176]{1,0:T(8,128)(2,1)S(1)} %get-tuple-element.76.refs_0_), channel_id=1, source_target_pairs={{0,1},{1,2},{2,3},{3,0},{4,5},{5,6},{6,7},{7,4},{8,9},{9,10},{10,1... | collective-permute-start | bytes 835592 | tf_op jit(solution)/shard_map/cond/branch_0_fun/ppermute | solution.py:96
  4.9 13.7 %collective-permute-start.4 = (bf16[64,2048]{1,0:T(8,128)(2,1)}, bf16[64,2048]{1,0:T(8,128)(2,1)}, u32[]{:S(2)}, u32[]{:S(2)}) collective-permute-start(bf16[64,2048]{1,0:T(8,128)(2,1)} %collective-permute-done.3), channel_id=1, source_target_pairs={{0,1},{1,2},{2,3},{3,0},{4,5},{5,6},{6,7},{7,4},{8,9},{9,10},{10,1... | collective-permute-start | bytes 786440 | tf_op jit(solution)/shard_map/cond/branch_0_fun/ppermute | solution.py:96
  12.9 10.7 %collective-permute-start.2 = (bf16[64,2176]{1,0:T(8,128)(2,1)}, bf16[64,2176]{1,0:T(8,128)(2,1)}, u32[]{:S(2)}, u32[]{:S(2)}) collective-permute-start(bf16[64,2176]{1,0:T(8,128)(2,1)} %collective-permute-done.1.refs_1_), channel_id=1, source_target_pairs={{0,1},{1,2},{2,3},{3,0},{4,5},{5,6},{6,7},{7,4},{8,9},{9,10},{10,1... | collective-permute-start | bytes 835592 | tf_op jit(solution)/shard_map/cond/branch_0_fun/ppermute | solution.py:96
  18.5 9.8 %collective-permute-start.5 = (bf16[64,2048]{1,0:T(8,128)(2,1)}, bf16[64,2048]{1,0:T(8,128)(2,1)}, u32[]{:S(2)}, u32[]{:S(2)}) collective-permute-start(bf16[64,2048]{1,0:T(8,128)(2,1)} %collective-permute-done.4), channel_id=1, source_target_pairs={{1,2},{2,3},{5,6},{6,7},{9,10},{10,11},{13,14},{14,15},{17,18},{18... | collective-permute-start | bytes 786440 | tf_op jit(solution)/shard_map/cond/branch_0_fun/ppermute | solution.py:96
  28.3 8.8 %copy-start = (bf16[128,5120]{1,0:T(8,128)(2,1)S(1)}, bf16[128,5120]{1,0:T(8,128)(2,1)}, u32[]{:S(2)}) copy-start(bf16[128,5120]{1,0:T(8,128)(2,1)} %q_ref.5) | copy-start | bytes 3932164
  28.3 8.8 %copy-start.4 = (s32[1,1,2]{2,1,0:T(1,128)S(1)}, s32[1,1,2]{2,1,0:T(1,128)}, u32[]{:S(2)}) copy-start(s32[1,1,2]{2,1,0:T(1,128)} %ids.5) | copy-start | bytes 28
  31.7 16.1 %collective-permute-start.48 = (bf16[64,1280]{1,0:T(8,128)(2,1)}, bf16[64,1280]{1,0:T(8,128)(2,1)S(1)}, u32[]{:S(2)}, u32[]{:S(2)}) collective-permute-start(bf16[64,1280]{1,0:T(8,128)(2,1)} %get-tuple-element.159), channel_id=1, source_target_pairs={{0,1},{1,2},{2,3},{3,0},{4,5},{5,6},{6,7},{7,4},{8,9},{9,10},{10,1... | collective-permute-start | bytes 491528 | tf_op jit(solution)/shard_map/ppermute | solution.py:343
  34.1 15.5 %collective-permute-start.49 = (bf16[64,1280]{1,0:T(8,128)(2,1)}, bf16[64,1280]{1,0:T(8,128)(2,1)S(1)}, u32[]{:S(2)}, u32[]{:S(2)}) collective-permute-start(bf16[64,1280]{1,0:T(8,128)(2,1)} %get-tuple-element.160), channel_id=1, source_target_pairs={{0,2},{1,3},{2,0},{3,1},{4,6},{5,7},{6,4},{7,5},{8,10},{9,11},{10,... | collective-permute-start | bytes 491528 | tf_op jit(solution)/shard_map/ppermute | solution.py:343
  35.2 35.5 %collective-permute-start.50 = (bf16[64,1280]{1,0:T(8,128)(2,1)}, bf16[64,1280]{1,0:T(8,128)(2,1)S(1)}, u32[]{:S(2)}, u32[]{:S(2)}) collective-permute-start(bf16[64,1280]{1,0:T(8,128)(2,1)} %get-tuple-element.161), channel_id=1, source_target_pairs={{0,3},{1,0},{2,1},{3,2},{4,7},{5,4},{6,5},{7,6},{8,11},{9,8},{10,9... | collective-permute-start | bytes 491528 | tf_op jit(solution)/shard_map/ppermute | solution.py:343
  37.2 0.9 copy-start.1
  38.1 32.6 %copy-start.2 = (bf16[64,1280]{1,0:T(8,128)(2,1)S(1)}, bf16[64,1280]{1,0:T(8,128)(2,1)}, u32[]{:S(2)}) copy-start(bf16[64,1280]{1,0:T(8,128)(2,1)} %get-tuple-element.158.refs_0_.refs_6_.first) | copy-start | bytes 491524
  44.1 37.2 %collective-permute-start.53 = (bf16[64,3840]{1,0:T(8,128)(2,1)}, bf16[64,3840]{1,0:T(8,128)(2,1)S(1)}, u32[]{:S(2)}, u32[]{:S(2)}) collective-permute-start(bf16[64,3840]{1,0:T(8,128)(2,1)} %get-tuple-element.167), channel_id=1, source_target_pairs={{0,1},{1,2},{2,3},{3,0},{4,5},{5,6},{6,7},{7,4},{8,9},{9,10},{10,1... | collective-permute-start | bytes 1474568 | tf_op jit(solution)/shard_map/ppermute | solution.py:343
  44.1 45.9 %collective-permute-start.52 = (bf16[64,3840]{1,0:T(8,128)(2,1)}, bf16[64,3840]{1,0:T(8,128)(2,1)S(1)}, u32[]{:S(2)}, u32[]{:S(2)}) collective-permute-start(bf16[64,3840]{1,0:T(8,128)(2,1)} %get-tuple-element.165), channel_id=1, source_target_pairs={{0,2},{1,3},{2,0},{3,1},{4,6},{5,7},{6,4},{7,5},{8,10},{9,11},{10,... | collective-permute-start | bytes 1474568 | tf_op jit(solution)/shard_map/ppermute | solution.py:343
  47.8 23.1 %copy-start.3 = (f32[5120]{0:T(1024)S(1)}, f32[5120]{0:T(1024)}, u32[]{:S(2)}) copy-start(f32[5120]{0:T(1024)} %param.20) | copy-start | bytes 61444
  47.8 43.9 %collective-permute-start.51 = (bf16[64,3840]{1,0:T(8,128)(2,1)S(1)}, bf16[64,3840]{1,0:T(8,128)(2,1)S(1)}, u32[]{:S(2)}, u32[]{:S(2)}) collective-permute-start(bf16[64,3840]{1,0:T(8,128)(2,1)S(1)} %get-tuple-element.163), channel_id=1, source_target_pairs={{0,3},{1,0},{2,1},{3,2},{4,7},{5,4},{6,5},{7,6},{8,11},{9,8},{10,9... | collective-permute-start | bytes 1474568 | tf_op jit(solution)/shard_map/ppermute | solution.py:343
